TPU v7x, 32 devices: a whole 2x2x4 slice. The times are simulated.
32 devices in a mesh: dp: 8 (over y, x, core), tensor: 4 (over z).
Axes of the slice: x: 2, y: 2, z: 4, core: 2. Of those that a mesh axis runs over, the one named last changes fastest.
Arguments:
- tokens: bfloat16 [24576, 1280], P(('dp', 'tensor')), may hold values from -6 to 6
- lengths: int32 [16], P('dp'), may hold values from 1383 to 1536
- cotangent: bfloat16 [24576, 1280], P(('dp', 'tensor')), may hold values from -6 to 6
- norm1_gain: float32 [1280], replicated, may hold values from 0.5 to 1.5
- norm1_shift: float32 [1280], replicated, may hold values from -2 to 2
- query_weight: bfloat16 [1280, 1280], P('dp', 'tensor'), may hold values from -0.15625 to 0.15625
- query_bias: float32 [1280], P('tensor'), may hold values from -2 to 2
- key_weight: bfloat16 [1280, 1280], P('dp', 'tensor'), may hold values from -0.15625 to 0.15625
- value_weight: bfloat16 [1280, 1280], P('dp', 'tensor'), may hold values from -0.15625 to 0.15625
- value_bias: float32 [1280], P('tensor'), may hold values from -2 to 2
- out_weight: bfloat16 [1280, 1280], P('tensor', 'dp'), may hold values from -3.5 to 3.5
- out_bias: float32 [1280], replicated, may hold values from -2 to 2
- norm2_gain: float32 [1280], replicated, may hold values from 0.5 to 1.5
- norm2_shift: float32 [1280], replicated, may hold values from -2 to 2
- up_weight: bfloat16 [1280, 5120], P('dp', 'tensor'), may hold values from -0.15625 to 0.15625
- up_bias: float32 [5120], P('tensor'), may hold values from -2 to 2
- down_weight: bfloat16 [5120, 1280], P('tensor', 'dp'), may hold values from -0.078125 to 0.078125
- down_bias: float32 [1280], replicated, may hold values from -2 to 2
Outputs:
- layer_out: bfloat16 [24576, 1280], P(('dp', 'tensor'))
- grad_tokens: bfloat16 [24576, 1280], P(('dp', 'tensor'))
- grad_norm1_gain: float32 [1280], replicated
- grad_norm1_shift: float32 [1280], replicated
- grad_query_weight: float32 [1280, 1280], P('dp', 'tensor')
- grad_query_bias: float32 [1280], P('tensor')
- grad_key_weight: float32 [1280, 1280], P('dp', 'tensor')
- grad_value_weight: float32 [1280, 1280], P('dp', 'tensor')
- grad_value_bias: float32 [1280], P('tensor')
- grad_out_weight: float32 [1280, 1280], P('tensor', 'dp')
- grad_out_bias: float32 [1280], replicated
- grad_norm2_gain: float32 [1280], replicated
- grad_norm2_shift: float32 [1280], replicated
- grad_up_weight: float32 [1280, 5120], P('dp', 'tensor')
- grad_up_bias: float32 [5120], P('tensor')
- grad_down_weight: float32 [5120, 1280], P('tensor', 'dp')
- grad_down_bias: float32 [1280], replicated
All inputs are finite; a program needn't handle non-finite values.
Results may differ from a plain program's by a relative error of at most 0.02.
Values may be sent and summed in bfloat16 or wider, within the bound.
A program may use at most 256 MiB of HBM per device.

v0:
```python
import jax
import jax.numpy as jnp
from jax import lax
from jax.sharding import PartitionSpec as P

HDIM = 80


EPS = 1e-05


def norm_rows(values, norm_gain, norm_shift):
    center = values - jnp.mean(values, -1, keepdims=True)
    spread = jnp.mean(center * center, -1, keepdims=True)
    return center * lax.rsqrt(spread + EPS) * norm_gain + norm_shift


def gelu_exact(values):
    return jax.nn.gelu(values, approximate=False)


def inner_rows(left, right):
    return lax.dot_general(
        left, right, (((0,), (0,)), ((), ())), preferred_element_type=jnp.float32
    )


def inner_cols(left, right):
    return lax.dot_general(
        left, right, (((1,), (1,)), ((), ())), preferred_element_type=jnp.float32
    )


def masked_scores(query_blk, key_clip, visible, scaling):
    scores = (
        jnp.einsum("qhd,khd->hqk", query_blk, key_clip, preferred_element_type=jnp.float32)
        * scaling
    )
    return jnp.where(visible, scores, -1e30)


def attend_clip(query_clip, key_clip, value_clip, clip_length, scaling):
    clip_len = query_clip.shape[0]
    block_rows = min(512, clip_len)
    visible = (jnp.arange(clip_len) < clip_length)[None, None, :]

    def one_block(query_blk):
        scores = masked_scores(query_blk, key_clip, visible, scaling)
        row_max = jnp.max(scores, -1, keepdims=True)
        exp_scores = jnp.exp(scores - row_max)
        totals = jnp.sum(exp_scores, -1, keepdims=True)
        probs_low = (exp_scores / totals).astype(jnp.bfloat16)
        mixed_heads = jnp.einsum(
            "hqk,khd->qhd", probs_low, value_clip, preferred_element_type=jnp.float32
        )
        return (mixed_heads.astype(jnp.bfloat16), (row_max + jnp.log(totals))[:, :, 0])

    blocked = query_clip.reshape((clip_len // block_rows, block_rows) + query_clip.shape[1:])
    outputs, log_totals = lax.map(one_block, blocked)
    return (outputs.reshape(query_clip.shape), log_totals)


def attend_back(query_clip, key_clip, value_clip, grad_clip, log_totals, clip_length, scaling):
    clip_len = query_clip.shape[0]
    block_rows = min(512, clip_len)
    block_count = clip_len // block_rows
    visible = (jnp.arange(clip_len) < clip_length)[None, None, :]
    block_shape = (block_count, block_rows) + query_clip.shape[1:]

    def one_block(carried, member):
        grad_key, grad_value = carried
        query_blk, grad_blk, total_blk = member
        scores = masked_scores(query_blk, key_clip, visible, scaling)
        attn_probs = jnp.exp(scores - total_blk[:, :, None])
        grad_probs = jnp.einsum(
            "qhd,khd->hqk", grad_blk, value_clip, preferred_element_type=jnp.float32
        )
        grad_scores = attn_probs * (
            grad_probs - jnp.sum(attn_probs * grad_probs, -1, keepdims=True)
        )
        scores_low = grad_scores.astype(jnp.bfloat16)
        grad_query = (
            jnp.einsum("hqk,khd->qhd", scores_low, key_clip, preferred_element_type=jnp.float32)
            * scaling
        )
        grad_key = (
            grad_key
            + jnp.einsum("hqk,qhd->khd", scores_low, query_blk, preferred_element_type=jnp.float32)
            * scaling
        )
        grad_value = grad_value + jnp.einsum(
            "hqk,qhd->khd",
            attn_probs.astype(jnp.bfloat16),
            grad_blk,
            preferred_element_type=jnp.float32,
        )
        return ((grad_key, grad_value), grad_query)

    zeros_clip = jnp.zeros(key_clip.shape, jnp.float32)
    (grad_key, grad_value), grad_query = lax.scan(
        one_block,
        (zeros_clip, zeros_clip),
        (query_clip.reshape(block_shape), grad_clip.reshape(block_shape), log_totals),
    )
    return (grad_query.reshape(query_clip.shape), grad_key, grad_value)


def local(
    tokens,
    lengths,
    cotangent,
    norm1_gain,
    norm1_shift,
    query_weight,
    query_bias,
    key_weight,
    value_weight,
    value_bias,
    out_weight,
    out_bias,
    norm2_gain,
    norm2_shift,
    up_weight,
    up_bias,
    down_weight,
    down_bias,
):
    tensor_size = lax.axis_size("tensor")
    tensor_pos = lax.axis_index("tensor")
    row_count = tokens.shape[0]
    group_rows = row_count * tensor_size
    clip_count = lengths.shape[0]
    clip_len = group_rows // clip_count
    scaling = HDIM ** (-0.5)
    wq_all, wk_all, wv_all, wo_all, wup_all, wdown_all = (
        lax.all_gather(query_weight, "dp", axis=0, tiled=True),
        lax.all_gather(key_weight, "dp", axis=0, tiled=True),
        lax.all_gather(value_weight, "dp", axis=0, tiled=True),
        lax.all_gather(out_weight, "dp", axis=1, tiled=True),
        lax.all_gather(up_weight, "dp", axis=0, tiled=True),
        lax.all_gather(down_weight, "dp", axis=1, tiled=True),
    )
    head_cols = wq_all.shape[1]
    w_joined = jnp.concatenate([wq_all, wk_all, wv_all], 1)
    source = tokens.astype(jnp.float32)
    first_in = norm_rows(source, norm1_gain, norm1_shift).astype(jnp.bfloat16)
    first_full = lax.all_gather(first_in, "tensor", axis=0, tiled=True)
    joined = jnp.dot(first_full, w_joined, preferred_element_type=jnp.float32)
    queries = (joined[:, :head_cols] + query_bias).astype(jnp.bfloat16)
    key_rows = joined[:, head_cols : 2 * head_cols].astype(jnp.bfloat16)
    value_rows = (joined[:, 2 * head_cols :] + value_bias).astype(jnp.bfloat16)
    heads_here = head_cols // HDIM
    clip_shape = (clip_count, clip_len, heads_here, HDIM)
    query_clips = queries.reshape(clip_shape)
    key_clips = key_rows.reshape(clip_shape)
    value_clips = value_rows.reshape(clip_shape)
    heads_clips, log_totals = lax.map(
        lambda member: attend_clip(member[0], member[1], member[2], member[3], scaling),
        (query_clips, key_clips, value_clips, lengths),
    )
    heads_out = heads_clips.reshape(group_rows, head_cols)
    piece = heads_out
    branch = lax.psum_scatter(
        jnp.dot(piece, wo_all, preferred_element_type=jnp.float32).astype(jnp.bfloat16),
        "tensor",
        scatter_dimension=0,
        tiled=True,
    ).astype(jnp.float32)
    middle = source + branch + out_bias
    second_in = norm_rows(middle, norm2_gain, norm2_shift).astype(jnp.bfloat16)
    second_full = lax.all_gather(second_in, "tensor", axis=0, tiled=True)
    hidden_pre = jnp.dot(second_full, wup_all, preferred_element_type=jnp.float32) + up_bias
    hidden = gelu_exact(hidden_pre).astype(jnp.bfloat16)
    piece = hidden
    down_out = lax.psum_scatter(
        jnp.dot(piece, wdown_all, preferred_element_type=jnp.float32).astype(jnp.bfloat16),
        "tensor",
        scatter_dimension=0,
        tiled=True,
    ).astype(jnp.float32)
    layer_out = (middle + down_out + down_bias).astype(jnp.bfloat16)
    row_ids = tensor_pos * row_count + jnp.arange(row_count)
    clip_ids = row_ids // clip_len
    frames = row_ids % clip_len
    row_length = jnp.sum(
        jnp.where(clip_ids[:, None] == jnp.arange(clip_count)[None, :], lengths[None, :], 0), 1
    )
    valid = (frames < row_length).astype(jnp.float32)[:, None]
    out_grad = cotangent.astype(jnp.float32) * valid
    out_full = lax.all_gather(out_grad.astype(jnp.bfloat16), "tensor", axis=0, tiled=True)
    grad_down = inner_rows(hidden, out_full)
    grad_hidden = inner_cols(out_full, wdown_all)
    unused_value, gelu_pull = jax.vjp(gelu_exact, hidden_pre)
    grad_pre = gelu_pull(grad_hidden)[0]
    grad_pre_low = grad_pre.astype(jnp.bfloat16)
    grad_up = inner_rows(second_full, grad_pre_low)
    piece = grad_pre_low
    grad_second = lax.psum_scatter(
        inner_cols(piece, wup_all).astype(jnp.bfloat16), "tensor", scatter_dimension=0, tiled=True
    ).astype(jnp.float32)
    unused_second, second_pull = jax.vjp(norm_rows, middle, norm2_gain, norm2_shift)
    grad_mid_part, grad_gain_two, grad_shift_two = second_pull(grad_second)
    grad_middle = out_grad + grad_mid_part
    branch_full = lax.all_gather(grad_middle.astype(jnp.bfloat16), "tensor", axis=0, tiled=True)
    grad_out_w = inner_rows(heads_out, branch_full)
    grad_heads = inner_cols(branch_full, wo_all).astype(jnp.bfloat16)
    grad_query, grad_key, grad_value = lax.map(
        lambda member: attend_back(
            member[0], member[1], member[2], member[3], member[4], member[5], scaling
        ),
        (query_clips, key_clips, value_clips, grad_heads.reshape(clip_shape), log_totals, lengths),
    )
    grad_query = grad_query.reshape(group_rows, head_cols)
    grad_key = grad_key.reshape(group_rows, head_cols)
    grad_value = grad_value.reshape(group_rows, head_cols)
    grad_joined = jnp.concatenate([grad_query, grad_key, grad_value], 1).astype(jnp.bfloat16)
    grad_w_joined = inner_rows(first_full, grad_joined)
    piece = grad_joined
    grad_first = lax.psum_scatter(
        inner_cols(piece, w_joined).astype(jnp.bfloat16), "tensor", scatter_dimension=0, tiled=True
    ).astype(jnp.float32)
    unused_first, first_pull = jax.vjp(norm_rows, source, norm1_gain, norm1_shift)
    grad_src_part, grad_gain_one, grad_shift_one = first_pull(grad_first)
    grad_tokens = (grad_middle + grad_src_part).astype(jnp.bfloat16)
    sum_q, sum_k, sum_v, sum_o, sum_up, sum_down = (
        lax.psum_scatter(
            grad_w_joined[:, :head_cols].astype(jnp.bfloat16), "dp", scatter_dimension=0, tiled=True
        ).astype(jnp.float32),
        lax.psum_scatter(
            grad_w_joined[:, head_cols : 2 * head_cols].astype(jnp.bfloat16),
            "dp",
            scatter_dimension=0,
            tiled=True,
        ).astype(jnp.float32),
        lax.psum_scatter(
            grad_w_joined[:, 2 * head_cols :].astype(jnp.bfloat16),
            "dp",
            scatter_dimension=0,
            tiled=True,
        ).astype(jnp.float32),
        lax.psum_scatter(
            grad_out_w.astype(jnp.bfloat16), "dp", scatter_dimension=1, tiled=True
        ).astype(jnp.float32),
        lax.psum_scatter(
            grad_up.astype(jnp.bfloat16), "dp", scatter_dimension=0, tiled=True
        ).astype(jnp.float32),
        lax.psum_scatter(
            grad_down.astype(jnp.bfloat16), "dp", scatter_dimension=1, tiled=True
        ).astype(jnp.float32),
    )

    def widen(piece):
        zeros_full = jnp.zeros((tensor_size * piece.shape[0],), jnp.float32)
        return lax.dynamic_update_slice_in_dim(zeros_full, piece, tensor_pos * piece.shape[0], 0)

    small = lax.psum(
        (
            widen(jnp.sum(grad_query, 0)),
            widen(jnp.sum(grad_value, 0)),
            widen(jnp.sum(grad_pre, 0)),
            grad_gain_one,
            grad_shift_one,
            jnp.sum(grad_middle, 0),
            grad_gain_two,
            grad_shift_two,
            jnp.sum(out_grad, 0),
        ),
        ("dp", "tensor"),
    )
    up_cols = wup_all.shape[1]
    bias_query = lax.dynamic_slice_in_dim(small[0], tensor_pos * head_cols, head_cols, 0)
    bias_value = lax.dynamic_slice_in_dim(small[1], tensor_pos * head_cols, head_cols, 0)
    bias_up = lax.dynamic_slice_in_dim(small[2], tensor_pos * up_cols, up_cols, 0)
    return (
        layer_out,
        grad_tokens,
        small[3],
        small[4],
        sum_q,
        bias_query,
        sum_k,
        sum_v,
        bias_value,
        sum_o,
        small[5],
        small[6],
        small[7],
        sum_up,
        bias_up,
        sum_down,
        small[8],
    )


def solution(mesh):
    placed = (
        P(("dp", "tensor"), None),
        P("dp"),
        P(("dp", "tensor"), None),
        P(),
        P(),
        P("dp", "tensor"),
        P("tensor"),
        P("dp", "tensor"),
        P("dp", "tensor"),
        P("tensor"),
        P("tensor", "dp"),
        P(),
        P(),
        P(),
        P("dp", "tensor"),
        P("tensor"),
        P("tensor", "dp"),
        P(),
    )
    return jax.shard_map(
        local,
        mesh=mesh,
        in_specs=placed,
        out_specs=(
            P(("dp", "tensor"), None),
            P(("dp", "tensor"), None),
            P(),
            P(),
            P("dp", "tensor"),
            P("tensor"),
            P("dp", "tensor"),
            P("dp", "tensor"),
            P("tensor"),
            P("tensor", "dp"),
            P(),
            P(),
            P(),
            P("dp", "tensor"),
            P("tensor"),
            P("tensor", "dp"),
            P(),
        ),
        check_vma=False,
    )
```

profile of v0, /device:TPU:1, one launch (start us, length us, event | category | flops | bytes accessed | tf_op | source)
XLA Modules:
  0.0 1815.5 jit_solution(13319453200435808220)
XLA Ops:
  15.2 12.2 all_gather.31
  27.4 11.1 all_gather.32
  38.5 10.2 all_gather.33
  48.7 12.2 all_gather.34
  60.9 97.8 %all-gather.7.cloned.1.call-done = bf16[3072,1280]{1,0:T(8,128)(2,1)} async-done(((bf16[768,1280]{1,0:T(8,128)(2,1)}), bf16[3072,1280]{1,0:T(8,128)(2,1)}) %all-gather.7.cloned.1.call-update) | async-done | bytes 7864336 | tf_op jit(solution)/shard_map/all_gather | solution.py:147
  158.6 11.3 fusion.72
  174.1 5.7 reshape.213
  182.9 5.7 reshape.212
  197.3 78.6 %while.55 = (s32[]{:T(128)}, bf16[2,1536,4,80]{3,2,1,0:T(4,128)(2,1)}, f32[2,3,4,512]{3,2,1,0:T(4,128)}, bf16[2,1536,4,80]{1,3,2,0:T(8,128)(2,1)}, bf16[2,1536,4...) while((s32[]{:T(128)}, ...), condition=%wide.region_7.8_spmd, body=%wide.region_2.7_spmd.sunk | while | flops 1044545024 | bytes 54844732 | solution.py:157
  203.8 29.9 %while.58 = (s32[]{:T(128)}, bf16[3,512,4,80]{1,3,2,0:T(8,128)(2,1)S(1)}, f32[3,4,512]{2,1,0:T(4,128)S(1)}, bf16[3,512,4,80]{1,3,2,0:T(8,128)(2,1)S(1)}, bf16[15...) while((s32[]{:T(128)}, ...), condition=%wide.region_6.6_spmd.clone, body=%wide.region_3.5_spmd.clone.sunk | while | flops 1044545024 | bytes 40442988 | solution.py:59
  209.2 4.5 fusion.156
  219.2 4.5 fusion.156
  229.1 4.5 fusion.156
  242.9 29.9 %while.58 = (s32[]{:T(128)}, bf16[3,512,4,80]{1,3,2,0:T(8,128)(2,1)S(1)}, f32[3,4,512]{2,1,0:T(4,128)S(1)}, bf16[3,512,4,80]{1,3,2,0:T(8,128)(2,1)S(1)}, bf16[15...) while((s32[]{:T(128)}, ...), condition=%wide.region_6.6_spmd.clone, body=%wide.region_3.5_spmd.clone.sunk | while | flops 1044545024 | bytes 40442988 | solution.py:59
  248.3 4.5 fusion.156
  258.3 4.5 fusion.156
  268.2 4.5 fusion.156
  276.0 5.1 reshape.219
  281.0 6.3 convolution_convert_fusion.3
  288.1 133.8 %reduce-scatter.17.cloned.1.call-done = bf16[768,1280]{1,0:T(8,128)(2,1)} async-done(((bf16[3072,1280]{1,0:T(8,128)(2,1)}), bf16[768,1280]{1,0:T(8,128)(2,1)}) %reduce-scatter.17.cloned.1.call-update) | async-done | bytes 1966096 | tf_op jit(solution)/shard_map/reduce_scatter | solution.py:163
  434.2 136.3 %all-gather.9.cloned.1.call-done = bf16[3072,1280]{1,0:T(8,128)(2,1)} async-done(((bf16[768,1280]{1,0:T(8,128)(2,1)}), bf16[3072,1280]{1,0:T(8,128)(2,1)}) %all-gather.9.cloned.1.call-update) | async-done | bytes 7864336 | tf_op jit(solution)/shard_map/all_gather | solution.py:171
  570.6 16.9 fusion.93
  587.5 16.0 all-gather.13.cloned.1.call-done
  603.5 142.9 %all-gather.15.cloned.1.call-done = bf16[3072,1280]{1,0:T(8,128)(2,1)} async-done(((bf16[768,1280]{1,0:T(8,128)(2,1)}), bf16[3072,1280]{1,0:T(8,128)(2,1)}) %all-gather.15.cloned.1.call-update) | async-done | bytes 7864336 | tf_op jit(solution)/shard_map/all_gather | solution.py:190
  746.4 50.6 %fusion.87 = (f32[1280]{0:T(1024)}, bf16[3072,1280]{1,0:T(8,128)(2,1)S(1)}, f32[3072,1280]{1,0:T(8,128)}) fusion(f32[3072,1280]{1,0:T(8,128)} %fusion.93, f32[1280]{0:T(1024)S(1)} %copy-done.60, bf16[3072,1280]{1,0:T(8,128)(2,1)} %all-gather.15.cloned.1.call-done, bf16[1280,1280]{0,1:T(8,128)(2,1)} %all-gather.13.cloned.1.call-done), kind=kOutput, calls=%fused_computation.161 | convolution fusion | flops 10357308416 | bytes 50472960 | tf_op jit(solution)/shard_map/dot_general | solution.py:29
  800.1 12.3 convolution_convert_fusion.1
  812.6 12.4 multiply_convert_fusion.1
  828.1 12.3 convolution_convert_fusion.2
  840.5 106.3 %reduce-scatter.21.cloned.1.call-done = bf16[768,1280]{1,0:T(8,128)(2,1)} async-done(((bf16[3072,1280]{1,0:T(8,128)(2,1)}), bf16[768,1280]{1,0:T(8,128)(2,1)}) %reduce-scatter.21.cloned.1.call-update) | async-done | bytes 1966096 | tf_op jit(solution)/shard_map/reduce_scatter | solution.py:198
  946.9 4.5 convert_reduce_fusion.1
  954.7 131.1 %reduce-scatter.19.cloned.1.call-done = bf16[768,1280]{1,0:T(8,128)(2,1)} async-done(((bf16[3072,1280]{1,0:T(8,128)(2,1)}), bf16[768,1280]{1,0:T(8,128)(2,1)}) %reduce-scatter.19.cloned.1.call-update) | async-done | bytes 1966096 | tf_op jit(solution)/shard_map/reduce_scatter | solution.py:175
  1085.8 6.6 fusion.89
  1096.3 16.3 convolution_convert_fusion.4
  1112.7 16.5 convolution_convert_fusion.5
  1129.2 108.3 %all-gather.17.cloned.1.call-done = bf16[3072,1280]{1,0:T(8,128)(2,1)} async-done(((bf16[768,1280]{1,0:T(8,128)(2,1)}), bf16[3072,1280]{1,0:T(8,128)(2,1)}) %all-gather.17.cloned.1.call-update) | async-done | bytes 7864336 | tf_op jit(solution)/shard_map/all_gather | solution.py:204
  1237.5 7.3 convolution_convert_fusion.6
  1244.8 5.0 reshape.215
  1251.4 175.6 %while.57 = (s32[]{:T(128)}, f32[2,1536,4,80]{3,2,1,0:T(4,128)}, bf16[2,1536,4,80]{1,3,2,0:T(8,128)(2,1)}, f32[2,1536,4,80]{1,3,2,0:T(8,128)}, bf16[2,1536,4,80]...) while((s32[]{:T(128)}, f32[2,1536,4,80]{3,2,1,0:T(4,128)}, ...), condition=%wide.region_20.21_spmd, body=%wide.region_16.20_spmd.sunk | while | flops 2547514880 | bytes 233074336 | solution.py:207
  1262.1 64.8 %while.59 = (s32[]{:T(128)}, f32[1536,4,80]{0,2,1:T(8,128)}, f32[1536,4,80]{0,2,1:T(8,128)S(1)}, f32[3,512,4,80]{1,3,2,0:T(8,128)}, bf16[3,512,4,80]{1,3,2,0:T(8...) while((s32[]{:T(128)}, f32[1536,4,80]{0,2,1:T(8,128)}, ...), condition=%wide.region_19.19_spmd.clone, body=%wide.region_17.18_spmd.clone.sunk | while | flops 2547514880 | bytes 152022288 | solution.py:100
  1265.6 5.5 multiply_reduce_fusion.3
  1271.1 3.6 multiply_convert_fusion.3
  1287.0 5.5 multiply_reduce_fusion.3
  1292.5 3.6 multiply_convert_fusion.3
  1309.1 5.5 multiply_reduce_fusion.3
  1314.5 3.6 multiply_convert_fusion.3
  1327.0 4.3 copy.148
  1350.2 64.0 %while.59 = (s32[]{:T(128)}, f32[1536,4,80]{0,2,1:T(8,128)}, f32[1536,4,80]{0,2,1:T(8,128)S(1)}, f32[3,512,4,80]{1,3,2,0:T(8,128)}, bf16[3,512,4,80]{1,3,2,0:T(8...) while((s32[]{:T(128)}, f32[1536,4,80]{0,2,1:T(8,128)}, ...), condition=%wide.region_19.19_spmd.clone, body=%wide.region_17.18_spmd.clone.sunk | while | flops 2547514880 | bytes 152022288 | solution.py:100
  1353.7 5.5 multiply_reduce_fusion.3
  1359.2 3.6 multiply_convert_fusion.3
  1375.1 5.5 multiply_reduce_fusion.3
  1380.5 3.6 multiply_convert_fusion.3
  1396.4 5.5 multiply_reduce_fusion.3
  1414.2 4.3 copy.148
  1427.0 3.8 fusion.91
  1444.6 4.3 copy.113
  1448.9 14.1 convolution_convert_fusion.7
  1467.4 9.6 convolution_convert_fusion.8
  1477.3 14.3 convolution_convert_fusion
  1499.8 37.4 %reduce-scatter.33.cloned.1.call-done = bf16[160,320]{1,0:T(8,128)(2,1)} async-done(((bf16[1280,320]{1,0:T(8,128)(2,1)}), bf16[160,320]{1,0:T(8,128)(2,1)}) %reduce-scatter.33.cloned.1.call-update) | async-done | bytes 102416
  1539.0 37.1 %reduce-scatter.31.cloned.1.call-done = bf16[160,320]{1,0:T(8,128)(2,1)} async-done(((bf16[1280,320]{1,0:T(8,128)(2,1)}), bf16[160,320]{1,0:T(8,128)(2,1)}) %reduce-scatter.31.cloned.1.call-update) | async-done | bytes 102416
  1578.0 37.3 %reduce-scatter.25.cloned.1.call-done = bf16[320,160]{0,1:T(8,128)(2,1)} async-done(((bf16[320,1280]{0,1:T(8,128)(2,1)}), bf16[320,160]{0,1:T(8,128)(2,1)}) %reduce-scatter.25.cloned.1.call-update) | async-done | bytes 102416 | tf_op jit(solution)/shard_map/reduce_scatter | solution.py:241
  1616.9 137.2 %reduce-scatter.23.cloned.1.call-done = bf16[768,1280]{1,0:T(8,128)(2,1)} async-done(((bf16[3072,1280]{1,0:T(8,128)(2,1)}), bf16[768,1280]{1,0:T(8,128)(2,1)}) %reduce-scatter.23.cloned.1.call-update) | async-done | bytes 1966096 | tf_op jit(solution)/shard_map/reduce_scatter | solution.py:219
  1759.3 42.5 %all-reduce = (f32[1280]{0:T(1024)}, f32[1280]{0:T(1024)}, f32[1280]{0:T(1024)S(1)}, f32[1280]{0:T(1024)S(1)}, f32[1280]{0:T(1024)}, /*index=5*/f32[1280]{0:T(10...) all-reduce(f32[1280]{0:T(1024)S(1)} %get-tuple-element.448, ...), channel_id=1, replica_groups=mesh['dp'=8,'tensor'=4] {'dp','tensor'}, use_global_device_ids=true, to_apply=%region_25.26 | all-reduce | flops 15360 | bytes 122880 | tf_op jit(solution)/shard_map/psum | solution.py:256
  1803.8 4.4 add_convert_fusion
  (396 shorter events, 256.3 us)
Async XLA Ops:
  8.0 5.0 copy-start.5
  8.0 5.0 copy-start.36
  8.0 5.0 copy-start.56
  8.1 150.6 %all-gather.7.cloned.1.call-start = ((), (), s32[]{:S(2)}) async-start(), calls=%async_computation.10 | async-start | bytes 9830400 | tf_op jit(solution)/shard_map/all_gather | solution.py:147
  10.1 5.1 copy-start.38
  13.0 14.4 copy-start.39
  13.0 14.4 copy-start.42
  13.0 25.5 %copy-start.40 = (bf16[160,320]{1,0:T(8,128)(2,1)S(1)}, bf16[160,320]{1,0:T(8,128)(2,1)}, u32[]{:S(2)}) copy-start(bf16[160,320]{1,0:T(8,128)(2,1)} %param.34) | copy-start | bytes 307204
  13.0 35.7 %copy-start.41 = (bf16[320,160]{0,1:T(8,128)(2,1)S(1)}, bf16[320,160]{0,1:T(8,128)(2,1)}, u32[]{:S(2)}) copy-start(bf16[320,160]{0,1:T(8,128)(2,1)} %param.36) | copy-start | bytes 307204
  15.1 406.8 %reduce-scatter.17.cloned.1.call-start = ((), (), s32[]{:S(2)}) async-start(), calls=%async_computation.11 | async-start | bytes 9830400 | tf_op jit(solution)/shard_map/reduce_scatter | solution.py:163
  27.4 142.6 %copy-start.22 = (bf16[1280,320]{1,0:T(8,128)(2,1)}, bf16[1280,320]{1,0:T(8,128)(2,1)S(1)}, u32[]{:S(2)}) copy-start(bf16[1280,320]{1,0:T(8,128)(2,1)S(1)} %all_gather.31) | copy-start | bytes 2457604
  38.5 131.5 %copy-start.24 = (bf16[1280,320]{1,0:T(8,128)(2,1)}, bf16[1280,320]{1,0:T(8,128)(2,1)S(1)}, u32[]{:S(2)}) copy-start(bf16[1280,320]{1,0:T(8,128)(2,1)S(1)} %all_gather.32) | copy-start | bytes 2457604
  48.7 121.3 %copy-start.25 = (bf16[1280,320]{1,0:T(8,128)(2,1)}, bf16[1280,320]{1,0:T(8,128)(2,1)S(1)}, u32[]{:S(2)}) copy-start(bf16[1280,320]{1,0:T(8,128)(2,1)S(1)} %all_gather.33) | copy-start | bytes 2457604
  275.9 5.1 copy-start.26
  281.0 6.4 copy-start.18
  287.4 134.5 %copy-start.6 = (bf16[768,1280]{1,0:T(8,128)(2,1)S(1)}, bf16[768,1280]{1,0:T(8,128)(2,1)}, u32[]{:S(2)}) copy-start(bf16[768,1280]{1,0:T(8,128)(2,1)} %param.26) | copy-start | bytes 5898244
  287.4 134.5 %copy-start.28 = (f32[1280]{0:T(1024)S(1)}, f32[1280]{0:T(1024)}, u32[]{:S(2)}) copy-start(f32[1280]{0:T(1024)} %param.37) | copy-start | bytes 15364
  287.4 146.8 %all-gather.11.cloned.1.call-start = ((), (), s32[]{:S(2)}) async-start(), calls=%async_computation.13 | async-start | bytes 3686400 | tf_op jit(solution)/shard_map/all_gather | solution.py:140
  288.0 138.5 %copy-start.34 = (f32[1280]{0:T(1024)S(1)}, f32[1280]{0:T(1024)}, u32[]{:S(2)}) copy-start(f32[1280]{0:T(1024)} %param.38) | copy-start | bytes 15364
  288.0 138.5 %copy-start.57 = (f32[1280]{0:T(1024)S(1)}, f32[1280]{0:T(1024)}, u32[]{:S(2)}) copy-start(f32[1280]{0:T(1024)} %param.39) | copy-start | bytes 15364
  288.0 282.5 %all-gather.9.cloned.1.call-start = ((), (), s32[]{:S(2)}) async-start(), calls=%async_computation.12 | async-start | bytes 9830400 | tf_op jit(solution)/shard_map/all_gather | solution.py:171
  428.9 174.6 %all-gather.13.cloned.1.call-start = ((), (), s32[]{:S(2)}) async-start(), calls=%async_computation.14 | async-start | bytes 3686400 | tf_op jit(solution)/shard_map/all_gather | solution.py:141
  429.5 316.9 %all-gather.15.cloned.1.call-start = ((), (), s32[]{:S(2)}) async-start(), calls=%async_computation.16 | async-start | bytes 9830400 | tf_op jit(solution)/shard_map/all_gather | solution.py:190
  434.1 312.3 %copy-start.60 = (f32[1280]{0:T(1024)S(1)}, f32[1280]{0:T(1024)}, u32[]{:S(2)}) copy-start(f32[1280]{0:T(1024)} %param.41) | copy-start | bytes 15364
  434.1 512.7 %reduce-scatter.21.cloned.1.call-start = ((), (), s32[]{:S(2)}) async-start(), calls=%async_computation.17 | async-start | bytes 9830400 | tf_op jit(solution)/shard_map/reduce_scatter | solution.py:198
  587.5 212.5 %copy-start.63 = (bf16[1280,1280]{1,0:T(8,128)(2,1)S(1)}, bf16[1280,1280]{1,0:T(8,128)(2,1)}, u32[]{:S(2)}) copy-start(bf16[1280,1280]{1,0:T(8,128)(2,1)} %all-gather.11.cloned.1.call-done) | copy-start | bytes 9830404
  812.4 273.4 %reduce-scatter.19.cloned.1.call-start = ((), (), s32[]{:S(2)}) async-start(), calls=%async_computation.15 | async-start | bytes 9830400 | tf_op jit(solution)/shard_map/reduce_scatter | solution.py:175
  812.6 15.5 copy-start.64
  840.4 106.4 %copy-start.7 = (bf16[768,1280]{1,0:T(8,128)(2,1)S(1)}, bf16[768,1280]{1,0:T(8,128)(2,1)}, u32[]{:S(2)}) copy-start(bf16[768,1280]{1,0:T(8,128)(2,1)} %param.26) | copy-start | bytes 5898244
  840.4 106.4 %copy-start.29 = (f32[1280]{0:T(1024)S(1)}, f32[1280]{0:T(1024)}, u32[]{:S(2)}) copy-start(f32[1280]{0:T(1024)} %param.37) | copy-start | bytes 15364
  840.4 106.4 %copy-start.33 = (f32[768]{0:T(1024)S(1)}, f32[768]{0:T(1024)}, u32[]{:S(2)}) copy-start(f32[768]{0:T(1024)} %copy-done.32) | copy-start | bytes 9220
  840.4 106.4 %copy-start.35 = (f32[1280]{0:T(1024)S(1)}, f32[1280]{0:T(1024)}, u32[]{:S(2)}) copy-start(f32[1280]{0:T(1024)} %param.38) | copy-start | bytes 15364
  840.4 110.9 %copy-start.51 = (f32[768]{0:T(1024)S(1)}, f32[768]{0:T(1024)}, u32[]{:S(2)}) copy-start(f32[768]{0:T(1024)} %copy-done.50) | copy-start | bytes 9220
  840.4 110.9 %copy-start.45 = (f32[768]{0:T(1024)S(1)}, f32[768]{0:T(1024)}, u32[]{:S(2)}) copy-start(f32[768]{0:T(1024)} %copy-done.44) | copy-start | bytes 9220
  840.5 397.1 %all-gather.17.cloned.1.call-start = ((), (), s32[]{:S(2)}) async-start(), calls=%async_computation.18 | async-start | bytes 9830400 | tf_op jit(solution)/shard_map/all_gather | solution.py:204
  946.8 4.5 copy-start.10
  946.9 4.5 copy-start.14
  951.3 134.4 %copy-start.47 = (f32[768]{0:T(1024)S(1)}, f32[768]{0:T(1024)}, u32[]{:S(2)}) copy-start(f32[768]{0:T(1024)} %copy-done.46) | copy-start | bytes 9220
  951.3 134.4 %copy-start.58 = (f32[1280]{0:T(1024)S(1)}, f32[1280]{0:T(1024)}, u32[]{:S(2)}) copy-start(f32[1280]{0:T(1024)} %param.43) | copy-start | bytes 15364
  1095.8 396.6 %reduce-scatter.27.cloned.1.call-start = ((), (), s32[]{:S(2)}) async-start(), calls=%async_computation.21 | async-start | bytes 3686400 | tf_op jit(solution)/shard_map/reduce_scatter | solution.py:244
  1112.6 381.8 %reduce-scatter.29.cloned.1.call-start = ((), (), s32[]{:S(2)}) async-start(), calls=%async_computation.22 | async-start | bytes 3686400 | tf_op jit(solution)/shard_map/reduce_scatter | solution.py:247
  1112.7 124.8 %copy-start.27 = (bf16[320,1280]{0,1:T(8,128)(2,1)S(1)}, bf16[320,1280]{0,1:T(8,128)(2,1)}, u32[]{:S(2)}) copy-start(bf16[320,1280]{0,1:T(8,128)(2,1)} %all_gather.34) | copy-start | bytes 2457604
  1129.2 368.8 %reduce-scatter.35.cloned.1.call-start = ((), (), s32[]{:S(2)}) async-start(), calls=%async_computation.25 | async-start | bytes 1105920
  1251.4 5.6 copy-start.12
  1331.3 4.9 copy-start.16
  1339.4 5.6 copy-start.12
  1418.5 4.8 copy-start.16
  1432.9 5.2 slice-start
  1444.6 4.3 copy-start.19
  1464.5 72.7 %reduce-scatter.33.cloned.1.call-start = ((), (), s32[]{:S(2)}) async-start(), calls=%async_computation.24 | async-start | bytes 1105920
  1465.9 110.2 %reduce-scatter.31.cloned.1.call-start = ((), (), s32[]{:S(2)}) async-start(), calls=%async_computation.23 | async-start | bytes 1105920
  1467.3 9.9 copy-start.20
  1467.3 9.9 copy-start.23
  1467.3 147.9 %reduce-scatter.25.cloned.1.call-start = ((), (), s32[]{:S(2)}) async-start(), calls=%async_computation.20 | async-start | bytes 1105920 | tf_op jit(solution)/shard_map/reduce_scatter | solution.py:241
  1477.0 277.0 %reduce-scatter.23.cloned.1.call-start = ((), (), s32[]{:S(2)}) async-start(), calls=%async_computation.19 | async-start | bytes 9830400 | tf_op jit(solution)/shard_map/reduce_scatter | solution.py:219
  1491.5 262.5 %copy-start.8 = (bf16[768,1280]{1,0:T(8,128)(2,1)S(1)}, bf16[768,1280]{1,0:T(8,128)(2,1)}, u32[]{:S(2)}) copy-start(bf16[768,1280]{1,0:T(8,128)(2,1)} %param.26) | copy-start | bytes 5898244
  1491.6 262.5 %copy-start.31 = (f32[768]{0:T(1024)S(1)}, f32[768]{0:T(1024)}, u32[]{:S(2)}) copy-start(f32[768]{0:T(1024)} %copy-done.30) | copy-start | bytes 9220
  1491.6 262.5 %copy-start.37 = (f32[1280]{0:T(1024)S(1)}, f32[1280]{0:T(1024)}, u32[]{:S(2)}) copy-start(f32[1280]{0:T(1024)} %param.29) | copy-start | bytes 15364
  1494.4 262.6 %copy-start.49 = (f32[768]{0:T(1024)S(1)}, f32[768]{0:T(1024)}, u32[]{:S(2)}) copy-start(f32[768]{0:T(1024)} %copy-done.48) | copy-start | bytes 9220
  1494.4 262.6 %copy-start.43 = (f32[768]{0:T(1024)S(1)}, f32[768]{0:T(1024)}, u32[]{:S(2)}) copy-start(f32[768]{0:T(1024)} %copy-done.42) | copy-start | bytes 9220
  1616.9 142.4 %copy-start.52 = (f32[1280]{0:T(1024)S(1)}, f32[1280]{0:T(1024)}, u32[]{:S(2)}) copy-start(f32[1280]{0:T(1024)} %get-tuple-element.450) | copy-start | bytes 15364
  1616.9 142.4 %copy-start.53 = (f32[1280]{0:T(1024)S(1)}, f32[1280]{0:T(1024)}, u32[]{:S(2)}) copy-start(f32[1280]{0:T(1024)} %get-tuple-element.446) | copy-start | bytes 15364
  1616.9 142.4 %copy-start.54 = (f32[1280]{0:T(1024)S(1)}, f32[1280]{0:T(1024)}, u32[]{:S(2)}) copy-start(f32[1280]{0:T(1024)} %get-tuple-element.534) | copy-start | bytes 15364
  1616.9 142.4 %copy-start.55 = (f32[1280]{0:T(1024)S(1)}, f32[1280]{0:T(1024)}, u32[]{:S(2)}) copy-start(f32[1280]{0:T(1024)} %get-tuple-element.554) | copy-start | bytes 15364
  (44 other events, 113.2 us)
Sparse Core Ops, SparseCore 0:
  15.2 143.3 all-gather.6
  287.5 134.2 reduce-scatter.16
  812.5 134.2 reduce-scatter.20
  949.0 136.7 reduce-scatter.18
Sparse Core Ops, SparseCore 1:
  289.8 31.1 all-gather.10
  429.0 141.5 all-gather.8
  572.3 31.1 all-gather.12
  605.7 140.7 all-gather.14
  1095.9 141.5 all-gather.16
  1240.9 44.6 reduce-scatter.26
  1288.9 46.7 reduce-scatter.28
  1464.6 33.3 reduce-scatter.34
  1501.4 35.7 reduce-scatter.32
  1540.4 35.6 reduce-scatter.30
  1579.5 35.6 reduce-scatter.24
  1617.6 136.4 reduce-scatter.22
where the time goes:
time: 1820 us
  waiting for transfers between devices  1120 us (62%)
  matrix products  325 us (18%)
  local copies, waits for them, and re-layouts  145 us (8%)
  other arithmetic  115 us (6%)
  blocking collectives  88.1 us (5%)
    all_gather x1, waiting for transfers between devices, local(): lax.all_gather(out_grad.astype(jnp.bfloat16), 'tensor', axis=0, tiled=True)  143 us
    reduce_scatter x1, waiting for transfers between devices, local(): lax.psum_scatter(inner_cols(piece, w_joined).astype(jnp.bfloat16), 'tenso...  137 us
    all_gather x1, waiting for transfers between devices, local(): second_full = lax.all_gather(second_in, 'tensor', axis=0, tiled=True)  136 us
    reduce_scatter x1, waiting for transfers between devices, local(): lax.psum_scatter(jnp.dot(piece, wo_all, preferred_element_type=jnp.float3...  134 us
    reduce_scatter x1, waiting for transfers between devices, local(): lax.psum_scatter(jnp.dot(piece, wdown_all, preferred_element_type=jnp.flo...  131 us
    all_gather x1, waiting for transfers between devices, local(): lax.all_gather(grad_middle.astype(jnp.bfloat16), 'tensor', axis=0, tiled=...  108 us
    reduce_scatter x1, waiting for transfers between devices, local(): lax.psum_scatter(inner_cols(piece, wup_all).astype(jnp.bfloat16), 'tensor...  106 us
    all_gather x1, waiting for transfers between devices, local(): first_full = lax.all_gather(first_in, 'tensor', axis=0, tiled=True)  97.8 us
  transfers between devices with their start and end apart: 16, of which 13 were waited for; matrix products, arithmetic and copies ran while one was open for 19% of the time, Pallas kernels for 0%

commit v1 on v0

v1 whole, which is shorter than its diff:
```python
import functools

import jax
import jax.numpy as jnp
from jax import lax
from jax.experimental import pallas as pl
from jax.experimental.pallas import tpu as pltpu
from jax.sharding import PartitionSpec as P

HDIM = 80
EPS = 1e-05
LOG2E = 1.4426950408889634
F32 = jnp.float32
BF16 = jnp.bfloat16


def norm_rows(values, norm_gain, norm_shift):
    center = values - jnp.mean(values, -1, keepdims=True)
    spread = jnp.mean(center * center, -1, keepdims=True)
    return center * lax.rsqrt(spread + EPS) * norm_gain + norm_shift


def norm_back(values, norm_gain, grad):
    center = values - jnp.mean(values, -1, keepdims=True)
    scale = lax.rsqrt(jnp.mean(center * center, -1, keepdims=True) + EPS)
    normed = center * scale
    scaled = grad * norm_gain
    back = scaled - jnp.mean(scaled, -1, keepdims=True)
    back = (back - normed * jnp.mean(scaled * normed, -1, keepdims=True)) * scale
    return back, jnp.sum(grad * normed, 0), jnp.sum(grad, 0)


def dot_nn(left, right):
    return jnp.dot(left, right, preferred_element_type=F32)


def dot_tn(left, right):
    return lax.dot_general(left, right, (((0,), (0,)), ((), ())), preferred_element_type=F32)


def dot_nt(left, right):
    return lax.dot_general(left, right, (((1,), (1,)), ((), ())), preferred_element_type=F32)


def up_kernel(rows_ref, weight_ref, bias_ref, hidden_ref, slope_ref):
    pre = dot_nn(rows_ref[...], weight_ref[...]) + bias_ref[...]
    cdf = 0.5 * lax.erf(pre * (0.5**0.5)) + 0.5
    density = jnp.exp(-0.5 * pre * pre) * 0.3989422804014327
    hidden_ref[...] = (pre * cdf).astype(BF16)
    slope_ref[...] = (cdf + pre * density).astype(BF16)


def up_gelu(rows, weight, bias):
    count, depth = rows.shape
    cols = weight.shape[1]
    block_rows, block_cols = min(512, count), min(640, cols)
    return pl.pallas_call(
        up_kernel,
        grid=(cols // block_cols, count // block_rows),
        in_specs=[
            pl.BlockSpec((block_rows, depth), lambda n, m: (m, 0)),
            pl.BlockSpec((depth, block_cols), lambda n, m: (0, n)),
            pl.BlockSpec((1, block_cols), lambda n, m: (0, n)),
        ],
        out_specs=[
            pl.BlockSpec((block_rows, block_cols), lambda n, m: (m, n)),
            pl.BlockSpec((block_rows, block_cols), lambda n, m: (m, n)),
        ],
        out_shape=[jax.ShapeDtypeStruct((count, cols), BF16)] * 2,
        cost_estimate=pl.CostEstimate(
            flops=2 * count * depth * cols, bytes_accessed=20_000_000, transcendentals=0
        ),
        compiler_params=pltpu.CompilerParams(vmem_limit_bytes=40 << 20),
        name="up_gelu",
    )(rows, weight, bias)


def attend_kernel(heads, scaling, query_ref, all_ref, mask_ref, out_ref, total_ref):
    width = heads * HDIM
    queries = query_ref[...]
    mask = mask_ref[...]
    outs, totals = [], []
    for head in range(heads):
        low = head * HDIM
        query = queries[:, low : low + HDIM]
        key = all_ref[:, width + low : width + low + HDIM]
        value = all_ref[:, 2 * width + low : 2 * width + low + HDIM]
        scores = dot_nt(query, key) * (scaling * LOG2E) + mask
        row_max = jnp.max(scores, -1, keepdims=True)
        exp_scores = jnp.exp2(scores - row_max)
        total = jnp.sum(exp_scores, -1, keepdims=True)
        mixed = dot_nn(exp_scores.astype(BF16), value)
        outs.append(mixed * (1.0 / total))
        totals.append(row_max + jnp.log2(total))
    out_ref[...] = jnp.concatenate(outs, -1).astype(BF16)
    for head in range(heads):
        wide = jnp.broadcast_to(totals[head], (totals[head].shape[0], 128))
        total_ref[head : head + 1, :] = wide.T[0:1, :]


def attend(joined, mask_row, heads, scaling):
    count, cols = joined.shape
    block_rows = min(256, count)
    width = heads * HDIM
    return pl.pallas_call(
        functools.partial(attend_kernel, heads, scaling),
        grid=(count // block_rows,),
        in_specs=[
            pl.BlockSpec((block_rows, cols), lambda m: (m, 0)),
            pl.BlockSpec((count, cols), lambda m: (0, 0)),
            pl.BlockSpec((1, count), lambda m: (0, 0)),
        ],
        out_specs=[
            pl.BlockSpec((block_rows, width), lambda m: (m, 0)),
            pl.BlockSpec((heads, block_rows), lambda m: (0, m)),
        ],
        out_shape=[
            jax.ShapeDtypeStruct((count, width), BF16),
            jax.ShapeDtypeStruct((heads, count), F32),
        ],
        cost_estimate=pl.CostEstimate(
            flops=2 * heads * count * count * 512,
            bytes_accessed=4_000_000,
            transcendentals=heads * count * count,
        ),
        compiler_params=pltpu.CompilerParams(vmem_limit_bytes=48 << 20),
        name="attend",
    )(joined, joined, mask_row)


def attend_back_kernel(
    heads, scaling, query_ref, all_ref, grad_ref, total_ref, mask_ref,
    out_ref, sums_ref, key_sum, value_sum,
):
    step = pl.program_id(0)
    steps = pl.num_programs(0)
    width = heads * HDIM
    block_rows = query_ref.shape[0]

    @pl.when(step == 0)
    def _():
        key_sum[...] = jnp.zeros_like(key_sum)
        value_sum[...] = jnp.zeros_like(value_sum)
        sums_ref[...] = jnp.zeros_like(sums_ref)

    queries = query_ref[...]
    grads = grad_ref[...]
    query_outs = []
    for head in range(heads):
        low = head * HDIM
        query = queries[:, low : low + HDIM]
        grad = grads[:, low : low + HDIM]
        key = all_ref[:, width + low : width + low + HDIM]
        value = all_ref[:, 2 * width + low : 2 * width + low + HDIM]
        scores = dot_nt(key, query) * (scaling * LOG2E) + mask_ref[...]
        probs = jnp.exp2(scores - total_ref[head : head + 1, :])
        grad_probs = dot_nt(value, grad)
        shared = jnp.sum(probs * grad_probs, 0, keepdims=True)
        grad_scores = (probs * (grad_probs - shared)).astype(BF16)
        value_sum[head, :, :HDIM] += dot_nn(probs.astype(BF16), grad)
        key_sum[head, :, :HDIM] += dot_nn(grad_scores, query)
        query_outs.append(dot_tn(grad_scores, key) * scaling)
    joined = jnp.concatenate(query_outs, -1)
    sums_ref[0:1, :width] += jnp.sum(joined, 0, keepdims=True)
    rows = pl.ds(pl.multiple_of(step * block_rows, block_rows), block_rows)
    out_ref[rows, :width] = joined.astype(BF16)

    @pl.when(step == steps - 1)
    def _():
        keys = jnp.concatenate([key_sum[head, :, :HDIM] for head in range(heads)], -1)
        values = jnp.concatenate([value_sum[head, :, :HDIM] for head in range(heads)], -1)
        sums_ref[1:2, :width] = jnp.sum(values, 0, keepdims=True)
        out_ref[:, width:] = jnp.concatenate([keys * scaling, values], -1).astype(BF16)


def attend_back(joined, grad_heads, totals, mask_col, heads, scaling):
    count, cols = joined.shape
    block_rows = min(256, count)
    width = heads * HDIM
    return pl.pallas_call(
        functools.partial(attend_back_kernel, heads, scaling),
        grid=(count // block_rows,),
        in_specs=[
            pl.BlockSpec((block_rows, cols), lambda m: (m, 0)),
            pl.BlockSpec((count, cols), lambda m: (0, 0)),
            pl.BlockSpec((block_rows, width), lambda m: (m, 0)),
            pl.BlockSpec((heads, block_rows), lambda m: (0, m)),
            pl.BlockSpec((count, 1), lambda m: (0, 0)),
        ],
        out_specs=[
            pl.BlockSpec((count, cols), lambda m: (0, 0)),
            pl.BlockSpec((8, 256), lambda m: (0, 0)),
        ],
        out_shape=[
            jax.ShapeDtypeStruct((count, cols), BF16),
            jax.ShapeDtypeStruct((8, 256), F32),
        ],
        scratch_shapes=[
            pltpu.VMEM((heads, count, 128), F32),
            pltpu.VMEM((heads, count, 128), F32),
        ],
        cost_estimate=pl.CostEstimate(
            flops=2 * heads * count * count * 1280,
            bytes_accessed=5_000_000,
            transcendentals=heads * count * count,
        ),
        compiler_params=pltpu.CompilerParams(vmem_limit_bytes=56 << 20),
        name="attend_back",
    )(joined, joined, grad_heads, totals, mask_col)


class Links:
    def __init__(self):
        self.dp = lax.axis_size("dp")
        self.tensor = lax.axis_size("tensor")
        self.dp_pos = lax.axis_index("dp")
        self.tensor_pos = lax.axis_index("tensor")
        self.chips = self.dp == 8 and self.tensor == 4
        self.half = (self.dp_pos if self.chips else self.tensor_pos) % 2
        if self.chips:
            self.x_odd = (self.dp_pos // 2) % 2 == 1
            self.y_odd = self.dp_pos // 4 == 1

    def pair(self, value):
        if self.chips:
            return lax.ppermute(value, "dp", [(i, i ^ 1) for i in range(self.dp)])
        return lax.ppermute(value, "tensor", [(i, i ^ 1) for i in range(self.tensor)])

    def along_x(self, value):
        return lax.ppermute(value, "dp", [(i, i ^ 2) for i in range(8)])

    def along_y(self, value):
        return lax.ppermute(value, "dp", [(i, i ^ 4) for i in range(8)])

    def along_z(self, value, shift):
        return lax.ppermute(value, "tensor", [(i, (i + shift) % 4) for i in range(4)])

    def move_rows(self, value):
        if not self.chips:
            return value
        swaps = [
            (a * 4 + b, (a ^ 1) * 4 + (b ^ 1)) for a in range(8) for b in range(4) if a % 2 != b % 2
        ]
        moved = lax.ppermute(value, ("dp", "tensor"), swaps)
        return jnp.where(self.half == self.tensor_pos % 2, value, moved)

    def turn(self, value):
        if not self.chips:
            return value
        cut = value.shape[-1] // 4
        parts = [value[..., i * cut : (i + 1) * cut] for i in range(4)]
        value = jnp.where(
            self.x_odd, jnp.concatenate([parts[1], parts[0], parts[3], parts[2]], -1), value
        )
        return jnp.where(
            self.y_odd, jnp.concatenate([value[..., 2 * cut :], value[..., : 2 * cut]], -1), value
        )

    def clip_length(self, lengths):
        if not self.chips:
            own, place = lengths, self.tensor_pos // 2
        else:
            own = jnp.where(self.half == self.tensor_pos % 2, lengths, self.pair(lengths))
            place = self.tensor_pos // 2
        return jnp.sum(jnp.where(jnp.arange(own.shape[0]) == place, own, 0))

    def columns(self, shard):
        rows, _, width = shard.shape
        if not self.chips:
            whole = lax.all_gather(shard, ("dp", "tensor"), axis=0)
            whole = lax.dynamic_index_in_dim(whole, self.half, 2, keepdims=False)
            whole = whole.reshape(self.dp, self.tensor, rows, width)
            return [whole[:, k].reshape(self.dp * rows, width) for k in range(self.tensor)]
        first = self.half == 0
        keep = jnp.where(first, shard[:, 0], shard[:, 1])
        got = self.pair(jnp.where(first, shard[:, 1], shard[:, 0]))
        own = jnp.where(first, jnp.concatenate([keep, got]), jnp.concatenate([got, keep]))
        blocks = []
        for k in range(4):
            here = own if k == 0 else self.along_z(own, k)
            if k % 2 == 0:
                by_x, by_y = self.along_x(here), self.along_y(here)
                by_both = self.along_y(by_x)
            else:
                by_y, by_x = self.along_y(here), self.along_x(here)
                by_both = self.along_x(by_y)
            blocks.append(jnp.concatenate([here, by_x, by_y, by_both]))
        return blocks

    def vectors(self, value):
        if not self.chips:
            whole = lax.all_gather(value, "tensor", axis=0)
            return [whole[k] for k in range(self.tensor)]
        return [value if k == 0 else self.along_z(value, k) for k in range(4)]

    def place(self, pieces):
        halves = (jnp.arange(2) == self.half)[None, :, None]
        total = 0.0
        for k, piece in enumerate(pieces):
            owner = (self.tensor_pos - k) % self.tensor if self.chips else k
            blocks = (jnp.arange(self.tensor) == owner)[:, None, None]
            total = total + jnp.where(halves & blocks, piece[None, None, :], 0.0)
        return total

    def total(self, value):
        if not self.chips:
            return lax.psum(value, ("dp", "tensor"))
        for bit in (1, 2, 4):
            value = value + lax.ppermute(value, "dp", [(i, i ^ bit) for i in range(8)])
        for bit in (1, 2):
            value = value + lax.ppermute(value, "tensor", [(i, i ^ bit) for i in range(4)])
        return value

    def scatter_plane(self, left, right, x_first):
        cut = left.shape[1] // 4

        def part(index):
            return dot_tn(left[:, index * cut : (index + 1) * cut], right)

        near, far = (1, 2) if x_first else (2, 1)
        go, follow = (self.along_x, self.along_y) if x_first else (self.along_y, self.along_x)
        sent_far = go(part(3).astype(BF16))
        sent_near = go(part(near).astype(BF16))
        second = (part(far) + sent_far.astype(F32)).astype(BF16)
        first = part(0) + sent_near.astype(F32)
        return (first + follow(second).astype(F32)).astype(BF16)

    def scatter_line(self, blocks):
        total = blocks[0].astype(F32)
        for k in range(1, 4):
            total = total + self.along_z(blocks[k], -k).astype(F32)
        return total

    def own_rows(self, total):
        rows = total.shape[0] // 2
        first = self.half == 0
        keep = jnp.where(first, total[:rows], total[rows:])
        got = self.pair(jnp.where(first, total[rows:], total[:rows]))
        return jnp.where(
            first, jnp.stack([keep, got], 1), jnp.stack([got, keep], 1)
        )

    def gradient(self, left, rights):
        if not self.chips:
            pieces = []
            for right, count, _ in rights:
                product = dot_tn(left, right).astype(BF16)
                width = product.shape[1] // count
                pieces += [product[:, i * width : (i + 1) * width] for i in range(count)]
            whole = jnp.stack(pieces, 0)
            features, width = whole.shape[1:]
            whole = whole.reshape(self.tensor, self.dp, features // self.dp, width)
            whole = jnp.moveaxis(whole, 1, 0)[:, :, :, None, :]
            halves = (jnp.arange(2) == self.half)[None, None, None, :, None]
            whole = jnp.where(halves, whole, jnp.zeros((), BF16))
            whole = whole.reshape((self.dp * self.tensor,) + whole.shape[2:])
            return lax.psum_scatter(whole, ("dp", "tensor"), tiled=False).astype(F32)
        blocks = []
        for right, count, x_first in rights:
            product = self.scatter_plane(left, right, x_first)
            width = product.shape[1] // count
            blocks += [product[:, i * width : (i + 1) * width] for i in range(count)]
        return self.own_rows(self.scatter_line(blocks))

    def merged(self, partial_of):
        got = self.pair(partial_of(1).astype(BF16))
        return partial_of(0) + got.astype(F32)


def local(
    tokens,
    lengths,
    cotangent,
    norm1_gain,
    norm1_shift,
    query_weight,
    query_bias,
    key_weight,
    value_weight,
    value_bias,
    out_weight,
    out_bias,
    norm2_gain,
    norm2_shift,
    up_weight,
    up_bias,
    down_weight,
    down_bias,
):
    links = Links()
    rows = tokens.shape[0]
    scaling = HDIM ** (-0.5)
    width = query_weight.shape[1] // 2
    heads = width // HDIM
    units = up_weight.shape[1] // 2
    count = links.tensor

    def halves(weight):
        return weight.reshape(weight.shape[0], 2, weight.shape[1] // 2)

    shard_attn = jnp.concatenate(
        [halves(query_weight), halves(key_weight), halves(value_weight), halves(out_weight.T)], -1
    )
    w_attn = links.columns(shard_attn)
    w_up = links.columns(halves(up_weight))
    w_down = links.columns(halves(down_weight.T))
    w_qkv = [block[:, : 3 * width] for block in w_attn]
    w_out = [block[:, 3 * width :] for block in w_attn]

    order = [0, 2, 1, 3] if links.chips else list(range(count))
    small = jnp.concatenate(
        [query_bias.reshape(2, width), value_bias.reshape(2, width), up_bias.reshape(2, units)], -1
    )
    small = links.vectors(jnp.where(links.half == 0, small[0], small[1]))
    bias_qkv = [
        jnp.concatenate([v[:width], jnp.zeros((width,), F32), v[width : 2 * width]]) for v in small
    ]
    bias_up = jnp.concatenate([small[k][2 * width :] for k in order])
    gain_one, shift_one, gain_two, shift_two, bias_out, bias_down = (
        links.turn(v)
        for v in (norm1_gain, norm1_shift, norm2_gain, norm2_shift, out_bias, down_bias)
    )

    clip_length = links.clip_length(lengths)
    frames = jnp.arange(rows)
    frames = jnp.concatenate([links.half * rows + frames, (1 - links.half) * rows + frames])
    visible = frames < clip_length
    mask = jnp.where(visible, 0.0, -1e30).astype(F32)

    source = links.turn(links.move_rows(tokens)).astype(F32)
    first_own = norm_rows(source, gain_one, shift_one).astype(BF16)
    first = jnp.concatenate([first_own, links.pair(first_own)])
    joined, heads_out, totals = [], [], []
    for k in range(count):
        joined.append((dot_nn(first, w_qkv[k]) + bias_qkv[k]).astype(BF16))
        mixed, total = attend(joined[k], mask[None, :], heads, scaling)
        heads_out.append(mixed)
        totals.append(total)
    heads_all = jnp.concatenate(heads_out, 1)
    w_out_all = jnp.concatenate(w_out, 1)
    branch = links.merged(
        lambda part: dot_nt(heads_all[part * rows : (part + 1) * rows], w_out_all)
    )
    middle = source + branch + bias_out
    second_own = norm_rows(middle, gain_two, shift_two).astype(BF16)
    second = jnp.concatenate([second_own, links.pair(second_own)])
    w_up_all = jnp.concatenate([w_up[k] for k in order], 1)
    hidden, slope = up_gelu(second, w_up_all, bias_up[None, :])
    w_down_all = jnp.concatenate([w_down[k] for k in order], 1)

    valid = visible[:rows].astype(BF16)[:, None]
    out_own = links.turn(links.move_rows(cotangent)) * valid
    out_grad = jnp.concatenate([out_own, links.pair(out_own)])
    if links.chips:
        groups = [(slice(0, 2 * units), 2, True), (slice(2 * units, 4 * units), 2, False)]
    else:
        groups = [(slice(0, count * units), count, True)]
    order_back = [order.index(k) for k in range(count)]

    def blocks_of(value):
        return [(value[:, cols], number, x_first) for cols, number, x_first in groups]

    grad_down = links_gradient(links, out_grad, blocks_of(hidden), order)

    down_out = links.merged(
        lambda part: dot_nt(hidden[part * rows : (part + 1) * rows], w_down_all)
    )
    layer_out = (middle + down_out + bias_down).astype(BF16)
    layer_out = links.move_rows(links.turn(layer_out))

    grad_pre = (dot_nn(out_grad, w_down_all) * slope.astype(F32)).astype(BF16)
    grad_up = links_gradient(links, second, blocks_of(grad_pre), order)
    grad_second = links.merged(
        lambda part: dot_nt(grad_pre[part * rows : (part + 1) * rows], w_up_all)
    )
    back_two, grad_gain_two, grad_shift_two = norm_back(middle, gain_two, grad_second)
    grad_middle = out_own.astype(F32) + back_two
    branch_own = grad_middle.astype(BF16)
    branch_grad = jnp.concatenate([branch_own, links.pair(branch_own)])
    grad_heads = [dot_nn(branch_grad, w_out[k]).astype(BF16) for k in range(count)]
    grad_out_w = links_gradient(links, branch_grad, [(heads_all, count, True)], None)
    grad_joined, grad_qkv, sums = [], [], []
    for k in range(count):
        back, sum_k = attend_back(joined[k], grad_heads[k], totals[k], mask[:, None], heads, scaling)
        grad_joined.append(back)
        sums.append(sum_k)
    grad_qkv = links_gradient(
        links, first, [(grad_joined[k], 1, k % 2 == 0) for k in range(count)], None
    )
    grad_all = jnp.concatenate(grad_joined, 1)
    w_qkv_all = jnp.concatenate(w_qkv, 1)
    grad_first = links.merged(
        lambda part: dot_nt(grad_all[part * rows : (part + 1) * rows], w_qkv_all)
    )
    back_one, grad_gain_one, grad_shift_one = norm_back(source, gain_one, grad_first)
    grad_tokens = (grad_middle + back_one).astype(BF16)
    grad_tokens = links.move_rows(links.turn(grad_tokens))

    up_sum = jnp.sum(grad_pre.astype(F32), 0)
    up_pieces = [
        up_sum[order_back[k] * units : (order_back[k] + 1) * units] for k in range(count)
    ]
    early = [links.place(up_pieces).reshape(-1)] + [
        links.turn(v)
        for v in (
            jnp.sum(grad_middle, 0),
            grad_gain_two,
            grad_shift_two,
            jnp.sum(out_own.astype(F32), 0),
        )
    ]
    late = [
        links.place([s[0, :width] for s in sums]).reshape(-1),
        links.place([s[1, :width] for s in sums]).reshape(-1),
        links.turn(grad_gain_one),
        links.turn(grad_shift_one),
    ]

    def summed(vectors):
        whole = links.total(jnp.concatenate(vectors))
        at = 0
        result = []
        for vector in vectors:
            result.append(whole[at : at + vector.shape[0]])
            at += vector.shape[0]
        return result

    sum_up, sum_out, sum_gain_two, sum_shift_two, sum_down = summed(early)
    sum_query, sum_value, sum_gain_one, sum_shift_one = summed(late)

    def own(vector):
        size = vector.shape[0] // count
        return lax.dynamic_slice_in_dim(vector, links.tensor_pos * size, size, 0)

    def flat(piece):
        return piece.reshape(piece.shape[0], -1)

    return (
        layer_out,
        grad_tokens,
        sum_gain_one,
        sum_shift_one,
        flat(grad_qkv[:, :, :width]),
        own(sum_query),
        flat(grad_qkv[:, :, width : 2 * width]),
        flat(grad_qkv[:, :, 2 * width :]),
        own(sum_value),
        flat(grad_out_w).T,
        sum_out,
        sum_gain_two,
        sum_shift_two,
        flat(grad_up),
        own(sum_up),
        flat(grad_down).T,
        sum_down,
    )


def links_gradient(links, left, rights, order):
    if order is None or not links.chips:
        return links.gradient(left, rights)
    blocks = []
    for right, count, x_first in rights:
        product = links.scatter_plane(left, right, x_first)
        size = product.shape[1] // count
        blocks += [product[:, i * size : (i + 1) * size] for i in range(count)]
    return links.own_rows(links.scatter_line([blocks[order.index(k)] for k in range(4)]))


def solution(mesh):
    rows = P(("dp", "tensor"), None)
    wide, tall = P("dp", "tensor"), P("tensor", "dp")
    piece, same = P("tensor"), P()
    return jax.shard_map(
        local,
        mesh=mesh,
        in_specs=(
            rows, P("dp"), rows, same, same, wide, piece, wide, wide, piece, tall, same, same, same,
            wide, piece, tall, same,
        ),
        out_specs=(
            rows, rows, same, same, wide, piece, wide, wide, piece, tall, same, same, same, wide, piece,
            tall, same,
        ),
        check_vma=False,
    )
```

time: 1820 us -> 1010 us (0.55)
  waiting for transfers between devices: 1120 us -> 233 us
  starting transfers between devices: 1.47 us -> 166 us
  Pallas kernels: 0 us -> 158 us
  matrix products: 325 us -> 192 us
  blocking collectives: 88.1 us -> 0 us
  local copies, waits for them, and re-layouts: 145 us -> 94.3 us
  other arithmetic: 115 us -> 156 us
    reduce_scatter x7 -> x0, waiting for transfers between devices: 546 us -> none  [the longest x1 137 us: local(): lax.psum_scatter(inner_cols(piece, w_joined).astype(jnp.bfloat16), 'tenso...]
    all_gather x6 -> x0, waiting for transfers between devices: 501 us -> none  [the longest x1 143 us: local(): lax.all_gather(out_grad.astype(jnp.bfloat16), 'tensor', axis=0, tiled=True)]
    ppermute x0 -> x117, waiting for transfers between devices: none -> 233 us  [the longest x31 97.1 us: along_y(): return lax.ppermute(value, 'dp', [(i, i ^ 4) for i in range(8)])]
    ppermute x0 -> x117, starting transfers between devices: none -> 166 us  [the longest x16 48.9 us: pair(): return lax.ppermute(value, 'dp', [(i, i ^ 1) for i in range(self.dp)])]
    pallas_call x0 -> x9, Pallas kernels: none -> 158 us  [the longest x4 93.8 us: attend_back(): pl.pallas_call(functools.partial(attend_back_kernel, heads, scaling), gri...]
    dot_general x54 -> x53, matrix products: 325 us -> 192 us  [the longest x36 95.9 us: dot_tn(): lax.dot_general(left, right, (((0,), (0,)), ((), ())), preferred_element_...]
    concatenate x0 -> x12, other arithmetic: none -> 111 us  [the longest x1 52.1 us: local(): w_down_all = jnp.concatenate([w_down[k] for k in order], 1)]
    unnamed x19 -> x0, waiting for transfers between devices: 76.8 us -> none
  transfers between devices with their start and end apart: 16 -> 117, of which waited for: 13 -> 37; matrix products, arithmetic and copies ran while one was open for 19% -> 37% of each run, Pallas kernels for 0% -> 6%
where the time goes in v1:
time: 1010 us; the launch traced here: 1000 us
  waiting for transfers between devices  233 us (23%)
  matrix products  192 us (19%)
  starting transfers between devices  166 us (16%)
  Pallas kernels  158 us (16%)
  other arithmetic  156 us (15%)
  local copies, waits for them, and re-layouts  94.3 us (9%)
    ppermute x31, waiting for transfers between devices, along_y(): return lax.ppermute(value, 'dp', [(i, i ^ 4) for i in range(8)])  97.1 us
    dot_general x36, matrix products, dot_tn(): lax.dot_general(left, right, (((0,), (0,)), ((), ())), preferred_element_...  95.9 us
    pallas_call x4, Pallas kernels, attend_back(): pl.pallas_call(functools.partial(attend_back_kernel, heads, scaling), gri...  93.8 us
    ppermute x24, waiting for transfers between devices, along_z(): lax.ppermute(value, 'tensor', [(i, (i + shift) % 4) for i in range(4)])  75.2 us
    dot_general x8, matrix products, dot_nt(): lax.dot_general(left, right, (((1,), (1,)), ((), ())), preferred_element_...  57.4 us
    concatenate x1, other arithmetic, local(): w_down_all = jnp.concatenate([w_down[k] for k in order], 1)  52.1 us
    ppermute x16, starting transfers between devices, pair(): return lax.ppermute(value, 'dp', [(i, i ^ 1) for i in range(self.dp)])  48.9 us
    ppermute x32, waiting for transfers between devices, along_x(): return lax.ppermute(value, 'dp', [(i, i ^ 2) for i in range(8)])  48.9 us
  transfers between devices with their start and end apart: 117, of which 37 were waited for; matrix products, arithmetic and copies ran while one was open for 37% of the time, Pallas kernels for 6%

profile of v1, /device:TPU:1, one launch (start us, length us, event | category | flops | bytes accessed | tf_op | source)
XLA Modules:
  0.0 1002.5 jit_solution(5454497421813680338)
XLA Ops:
  30.9 27.7 %collective-permute-done.7 = bf16[320,640]{1,0:T(8,128)(2,1)S(1)} collective-permute-done((bf16[320,640]{1,0:T(8,128)(2,1)S(1)}, bf16[320,640]{1,0:T(8,128)(2,1)S(1)}, u32[]{:S(2)}, u32[]{:S(2)}) %collective-permute-start.7) | collective-permute-done | bytes 409632 | tf_op jit(solution)/shard_map/ppermute | solution.py:236
  70.4 5.8 collective-permute-done.13
  78.4 8.7 collective-permute-done.4
  87.1 8.9 collective-permute-done.5
  97.5 4.4 collective-permute-start.36
  112.6 4.5 concatenate.236
  122.5 12.0 %collective-permute-done.34 = bf16[320,640]{1,0:T(8,128)(2,1)S(1)} collective-permute-done((bf16[320,640]{1,0:T(8,128)(2,1)}, bf16[320,640]{1,0:T(8,128)(2,1)S(1)}, u32[]{:S(2)}, u32[]{:S(2)}) %collective-permute-start.34) | collective-permute-done | bytes 409632 | tf_op jit(solution)/shard_map/ppermute | solution.py:233
  134.7 8.6 collective-permute-done.38
  146.4 5.6 collective-permute-done.27
  153.9 6.9 collective-permute-done.31
  162.9 10.3 %collective-permute-start.1 = (bf16[768,1280]{1,0:T(8,128)(2,1)S(1)}, bf16[768,1280]{1,0:T(8,128)(2,1)S(1)}, u32[]{:S(2)}, u32[]{:S(2)}) collective-permute-start(bf16[768,1280]{1,0:T(8,128)(2,1)S(1)} %fusion.7), channel_id=1, source_target_pairs={{0,4},{4,0},{8,12},{12,8},{16,20},{20,16},{24,28},{28,24},{1,5},{5... | collective-permute-start | bytes 5898248 | tf_op jit(solution)/shard_map/ppermute | solution.py:226
  173.3 47.0 %maximum_maximum_fusion.weight_ref = bf16[1280,2560]{1,0:T(8,128)(2,1)} fusion(bf16[320,640]{1,0:T(8,128)(2,1)S(1)} %collective-permute-done.39, bf16[320,640]{1,0:T(8,128)(2,1)S(1)} %collective-permute-done.38, bf16[320,640]{1,0:T(8,128)(2,1)S(1)} %collective-permute-done.37, bf16[320,640]{1,0:T(8,128)(2,1)} %collective-permute-done.36, ...), kind=kLoop, calls=%fused_computation.2 | loop fusion | flops 104857600 | bytes 13107200 | tf_op jit(solution)/shard_map/concatenate | solution.py:447
  232.6 11.2 %attend.4 = (bf16[1536,160]{1,0:T(8,128)(2,1)S(1)}, f32[2,1536]{1,0:T(2,128)S(1)}) custom-call(bf16[1536,480]{1,0:T(8,128)(2,1)S(1)} %fusion.34.query_ref.all_ref, bf16[1536,480]{1,0:T(8,128)(2,1)S(1)} %fusion.34.query_ref.all_ref, f32[1,1536]{1,0:T(1,128)S(1)} %compare_select_fusion.mask_ref), custom_call_target="tpu_custom_call" | custom-call | flops 4831838208 | bytes 4000000 | tf_op jit(solution)/shard_map/attend/pallas_call | solution.py:105
  246.7 10.8 %attend.5 = (bf16[1536,160]{1,0:T(8,128)(2,1)S(1)}, f32[2,1536]{1,0:T(2,128)S(1)}) custom-call(bf16[1536,480]{1,0:T(8,128)(2,1)S(1)} %fusion.35.query_ref.all_ref, bf16[1536,480]{1,0:T(8,128)(2,1)S(1)} %fusion.35.query_ref.all_ref, f32[1,1536]{1,0:T(1,128)S(1)} %compare_select_fusion.mask_ref), custom_call_target="tpu_custom_call" | custom-call | flops 4831838208 | bytes 4000000 | tf_op jit(solution)/shard_map/attend/pallas_call | solution.py:105
  257.5 3.9 fusion.36.query_ref.all_ref
  263.7 10.8 %attend.6 = (bf16[1536,160]{1,0:T(8,128)(2,1)S(1)}, f32[2,1536]{1,0:T(2,128)S(1)}) custom-call(bf16[1536,480]{1,0:T(8,128)(2,1)S(1)} %fusion.36.query_ref.all_ref, bf16[1536,480]{1,0:T(8,128)(2,1)S(1)} %fusion.36.query_ref.all_ref, f32[1,1536]{1,0:T(1,128)S(1)} %compare_select_fusion.mask_ref), custom_call_target="tpu_custom_call" | custom-call | flops 4831838208 | bytes 4000000 | tf_op jit(solution)/shard_map/attend/pallas_call | solution.py:105
  277.7 10.9 %attend.7 = (bf16[1536,160]{1,0:T(8,128)(2,1)S(1)}, f32[2,1536]{1,0:T(2,128)S(1)}) custom-call(bf16[1536,480]{1,0:T(8,128)(2,1)S(1)} %fusion.37.query_ref.all_ref, bf16[1536,480]{1,0:T(8,128)(2,1)S(1)} %fusion.37.query_ref.all_ref, f32[1,1536]{1,0:T(1,128)S(1)} %compare_select_fusion.mask_ref), custom_call_target="tpu_custom_call" | custom-call | flops 4831838208 | bytes 4000000 | tf_op jit(solution)/shard_map/attend/pallas_call | solution.py:105
  293.7 8.6 collective-permute-done.54
  314.1 5.7 collective-permute-done.47
  319.8 52.1 %maximum_maximum_fusion.1 = bf16[1280,2560]{1,0:T(8,128)(2,1)} fusion(bf16[320,640]{1,0:T(8,128)(2,1)S(1)} %collective-permute-done.55, bf16[320,640]{1,0:T(8,128)(2,1)} %collective-permute-done.54, bf16[320,640]{1,0:T(8,128)(2,1)S(1)} %collective-permute-done.53, bf16[320,640]{1,0:T(8,128)(2,1)} %collective-permute-done.52, ...), kind=kLoop, calls=%fused_computation.3 | loop fusion | flops 104857600 | bytes 13107200 | tf_op jit(solution)/shard_map/concatenate | solution.py:449
  375.5 9.1 concatenate.295
  388.0 4.7 concatenate.286
  392.7 5.4 fusion.202
  408.8 6.0 fusion.106
  417.3 20.5 %up_gelu.1 = (bf16[1536,2560]{1,0:T(8,128)(2,1)}, bf16[1536,2560]{1,0:T(8,128)(2,1)}) custom-call(bf16[1536,1280]{1,0:T(8,128)(2,1)S(1)} %pad_maximum_fusion.1.rows_ref, bf16[1280,2560]{1,0:T(8,128)(2,1)S(1)} %bitcast.91, f32[1,2560]{1,0:T(1,128)S(1)} %broadcast_in_dim.232.bias_ref), custom_call_target="tpu_custom_call" | custom-call | flops 10066329600 | bytes 20000000 | tf_op jit(solution)/shard_map/up_gelu/pallas_call | solution.py:57
  437.8 5.3 convolution_convert_fusion.5
  444.4 3.8 convolution_convert_fusion.4
  448.4 3.8 convolution_convert_fusion.3
  453.4 3.9 convolution_convert_fusion.2
  457.6 6.5 fusion.28
  464.1 16.1 %convert_reduce_fusion = (f32[2560]{0:T(1024)S(1)}, bf16[1536,2560]{1,0:T(8,128)(2,1)}) fusion(bf16[1536,2560]{1,0:T(8,128)(2,1)} %get-tuple-element.40, bf16[1280,2560]{1,0:T(8,128)(2,1)S(1)} %bitcast.95, bf16[768,1280]{1,0:T(8,128)(2,1)} %collective-permute-done.59, bf16[768,1280]{1,0:T(8,128)(2,1)} %get-tuple-element.62), kind=kOutput, calls=%fused_computation | convolution fusion | flops 10093852672 | bytes 26224640 | tf_op jit(solution)/shard_map/dot_general | solution.py:34
  480.2 8.3 fusion.31
  488.5 3.9 convolution_convert_fusion.9
  504.1 4.3 fusion.46
  509.6 4.5 fusion.47
  514.1 14.7 %collective-permute-done.98 = bf16[320,1280]{1,0:T(8,128)(2,1)S(1)} collective-permute-done((bf16[320,1280]{1,0:T(8,128)(2,1)S(1)}, bf16[320,1280]{1,0:T(8,128)(2,1)S(1)}, u32[]{:S(2)}, u32[]{:S(2)}) %collective-permute-start.98) | collective-permute-done | bytes 819232 | tf_op jit(solution)/shard_map/ppermute | solution.py:230
  538.0 8.5 collective-permute-done.109
  551.4 5.5 collective-permute-start.60
  556.9 7.1 collective-permute-done.99
  564.0 5.6 collective-permute-start.56
  583.3 11.0 %collective-permute-done.102 = bf16[320,1280]{1,0:T(8,128)(2,1)S(1)} collective-permute-done((bf16[320,1280]{1,0:T(8,128)(2,1)S(1)}, bf16[320,1280]{1,0:T(8,128)(2,1)S(1)}, u32[]{:S(2)}, u32[]{:S(2)}) %collective-permute-start.102) | collective-permute-done | bytes 819232 | tf_op jit(solution)/shard_map/ppermute | solution.py:230
  594.4 4.2 fusion.49
  601.7 8.3 multiply_reduce_fusion
  610.2 4.7 fusion.152
  621.9 11.0 %add_convert_fusion = bf16[768,1280]{1,0:T(8,128)(2,1)S(1)} fusion(f32[768,1280]{1,0:T(8,128)} %copy-done.21, bf16[768,1280]{1,0:T(8,128)(2,1)} %collective-permute-done.56, bf16[1280,2560]{1,0:T(8,128)(2,1)} %maximum_maximum_fusion.1, bf16[1536,2560]{1,0:T(8,128)(2,1)} %get-tuple-element.39, f32[1280]{0:T(1024)S(1)} %copy-done.105), kind=kOutput, calls=%fused_computation.70 | convolution fusion | flops 5038080000 | bytes 18355200 | tf_op jit(solution)/shard_map/dot_general | solution.py:42
  634.5 4.5 concatenate.284
  651.9 11.0 %collective-permute-done.103 = bf16[320,640]{1,0:T(8,128)(2,1)S(1)} collective-permute-done((bf16[320,640]{1,0:T(8,128)(2,1)S(1)}, bf16[320,640]{1,0:T(8,128)(2,1)S(1)}, u32[]{:S(2)}, u32[]{:S(2)}) %collective-permute-start.103) | collective-permute-done | bytes 409632 | tf_op jit(solution)/shard_map/ppermute | solution.py:236
  678.1 23.5 %attend_back.4 = (bf16[1536,480]{1,0:T(8,128)(2,1)}, f32[8,256]{1,0:T(8,128)}) custom-call(bf16[1536,480]{1,0:T(8,128)(2,1)} %copy-done.3, bf16[1536,480]{1,0:T(8,128)(2,1)} %copy-done.3, bf16[1536,160]{1,0:T(8,128)(2,1)} %copy.104.grad_ref, f32[2,1536]{1,0:T(2,128)} %copy-done.5, f32[1536,1]{1,0:T(8,128)} %broadcast_select_fusion.8.mask_ref), custom_call_target="tpu_custom_call" | custom-call | flops 12079595520 | bytes 5000000 | tf_op jit(solution)/shard_map/attend_back/pallas_call | solution.py:180
  711.7 23.5 %attend_back.6 = (bf16[1536,480]{1,0:T(8,128)(2,1)}, f32[8,256]{1,0:T(8,128)}) custom-call(bf16[1536,480]{1,0:T(8,128)(2,1)} %copy-done.2, bf16[1536,480]{1,0:T(8,128)(2,1)} %copy-done.2, bf16[1536,160]{1,0:T(8,128)(2,1)} %copy.106.grad_ref, f32[2,1536]{1,0:T(2,128)} %copy-done.6, f32[1536,1]{1,0:T(8,128)} %broadcast_select_fusion.8.mask_ref), custom_call_target="tpu_custom_call" | custom-call | flops 12079595520 | bytes 5000000 | tf_op jit(solution)/shard_map/attend_back/pallas_call | solution.py:180
  745.4 23.3 %attend_back.5 = (bf16[1536,480]{1,0:T(8,128)(2,1)}, f32[8,256]{1,0:T(8,128)}) custom-call(bf16[1536,480]{1,0:T(8,128)(2,1)} %copy-done.1, bf16[1536,480]{1,0:T(8,128)(2,1)} %copy-done.1, bf16[1536,160]{1,0:T(8,128)(2,1)} %copy.105.grad_ref, f32[2,1536]{1,0:T(2,128)} %copy-done.4, f32[1536,1]{1,0:T(8,128)} %broadcast_select_fusion.8.mask_ref), custom_call_target="tpu_custom_call" | custom-call | flops 12079595520 | bytes 5000000 | tf_op jit(solution)/shard_map/attend_back/pallas_call | solution.py:180
  778.9 23.6 %attend_back.7 = (bf16[1536,480]{1,0:T(8,128)(2,1)}, f32[8,256]{1,0:T(8,128)}) custom-call(bf16[1536,480]{1,0:T(8,128)(2,1)} %copy-done, bf16[1536,480]{1,0:T(8,128)(2,1)} %copy-done, bf16[1536,160]{1,0:T(8,128)(2,1)} %copy.107.grad_ref, f32[2,1536]{1,0:T(2,128)} %copy-done.7, f32[1536,1]{1,0:T(8,128)} %broadcast_select_fusion.8.mask_ref), custom_call_target="tpu_custom_call" | custom-call | flops 12079595520 | bytes 5000000 | tf_op jit(solution)/shard_map/attend_back/pallas_call | solution.py:180
  805.3 10.6 %concatenate.294 = bf16[1536,1920]{1,0:T(8,128)(2,1)} concatenate(bf16[1536,480]{1,0:T(8,128)(2,1)S(1)} %copy-done.13, bf16[1536,480]{1,0:T(8,128)(2,1)} %get-tuple-element.44, bf16[1536,480]{1,0:T(8,128)(2,1)} %get-tuple-element.46, bf16[1536,480]{1,0:T(8,128)(2,1)} %get-tuple-element.48), dimensions={1} | concatenate | bytes 11796480 | tf_op jit(solution)/shard_map/concatenate | solution.py:490
  830.4 8.1 convolution_convert_fusion.1
  850.3 8.0 collective-permute-done.77
  859.9 4.3 collective-permute-done.81
  869.1 9.2 collective-permute-start.62
  888.5 5.6 collective-permute-done.69
  899.8 10.9 %collective-permute-start.57 = (bf16[768,1280]{1,0:T(8,128)(2,1)}, bf16[768,1280]{1,0:T(8,128)(2,1)}, u32[]{:S(2)}, u32[]{:S(2)}) collective-permute-start(bf16[768,1280]{1,0:T(8,128)(2,1)} %maximum_select_fusion.1), channel_id=1, source_target_pairs={{1,4},{3,6},{4,1},{6,3},{9,12},{11,14},{12,9},{14,11},{17,20},{19,... | collective-permute-start | bytes 5898248 | tf_op jit(solution)/shard_map/ppermute | solution.py:244
  910.7 12.1 %collective-permute-done.79 = bf16[320,480]{1,0:T(8,128)(2,1)S(1)} collective-permute-done((bf16[320,480]{1,0:T(8,128)(2,1)S(1)}, bf16[320,480]{1,0:T(8,128)(2,1)S(1)}, u32[]{:S(2)}, u32[]{:S(2)}) %collective-permute-start.79) | collective-permute-done | bytes 307232 | tf_op jit(solution)/shard_map/ppermute | solution.py:236
  926.9 20.2 %collective-permute-done.88 = bf16[320,160]{1,0:T(8,128)(2,1)S(1)} collective-permute-done((bf16[320,160]{1,0:T(8,128)(2,1)S(1)}, bf16[320,160]{1,0:T(8,128)(2,1)S(1)}, u32[]{:S(2)}, u32[]{:S(2)}) %collective-permute-start.88) | collective-permute-done | bytes 102432 | tf_op jit(solution)/shard_map/ppermute | solution.py:236
  947.0 6.1 collective-permute-start.84
  954.0 6.6 fusion.13
  964.1 4.5 concatenate.296
  984.7 8.8 collective-permute-done.67
  (746 shorter events, 323.7 us)
Async XLA Ops:
  16.7 91.1 %collective-permute-start = (bf16[768,1280]{1,0:T(8,128)(2,1)}, bf16[768,1280]{1,0:T(8,128)(2,1)}, u32[]{:S(2)}, u32[]{:S(2)}) collective-permute-start(bf16[768,1280]{1,0:T(8,128)(2,1)} %param.18), channel_id=1, source_target_pairs={{1,4},{3,6},{4,1},{6,3},{9,12},{11,14},{12,9},{14,11},{17,20},{19,... | collective-permute-start | bytes 5898248 | tf_op jit(solution)/shard_map/ppermute | solution.py:244
  24.9 34.9 %collective-permute-start.3 = (bf16[320,640]{1,0:T(8,128)(2,1)S(1)}, bf16[320,640]{1,0:T(8,128)(2,1)S(1)}, u32[]{:S(2)}, u32[]{:S(2)}) collective-permute-start(bf16[320,640]{1,0:T(8,128)(2,1)S(1)} %maximum_select_fusion.7), channel_id=1, source_target_pairs={{0,8},{4,12},{8,0},{12,4},{16,24},{20,28},{24,16},{28,20},{1,9},{5... | collective-permute-start | bytes 1228808 | tf_op jit(solution)/shard_map/ppermute | solution.py:230
  26.2 32.4 %collective-permute-start.7 = (bf16[320,640]{1,0:T(8,128)(2,1)S(1)}, bf16[320,640]{1,0:T(8,128)(2,1)S(1)}, u32[]{:S(2)}, u32[]{:S(2)}) collective-permute-start(bf16[320,640]{1,0:T(8,128)(2,1)S(1)} %maximum_select_fusion.7), channel_id=1, source_target_pairs={{0,1},{1,2},{2,3},{3,0},{4,5},{5,6},{6,7},{7,4},{8,9},{9,10},{10,1... | collective-permute-start | bytes 1228808 | tf_op jit(solution)/shard_map/ppermute | solution.py:236
  27.3 35.7 %collective-permute-start.12 = (bf16[320,640]{1,0:T(8,128)(2,1)S(1)}, bf16[320,640]{1,0:T(8,128)(2,1)S(1)}, u32[]{:S(2)}, u32[]{:S(2)}) collective-permute-start(bf16[320,640]{1,0:T(8,128)(2,1)S(1)} %maximum_select_fusion.7), channel_id=1, source_target_pairs={{0,2},{1,3},{2,0},{3,1},{4,6},{5,7},{6,4},{7,5},{8,10},{9,11},{10,... | collective-permute-start | bytes 1228808 | tf_op jit(solution)/shard_map/ppermute | solution.py:236
  27.5 39.9 %collective-permute-start.17 = (bf16[320,640]{1,0:T(8,128)(2,1)S(1)}, bf16[320,640]{1,0:T(8,128)(2,1)S(1)}, u32[]{:S(2)}, u32[]{:S(2)}) collective-permute-start(bf16[320,640]{1,0:T(8,128)(2,1)S(1)} %maximum_select_fusion.7), channel_id=1, source_target_pairs={{0,3},{1,0},{2,1},{3,2},{4,7},{5,4},{6,5},{7,6},{8,11},{9,8},{10,9... | collective-permute-start | bytes 1228808 | tf_op jit(solution)/shard_map/ppermute | solution.py:236
  69.0 27.0 %collective-permute-start.5 = (bf16[320,640]{1,0:T(8,128)(2,1)S(1)}, bf16[320,640]{1,0:T(8,128)(2,1)S(1)}, u32[]{:S(2)}, u32[]{:S(2)}) collective-permute-start(bf16[320,640]{1,0:T(8,128)(2,1)S(1)} %collective-permute-done.3), channel_id=1, source_target_pairs={{0,16},{4,20},{8,24},{12,28},{16,0},{20,4},{24,8},{28,12},{1,17},{... | collective-permute-start | bytes 1228808 | tf_op jit(solution)/shard_map/ppermute | solution.py:233
  76.1 30.4 %collective-permute-start.28 = (bf16[320,640]{1,0:T(8,128)(2,1)}, bf16[320,640]{1,0:T(8,128)(2,1)}, u32[]{:S(2)}, u32[]{:S(2)}) collective-permute-start(bf16[320,640]{1,0:T(8,128)(2,1)} %maximum_select_fusion.8), channel_id=1, source_target_pairs={{0,2},{1,3},{2,0},{3,1},{4,6},{5,7},{6,4},{7,5},{8,10},{9,11},{10,... | collective-permute-start | bytes 1228808 | tf_op jit(solution)/shard_map/ppermute | solution.py:236
  87.1 31.1 %collective-permute-start.32 = (bf16[320,640]{1,0:T(8,128)(2,1)}, bf16[320,640]{1,0:T(8,128)(2,1)}, u32[]{:S(2)}, u32[]{:S(2)}) collective-permute-start(bf16[320,640]{1,0:T(8,128)(2,1)} %maximum_select_fusion.8), channel_id=1, source_target_pairs={{0,1},{1,2},{2,3},{3,0},{4,5},{5,6},{6,7},{7,4},{8,9},{9,10},{10,1... | collective-permute-start | bytes 1228808 | tf_op jit(solution)/shard_map/ppermute | solution.py:236
  97.5 21.0 %collective-permute-start.36 = (bf16[320,640]{1,0:T(8,128)(2,1)}, bf16[320,640]{1,0:T(8,128)(2,1)}, u32[]{:S(2)}, u32[]{:S(2)}) collective-permute-start(bf16[320,640]{1,0:T(8,128)(2,1)} %maximum_select_fusion.8), channel_id=1, source_target_pairs={{0,3},{1,0},{2,1},{3,2},{4,7},{5,4},{6,5},{7,6},{8,11},{9,8},{10,9... | collective-permute-start | bytes 1228808 | tf_op jit(solution)/shard_map/ppermute | solution.py:236
  118.2 25.3 %collective-permute-start.30 = (bf16[320,640]{1,0:T(8,128)(2,1)}, bf16[320,640]{1,0:T(8,128)(2,1)S(1)}, u32[]{:S(2)}, u32[]{:S(2)}) collective-permute-start(bf16[320,640]{1,0:T(8,128)(2,1)} %collective-permute-done.28), channel_id=1, source_target_pairs={{0,16},{4,20},{8,24},{12,28},{16,0},{20,4},{24,8},{28,12},{1,17},{... | collective-permute-start | bytes 1228808 | tf_op jit(solution)/shard_map/ppermute | solution.py:233
  119.8 25.6 %collective-permute-start.33 = (bf16[320,640]{1,0:T(8,128)(2,1)}, bf16[320,640]{1,0:T(8,128)(2,1)S(1)}, u32[]{:S(2)}, u32[]{:S(2)}) collective-permute-start(bf16[320,640]{1,0:T(8,128)(2,1)} %collective-permute-done.32), channel_id=1, source_target_pairs={{0,8},{4,12},{8,0},{12,4},{16,24},{20,28},{24,16},{28,20},{1,9},{5... | collective-permute-start | bytes 1228808 | tf_op jit(solution)/shard_map/ppermute | solution.py:230
  121.3 21.9 %collective-permute-start.38 = (bf16[320,640]{1,0:T(8,128)(2,1)}, bf16[320,640]{1,0:T(8,128)(2,1)S(1)}, u32[]{:S(2)}, u32[]{:S(2)}) collective-permute-start(bf16[320,640]{1,0:T(8,128)(2,1)} %collective-permute-done.36), channel_id=1, source_target_pairs={{0,16},{4,20},{8,24},{12,28},{16,0},{20,4},{24,8},{28,12},{1,17},{... | collective-permute-start | bytes 1228808 | tf_op jit(solution)/shard_map/ppermute | solution.py:233
  122.3 24.0 %collective-permute-start.37 = (bf16[320,640]{1,0:T(8,128)(2,1)}, bf16[320,640]{1,0:T(8,128)(2,1)S(1)}, u32[]{:S(2)}, u32[]{:S(2)}) collective-permute-start(bf16[320,640]{1,0:T(8,128)(2,1)} %collective-permute-done.36), channel_id=1, source_target_pairs={{0,8},{4,12},{8,0},{12,4},{16,24},{20,28},{24,16},{28,20},{1,9},{5... | collective-permute-start | bytes 1228808 | tf_op jit(solution)/shard_map/ppermute | solution.py:230
  146.3 82.3 %collective-permute-start.44 = (bf16[320,640]{1,0:T(8,128)(2,1)S(1)}, bf16[320,640]{1,0:T(8,128)(2,1)S(1)}, u32[]{:S(2)}, u32[]{:S(2)}) collective-permute-start(bf16[320,640]{1,0:T(8,128)(2,1)S(1)} %copy-done.59), channel_id=1, source_target_pairs={{0,2},{1,3},{2,0},{3,1},{4,6},{5,7},{6,4},{7,5},{8,10},{9,11},{10,... | collective-permute-start | bytes 1228808 | tf_op jit(solution)/shard_map/ppermute | solution.py:236
  152.1 68.2 %collective-permute-start.10 = (bf16[320,640]{1,0:T(8,128)(2,1)S(1)}, bf16[320,640]{1,0:T(8,128)(2,1)S(1)}, u32[]{:S(2)}, u32[]{:S(2)}) collective-permute-start(bf16[320,640]{1,0:T(8,128)(2,1)S(1)} %copy-done.76), channel_id=1, source_target_pairs={{0,8},{4,12},{8,0},{12,4},{16,24},{20,28},{24,16},{28,20},{1,9},{5... | collective-permute-start | bytes 1228808 | tf_op jit(solution)/shard_map/ppermute | solution.py:230
  160.8 59.9 %collective-permute-start.15 = (bf16[320,640]{1,0:T(8,128)(2,1)S(1)}, bf16[320,640]{1,0:T(8,128)(2,1)S(1)}, u32[]{:S(2)}, u32[]{:S(2)}) collective-permute-start(bf16[320,640]{1,0:T(8,128)(2,1)S(1)} %copy-done.78), channel_id=1, source_target_pairs={{0,16},{4,20},{8,24},{12,28},{16,0},{20,4},{24,8},{28,12},{1,17},{... | collective-permute-start | bytes 1228808 | tf_op jit(solution)/shard_map/ppermute | solution.py:233
  161.1 64.4 %collective-permute-start.20 = (bf16[320,640]{1,0:T(8,128)(2,1)S(1)}, bf16[320,640]{1,0:T(8,128)(2,1)S(1)}, u32[]{:S(2)}, u32[]{:S(2)}) collective-permute-start(bf16[320,640]{1,0:T(8,128)(2,1)S(1)} %copy-done.80), channel_id=1, source_target_pairs={{0,8},{4,12},{8,0},{12,4},{16,24},{20,28},{24,16},{28,20},{1,9},{5... | collective-permute-start | bytes 1228808 | tf_op jit(solution)/shard_map/ppermute | solution.py:230
  162.9 67.4 %collective-permute-start.1 = (bf16[768,1280]{1,0:T(8,128)(2,1)S(1)}, bf16[768,1280]{1,0:T(8,128)(2,1)S(1)}, u32[]{:S(2)}, u32[]{:S(2)}) collective-permute-start(bf16[768,1280]{1,0:T(8,128)(2,1)S(1)} %fusion.7), channel_id=1, source_target_pairs={{0,4},{4,0},{8,12},{12,8},{16,20},{20,16},{24,28},{28,24},{1,5},{5... | collective-permute-start | bytes 5898248 | tf_op jit(solution)/shard_map/ppermute | solution.py:226
  220.3 54.2 %collective-permute-start.48 = (bf16[320,640]{1,0:T(8,128)(2,1)S(1)}, bf16[320,640]{1,0:T(8,128)(2,1)}, u32[]{:S(2)}, u32[]{:S(2)}) collective-permute-start(bf16[320,640]{1,0:T(8,128)(2,1)S(1)} %copy-done.59), channel_id=1, source_target_pairs={{0,1},{1,2},{2,3},{3,0},{4,5},{5,6},{6,7},{7,4},{8,9},{9,10},{10,1... | collective-permute-start | bytes 1228808 | tf_op jit(solution)/shard_map/ppermute | solution.py:236
  220.8 53.9 %collective-permute-start.52 = (bf16[320,640]{1,0:T(8,128)(2,1)S(1)}, bf16[320,640]{1,0:T(8,128)(2,1)}, u32[]{:S(2)}, u32[]{:S(2)}) collective-permute-start(bf16[320,640]{1,0:T(8,128)(2,1)S(1)} %copy-done.59), channel_id=1, source_target_pairs={{0,3},{1,0},{2,1},{3,2},{4,7},{5,4},{6,5},{7,6},{8,11},{9,8},{10,9... | collective-permute-start | bytes 1228808 | tf_op jit(solution)/shard_map/ppermute | solution.py:236
  225.5 50.5 %collective-permute-start.41 = (bf16[320,640]{1,0:T(8,128)(2,1)S(1)}, bf16[320,640]{1,0:T(8,128)(2,1)S(1)}, u32[]{:S(2)}, u32[]{:S(2)}) collective-permute-start(bf16[320,640]{1,0:T(8,128)(2,1)S(1)} %copy-done.59), channel_id=1, source_target_pairs={{0,8},{4,12},{8,0},{12,4},{16,24},{20,28},{24,16},{28,20},{1,9},{5... | collective-permute-start | bytes 1228808 | tf_op jit(solution)/shard_map/ppermute | solution.py:230
  228.7 48.8 %collective-permute-start.42 = (bf16[320,640]{1,0:T(8,128)(2,1)S(1)}, bf16[320,640]{1,0:T(8,128)(2,1)S(1)}, u32[]{:S(2)}, u32[]{:S(2)}) collective-permute-start(bf16[320,640]{1,0:T(8,128)(2,1)S(1)} %copy-done.59), channel_id=1, source_target_pairs={{0,16},{4,20},{8,24},{12,28},{16,0},{20,4},{24,8},{28,12},{1,17},{... | collective-permute-start | bytes 1228808 | tf_op jit(solution)/shard_map/ppermute | solution.py:233
  230.4 59.7 %collective-permute-start.45 = (bf16[320,640]{1,0:T(8,128)(2,1)S(1)}, bf16[320,640]{1,0:T(8,128)(2,1)}, u32[]{:S(2)}, u32[]{:S(2)}) collective-permute-start(bf16[320,640]{1,0:T(8,128)(2,1)S(1)} %collective-permute-done.44), channel_id=1, source_target_pairs={{0,8},{4,12},{8,0},{12,4},{16,24},{20,28},{24,16},{28,20},{1,9},{5... | collective-permute-start | bytes 1228808 | tf_op jit(solution)/shard_map/ppermute | solution.py:230
  274.5 28.1 %collective-permute-start.46 = (bf16[320,640]{1,0:T(8,128)(2,1)S(1)}, bf16[320,640]{1,0:T(8,128)(2,1)S(1)}, u32[]{:S(2)}, u32[]{:S(2)}) collective-permute-start(bf16[320,640]{1,0:T(8,128)(2,1)S(1)} %collective-permute-done.44), channel_id=1, source_target_pairs={{0,16},{4,20},{8,24},{12,28},{16,0},{20,4},{24,8},{28,12},{1,17},{... | collective-permute-start | bytes 1228808 | tf_op jit(solution)/shard_map/ppermute | solution.py:233
  276.1 27.9 %collective-permute-start.49 = (bf16[320,640]{1,0:T(8,128)(2,1)}, bf16[320,640]{1,0:T(8,128)(2,1)S(1)}, u32[]{:S(2)}, u32[]{:S(2)}) collective-permute-start(bf16[320,640]{1,0:T(8,128)(2,1)} %collective-permute-done.48), channel_id=1, source_target_pairs={{0,8},{4,12},{8,0},{12,4},{16,24},{20,28},{24,16},{28,20},{1,9},{5... | collective-permute-start | bytes 1228808 | tf_op jit(solution)/shard_map/ppermute | solution.py:230
  277.5 24.9 %collective-permute-start.54 = (bf16[320,640]{1,0:T(8,128)(2,1)}, bf16[320,640]{1,0:T(8,128)(2,1)}, u32[]{:S(2)}, u32[]{:S(2)}) collective-permute-start(bf16[320,640]{1,0:T(8,128)(2,1)} %collective-permute-done.52), channel_id=1, source_target_pairs={{0,16},{4,20},{8,24},{12,28},{16,0},{20,4},{24,8},{28,12},{1,17},{... | collective-permute-start | bytes 1228808 | tf_op jit(solution)/shard_map/ppermute | solution.py:233
  307.3 77.3 %collective-permute-start.58 = (bf16[768,1280]{1,0:T(8,128)(2,1)}, bf16[768,1280]{1,0:T(8,128)(2,1)}, u32[]{:S(2)}, u32[]{:S(2)}) collective-permute-start(bf16[768,1280]{1,0:T(8,128)(2,1)} %param.20), channel_id=1, source_target_pairs={{1,4},{3,6},{4,1},{6,3},{9,12},{11,14},{12,9},{14,11},{17,20},{19,... | collective-permute-start | bytes 5898248 | tf_op jit(solution)/shard_map/ppermute | solution.py:244
  311.0 81.7 %collective-permute-start.22 = (bf16[768,1280]{1,0:T(8,128)(2,1)}, bf16[768,1280]{1,0:T(8,128)(2,1)}, u32[]{:S(2)}, u32[]{:S(2)}) collective-permute-start(bf16[768,1280]{1,0:T(8,128)(2,1)} %convolution_convert_fusion), channel_id=1, source_target_pairs={{0,4},{4,0},{8,12},{12,8},{16,20},{20,16},{24,28},{28,24},{1,5},{5... | collective-permute-start | bytes 5898248 | tf_op jit(solution)/shard_map/ppermute | solution.py:226
  407.8 30.0 %collective-permute-start.59 = (bf16[768,1280]{1,0:T(8,128)(2,1)}, bf16[768,1280]{1,0:T(8,128)(2,1)}, u32[]{:S(2)}, u32[]{:S(2)}) collective-permute-start(bf16[768,1280]{1,0:T(8,128)(2,1)} %get-tuple-element.62), channel_id=1, source_target_pairs={{0,4},{4,0},{8,12},{12,8},{16,20},{20,16},{24,28},{28,24},{1,5},{5... | collective-permute-start | bytes 5898248 | tf_op jit(solution)/shard_map/ppermute | solution.py:226
  443.1 93.7 %collective-permute-start.107 = (bf16[320,1280]{1,0:T(8,128)(2,1)}, bf16[320,1280]{1,0:T(8,128)(2,1)}, u32[]{:S(2)}, u32[]{:S(2)}) collective-permute-start(bf16[320,1280]{1,0:T(8,128)(2,1)} %convolution_convert_fusion.5), channel_id=1, source_target_pairs={{0,8},{4,12},{8,0},{12,4},{16,24},{20,28},{24,16},{28,20},{1,9},{5... | collective-permute-start | bytes 2457608 | tf_op jit(solution)/shard_map/ppermute | solution.py:230
  448.2 55.9 %collective-permute-start.108 = (bf16[320,1280]{1,0:T(8,128)(2,1)}, bf16[320,1280]{1,0:T(8,128)(2,1)}, u32[]{:S(2)}, u32[]{:S(2)}) collective-permute-start(bf16[320,1280]{1,0:T(8,128)(2,1)} %convolution_convert_fusion.4), channel_id=1, source_target_pairs={{0,8},{4,12},{8,0},{12,4},{16,24},{20,28},{24,16},{28,20},{1,9},{5... | collective-permute-start | bytes 2457608 | tf_op jit(solution)/shard_map/ppermute | solution.py:230
  452.2 122.2 %collective-permute-start.110 = (bf16[320,1280]{1,0:T(8,128)(2,1)}, bf16[320,1280]{1,0:T(8,128)(2,1)S(1)}, u32[]{:S(2)}, u32[]{:S(2)}) collective-permute-start(bf16[320,1280]{1,0:T(8,128)(2,1)} %convolution_convert_fusion.3), channel_id=1, source_target_pairs={{0,16},{4,20},{8,24},{12,28},{16,0},{20,4},{24,8},{28,12},{1,17},{... | collective-permute-start | bytes 2457608 | tf_op jit(solution)/shard_map/ppermute | solution.py:233
  457.2 51.2 %collective-permute-start.111 = (bf16[320,1280]{1,0:T(8,128)(2,1)}, bf16[320,1280]{1,0:T(8,128)(2,1)}, u32[]{:S(2)}, u32[]{:S(2)}) collective-permute-start(bf16[320,1280]{1,0:T(8,128)(2,1)} %convolution_convert_fusion.2), channel_id=1, source_target_pairs={{0,16},{4,20},{8,24},{12,28},{16,0},{20,4},{24,8},{28,12},{1,17},{... | collective-permute-start | bytes 2457608 | tf_op jit(solution)/shard_map/ppermute | solution.py:233
  492.4 59.0 %collective-permute-start.97 = (bf16[320,1280]{1,0:T(8,128)(2,1)}, bf16[320,1280]{1,0:T(8,128)(2,1)}, u32[]{:S(2)}, u32[]{:S(2)}) collective-permute-start(bf16[320,1280]{1,0:T(8,128)(2,1)} %convolution_convert_fusion.9), channel_id=1, source_target_pairs={{0,8},{4,12},{8,0},{12,4},{16,24},{20,28},{24,16},{28,20},{1,9},{5... | collective-permute-start | bytes 2457608 | tf_op jit(solution)/shard_map/ppermute | solution.py:230
  504.1 24.7 %collective-permute-start.98 = (bf16[320,1280]{1,0:T(8,128)(2,1)S(1)}, bf16[320,1280]{1,0:T(8,128)(2,1)S(1)}, u32[]{:S(2)}, u32[]{:S(2)}) collective-permute-start(bf16[320,1280]{1,0:T(8,128)(2,1)S(1)} %convolution_convert_fusion.8), channel_id=1, source_target_pairs={{0,8},{4,12},{8,0},{12,4},{16,24},{20,28},{24,16},{28,20},{1,9},{5... | collective-permute-start | bytes 2457608 | tf_op jit(solution)/shard_map/ppermute | solution.py:230
  508.5 24.4 %collective-permute-start.101 = (bf16[320,1280]{1,0:T(8,128)(2,1)S(1)}, bf16[320,1280]{1,0:T(8,128)(2,1)S(1)}, u32[]{:S(2)}, u32[]{:S(2)}) collective-permute-start(bf16[320,1280]{1,0:T(8,128)(2,1)S(1)} %convolution_convert_fusion.6), channel_id=1, source_target_pairs={{0,16},{4,20},{8,24},{12,28},{16,0},{20,4},{24,8},{28,12},{1,17},{... | collective-permute-start | bytes 2457608 | tf_op jit(solution)/shard_map/ppermute | solution.py:233
  532.9 31.1 %collective-permute-start.99 = (bf16[320,1280]{1,0:T(8,128)(2,1)S(1)}, bf16[320,1280]{1,0:T(8,128)(2,1)S(1)}, u32[]{:S(2)}, u32[]{:S(2)}) collective-permute-start(bf16[320,1280]{1,0:T(8,128)(2,1)S(1)} %fusion.44), channel_id=1, source_target_pairs={{0,16},{4,20},{8,24},{12,28},{16,0},{20,4},{24,8},{28,12},{1,17},{... | collective-permute-start | bytes 2457608 | tf_op jit(solution)/shard_map/ppermute | solution.py:233
  536.8 44.7 %collective-permute-start.100 = (bf16[320,1280]{1,0:T(8,128)(2,1)S(1)}, bf16[320,1280]{1,0:T(8,128)(2,1)S(1)}, u32[]{:S(2)}, u32[]{:S(2)}) collective-permute-start(bf16[320,1280]{1,0:T(8,128)(2,1)S(1)} %copy-done.119), channel_id=1, source_target_pairs={{0,16},{4,20},{8,24},{12,28},{16,0},{20,4},{24,8},{28,12},{1,17},{... | collective-permute-start | bytes 2457608 | tf_op jit(solution)/shard_map/ppermute | solution.py:233
  546.4 29.4 %collective-permute-start.112 = (bf16[320,1280]{1,0:T(8,128)(2,1)S(1)}, bf16[320,1280]{1,0:T(8,128)(2,1)S(1)}, u32[]{:S(2)}, u32[]{:S(2)}) collective-permute-start(bf16[320,1280]{1,0:T(8,128)(2,1)S(1)} %fusion.47), channel_id=1, source_target_pairs={{0,8},{4,12},{8,0},{12,4},{16,24},{20,28},{24,16},{28,20},{1,9},{5... | collective-permute-start | bytes 2457608 | tf_op jit(solution)/shard_map/ppermute | solution.py:230
  551.4 48.1 %collective-permute-start.60 = (bf16[768,1280]{1,0:T(8,128)(2,1)S(1)}, bf16[768,1280]{1,0:T(8,128)(2,1)S(1)}, u32[]{:S(2)}, u32[]{:S(2)}) collective-permute-start(bf16[768,1280]{1,0:T(8,128)(2,1)S(1)} %copy-done.117), channel_id=1, source_target_pairs={{0,4},{4,0},{8,12},{12,8},{16,20},{20,16},{24,28},{28,24},{1,5},{5... | collective-permute-start | bytes 5898248 | tf_op jit(solution)/shard_map/ppermute | solution.py:226
  564.0 56.5 %collective-permute-start.56 = (bf16[768,1280]{1,0:T(8,128)(2,1)S(1)}, bf16[768,1280]{1,0:T(8,128)(2,1)}, u32[]{:S(2)}, u32[]{:S(2)}) collective-permute-start(bf16[768,1280]{1,0:T(8,128)(2,1)S(1)} %copy-done.115), channel_id=1, source_target_pairs={{0,4},{4,0},{8,12},{12,8},{16,20},{20,16},{24,28},{28,24},{1,5},{5... | collective-permute-start | bytes 5898248 | tf_op jit(solution)/shard_map/ppermute | solution.py:226
  575.8 68.8 %collective-permute-start.114 = (bf16[320,640]{1,0:T(8,128)(2,1)}, bf16[320,640]{1,0:T(8,128)(2,1)S(1)}, u32[]{:S(2)}, u32[]{:S(2)}) collective-permute-start(bf16[320,640]{1,0:T(8,128)(2,1)} %slice.995), channel_id=1, source_target_pairs={{0,2},{1,3},{2,0},{3,1},{4,6},{5,7},{6,4},{7,5},{8,10},{9,11},{10,... | collective-permute-start | bytes 1228808 | tf_op jit(solution)/shard_map/ppermute | solution.py:236
  581.6 63.8 %collective-permute-start.113 = (bf16[320,640]{1,0:T(8,128)(2,1)}, bf16[320,640]{1,0:T(8,128)(2,1)}, u32[]{:S(2)}, u32[]{:S(2)}) collective-permute-start(bf16[320,640]{1,0:T(8,128)(2,1)} %get-tuple-element.97), channel_id=1, source_target_pairs={{0,3},{1,0},{2,1},{3,2},{4,7},{5,4},{6,5},{7,6},{8,11},{9,8},{10,9... | collective-permute-start | bytes 1228808 | tf_op jit(solution)/shard_map/ppermute | solution.py:236
  594.3 51.4 %collective-permute-start.115 = (bf16[320,640]{1,0:T(8,128)(2,1)}, bf16[320,640]{1,0:T(8,128)(2,1)}, u32[]{:S(2)}, u32[]{:S(2)}) collective-permute-start(bf16[320,640]{1,0:T(8,128)(2,1)} %get-tuple-element.98), channel_id=1, source_target_pairs={{0,1},{1,2},{2,3},{3,0},{4,5},{5,6},{6,7},{7,4},{8,9},{9,10},{10,1... | collective-permute-start | bytes 1228808 | tf_op jit(solution)/shard_map/ppermute | solution.py:236
  599.5 51.4 %collective-permute-start.104 = (bf16[320,640]{1,0:T(8,128)(2,1)}, bf16[320,640]{1,0:T(8,128)(2,1)}, u32[]{:S(2)}, u32[]{:S(2)}) collective-permute-start(bf16[320,640]{1,0:T(8,128)(2,1)} %slice.980), channel_id=1, source_target_pairs={{0,2},{1,3},{2,0},{3,1},{4,6},{5,7},{6,4},{7,5},{8,10},{9,11},{10,... | collective-permute-start | bytes 1228808 | tf_op jit(solution)/shard_map/ppermute | solution.py:236
  620.5 21.0 %collective-permute-start.92 = (f32[10240]{0:T(1024)}, f32[10240]{0:T(1024)}, u32[]{:S(2)}, u32[]{:S(2)}) collective-permute-start(f32[10240]{0:T(1024)} %fusion.115), channel_id=1, source_target_pairs={{0,4},{4,0},{8,12},{12,8},{16,20},{20,16},{24,28},{28,24},{1,5},{5... | collective-permute-start | bytes 122888 | tf_op jit(solution)/shard_map/ppermute | solution.py:309
  645.4 28.8 %collective-permute-start.61 = (bf16[768,1280]{1,0:T(8,128)(2,1)S(1)}, bf16[768,1280]{1,0:T(8,128)(2,1)S(1)}, u32[]{:S(2)}, u32[]{:S(2)}) collective-permute-start(bf16[768,1280]{1,0:T(8,128)(2,1)S(1)} %convert_element_type.337), channel_id=1, source_target_pairs={{0,4},{4,0},{8,12},{12,8},{16,20},{20,16},{24,28},{28,24},{1,5},{5... | collective-permute-start | bytes 5898248 | tf_op jit(solution)/shard_map/ppermute | solution.py:226
  650.2 21.9 %collective-permute-start.116 = (f32[160,640]{1,0:T(8,128)S(1)}, f32[160,640]{1,0:T(8,128)S(1)}, u32[]{:S(2)}, u32[]{:S(2)}) collective-permute-start(f32[160,640]{1,0:T(8,128)S(1)} %get-tuple-element.96), channel_id=1, source_target_pairs={{0,4},{4,0},{8,12},{12,8},{16,20},{20,16},{24,28},{28,24},{1,5},{5... | collective-permute-start | bytes 1228808 | tf_op jit(solution)/shard_map/ppermute | solution.py:226
  819.5 77.8 %collective-permute-start.85 = (bf16[320,640]{1,0:T(8,128)(2,1)}, bf16[320,640]{1,0:T(8,128)(2,1)}, u32[]{:S(2)}, u32[]{:S(2)}) collective-permute-start(bf16[320,640]{1,0:T(8,128)(2,1)} %convolution_convert_fusion.15), channel_id=1, source_target_pairs={{0,8},{4,12},{8,0},{12,4},{16,24},{20,28},{24,16},{28,20},{1,9},{5... | collective-permute-start | bytes 1228808 | tf_op jit(solution)/shard_map/ppermute | solution.py:230
  824.3 41.5 %collective-permute-start.86 = (bf16[320,640]{1,0:T(8,128)(2,1)}, bf16[320,640]{1,0:T(8,128)(2,1)}, u32[]{:S(2)}, u32[]{:S(2)}) collective-permute-start(bf16[320,640]{1,0:T(8,128)(2,1)} %convolution_convert_fusion.14), channel_id=1, source_target_pairs={{0,8},{4,12},{8,0},{12,4},{16,24},{20,28},{24,16},{28,20},{1,9},{5... | collective-permute-start | bytes 1228808 | tf_op jit(solution)/shard_map/ppermute | solution.py:230
  824.3 20.9 %collective-permute-start.70 = (bf16[320,480]{1,0:T(8,128)(2,1)}, bf16[320,480]{1,0:T(8,128)(2,1)}, u32[]{:S(2)}, u32[]{:S(2)}) collective-permute-start(bf16[320,480]{1,0:T(8,128)(2,1)} %convolution_convert_fusion.22), channel_id=1, source_target_pairs={{0,8},{4,12},{8,0},{12,4},{16,24},{20,28},{24,16},{28,20},{1,9},{5... | collective-permute-start | bytes 921608 | tf_op jit(solution)/shard_map/ppermute | solution.py:230
  825.8 43.3 %collective-permute-start.72 = (bf16[320,480]{1,0:T(8,128)(2,1)}, bf16[320,480]{1,0:T(8,128)(2,1)}, u32[]{:S(2)}, u32[]{:S(2)}) collective-permute-start(bf16[320,480]{1,0:T(8,128)(2,1)} %convolution_convert_fusion.21), channel_id=1, source_target_pairs={{0,16},{4,20},{8,24},{12,28},{16,0},{20,4},{24,8},{28,12},{1,17},{... | collective-permute-start | bytes 921608 | tf_op jit(solution)/shard_map/ppermute | solution.py:233
  826.7 21.5 %collective-permute-start.73 = (bf16[320,480]{1,0:T(8,128)(2,1)}, bf16[320,480]{1,0:T(8,128)(2,1)}, u32[]{:S(2)}, u32[]{:S(2)}) collective-permute-start(bf16[320,480]{1,0:T(8,128)(2,1)} %convolution_convert_fusion.20), channel_id=1, source_target_pairs={{0,16},{4,20},{8,24},{12,28},{16,0},{20,4},{24,8},{28,12},{1,17},{... | collective-permute-start | bytes 921608 | tf_op jit(solution)/shard_map/ppermute | solution.py:233
  845.2 35.4 %collective-permute-start.76 = (bf16[320,480]{1,0:T(8,128)(2,1)S(1)}, bf16[320,480]{1,0:T(8,128)(2,1)S(1)}, u32[]{:S(2)}, u32[]{:S(2)}) collective-permute-start(bf16[320,480]{1,0:T(8,128)(2,1)S(1)} %copy-done.71), channel_id=1, source_target_pairs={{0,8},{4,12},{8,0},{12,4},{16,24},{20,28},{24,16},{28,20},{1,9},{5... | collective-permute-start | bytes 921608 | tf_op jit(solution)/shard_map/ppermute | solution.py:230
  864.2 21.3 %collective-permute-start.80 = (bf16[320,480]{1,0:T(8,128)(2,1)S(1)}, bf16[320,480]{1,0:T(8,128)(2,1)S(1)}, u32[]{:S(2)}, u32[]{:S(2)}) collective-permute-start(bf16[320,480]{1,0:T(8,128)(2,1)S(1)} %copy-done.72), channel_id=1, source_target_pairs={{0,16},{4,20},{8,24},{12,28},{16,0},{20,4},{24,8},{28,12},{1,17},{... | collective-permute-start | bytes 921608 | tf_op jit(solution)/shard_map/ppermute | solution.py:233
  869.1 84.8 %collective-permute-start.62 = (bf16[768,1280]{1,0:T(8,128)(2,1)S(1)}, bf16[768,1280]{1,0:T(8,128)(2,1)}, u32[]{:S(2)}, u32[]{:S(2)}) collective-permute-start(bf16[768,1280]{1,0:T(8,128)(2,1)S(1)} %copy-done.116), channel_id=1, source_target_pairs={{0,4},{4,0},{8,12},{12,8},{16,20},{20,16},{24,28},{28,24},{1,5},{5... | collective-permute-start | bytes 5898248 | tf_op jit(solution)/shard_map/ppermute | solution.py:226
  897.3 25.5 %collective-permute-start.79 = (bf16[320,480]{1,0:T(8,128)(2,1)S(1)}, bf16[320,480]{1,0:T(8,128)(2,1)S(1)}, u32[]{:S(2)}, u32[]{:S(2)}) collective-permute-start(bf16[320,480]{1,0:T(8,128)(2,1)S(1)} %fusion.77), channel_id=1, source_target_pairs={{0,2},{1,3},{2,0},{3,1},{4,6},{5,7},{6,4},{7,5},{8,10},{9,11},{10,... | collective-permute-start | bytes 921608 | tf_op jit(solution)/shard_map/ppermute | solution.py:236
  897.3 25.5 %collective-permute-start.83 = (bf16[320,480]{1,0:T(8,128)(2,1)S(1)}, bf16[320,480]{1,0:T(8,128)(2,1)S(1)}, u32[]{:S(2)}, u32[]{:S(2)}) collective-permute-start(bf16[320,480]{1,0:T(8,128)(2,1)S(1)} %fusion.76), channel_id=1, source_target_pairs={{0,1},{1,2},{2,3},{3,0},{4,5},{5,6},{6,7},{7,4},{8,9},{9,10},{10,1... | collective-permute-start | bytes 921608 | tf_op jit(solution)/shard_map/ppermute | solution.py:236
  899.8 76.1 %collective-permute-start.57 = (bf16[768,1280]{1,0:T(8,128)(2,1)}, bf16[768,1280]{1,0:T(8,128)(2,1)}, u32[]{:S(2)}, u32[]{:S(2)}) collective-permute-start(bf16[768,1280]{1,0:T(8,128)(2,1)} %maximum_select_fusion.1), channel_id=1, source_target_pairs={{1,4},{3,6},{4,1},{6,3},{9,12},{11,14},{12,9},{14,11},{17,20},{19,... | collective-permute-start | bytes 5898248 | tf_op jit(solution)/shard_map/ppermute | solution.py:244
  910.6 36.4 %collective-permute-start.88 = (bf16[320,160]{1,0:T(8,128)(2,1)S(1)}, bf16[320,160]{1,0:T(8,128)(2,1)S(1)}, u32[]{:S(2)}, u32[]{:S(2)}) collective-permute-start(bf16[320,160]{1,0:T(8,128)(2,1)S(1)} %get-tuple-element.112), channel_id=1, source_target_pairs={{0,3},{1,0},{2,1},{3,2},{4,7},{5,4},{6,5},{7,6},{8,11},{9,8},{10,9... | collective-permute-start | bytes 307208 | tf_op jit(solution)/shard_map/ppermute | solution.py:236
  922.8 30.3 %collective-permute-start.89 = (bf16[320,160]{1,0:T(8,128)(2,1)S(1)}, bf16[320,160]{1,0:T(8,128)(2,1)S(1)}, u32[]{:S(2)}, u32[]{:S(2)}) collective-permute-start(bf16[320,160]{1,0:T(8,128)(2,1)S(1)} %get-tuple-element.114), channel_id=1, source_target_pairs={{0,2},{1,3},{2,0},{3,1},{4,6},{5,7},{6,4},{7,5},{8,10},{9,11},{10,... | collective-permute-start | bytes 307208 | tf_op jit(solution)/shard_map/ppermute | solution.py:236
  922.8 30.3 %collective-permute-start.90 = (bf16[320,160]{1,0:T(8,128)(2,1)S(1)}, bf16[320,160]{1,0:T(8,128)(2,1)S(1)}, u32[]{:S(2)}, u32[]{:S(2)}) collective-permute-start(bf16[320,160]{1,0:T(8,128)(2,1)S(1)} %get-tuple-element.113), channel_id=1, source_target_pairs={{0,1},{1,2},{2,3},{3,0},{4,5},{5,6},{6,7},{7,4},{8,9},{9,10},{10,1... | collective-permute-start | bytes 307208 | tf_op jit(solution)/shard_map/ppermute | solution.py:236
  947.0 36.5 %collective-permute-start.84 = (f32[160,480]{1,0:T(8,128)}, f32[160,480]{1,0:T(8,128)}, u32[]{:S(2)}, u32[]{:S(2)}) collective-permute-start(f32[160,480]{1,0:T(8,128)} %get-tuple-element.111), channel_id=1, source_target_pairs={{0,4},{4,0},{8,12},{12,8},{16,20},{20,16},{24,28},{28,24},{1,5},{5... | collective-permute-start | bytes 921608 | tf_op jit(solution)/shard_map/ppermute | solution.py:226
  969.6 29.7 %collective-permute-start.63 = (bf16[768,1280]{1,0:T(8,128)(2,1)S(1)}, bf16[768,1280]{1,0:T(8,128)(2,1)}, u32[]{:S(2)}, u32[]{:S(2)}) collective-permute-start(bf16[768,1280]{1,0:T(8,128)(2,1)S(1)} %maximum_select_fusion.3), channel_id=1, source_target_pairs={{1,4},{3,6},{4,1},{6,3},{9,12},{11,14},{12,9},{14,11},{17,20},{19,... | collective-permute-start | bytes 5898248 | tf_op jit(solution)/shard_map/ppermute | solution.py:244
  (189 other events, 3720.3 us)

commit v2 on v1

v2 whole, which is shorter than its diff:
```python
import functools

import jax
import jax.numpy as jnp
from jax import lax
from jax.experimental import pallas as pl
from jax.experimental.pallas import tpu as pltpu
from jax.sharding import PartitionSpec as P

HDIM = 80
EPS = 1e-05
LOG2E = 1.4426950408889634
F32 = jnp.float32
BF16 = jnp.bfloat16


def norm_rows(values, norm_gain, norm_shift):
    center = values - jnp.mean(values, -1, keepdims=True)
    spread = jnp.mean(center * center, -1, keepdims=True)
    return center * lax.rsqrt(spread + EPS) * norm_gain + norm_shift


def norm_back(values, norm_gain, grad):
    center = values - jnp.mean(values, -1, keepdims=True)
    scale = lax.rsqrt(jnp.mean(center * center, -1, keepdims=True) + EPS)
    normed = center * scale
    scaled = grad * norm_gain
    back = scaled - jnp.mean(scaled, -1, keepdims=True)
    back = (back - normed * jnp.mean(scaled * normed, -1, keepdims=True)) * scale
    return back, jnp.sum(grad * normed, 0), jnp.sum(grad, 0)


def dot_nn(left, right):
    return jnp.dot(left, right, preferred_element_type=F32)


def dot_tn(left, right):
    return lax.dot_general(left, right, (((0,), (0,)), ((), ())), preferred_element_type=F32)


def dot_nt(left, right):
    return lax.dot_general(left, right, (((1,), (1,)), ((), ())), preferred_element_type=F32)


def up_kernel(rows_ref, weight_ref, bias_ref, hidden_ref, slope_ref):
    pre = dot_nn(rows_ref[...], weight_ref[...]) + bias_ref[...]
    cdf = 0.5 * lax.erf(pre * (0.5**0.5)) + 0.5
    density = jnp.exp(-0.5 * pre * pre) * 0.3989422804014327
    hidden_ref[...] = (pre * cdf).astype(BF16)
    slope_ref[...] = (cdf + pre * density).astype(BF16)


def up_gelu(rows, weight, bias):
    count, depth = rows.shape
    cols = weight.shape[1]
    block_rows, block_cols = min(512, count), min(640, cols)
    return pl.pallas_call(
        up_kernel,
        grid=(cols // block_cols, count // block_rows),
        in_specs=[
            pl.BlockSpec((block_rows, depth), lambda n, m: (m, 0)),
            pl.BlockSpec((depth, block_cols), lambda n, m: (0, n)),
            pl.BlockSpec((1, block_cols), lambda n, m: (0, n)),
        ],
        out_specs=[
            pl.BlockSpec((block_rows, block_cols), lambda n, m: (m, n)),
            pl.BlockSpec((block_rows, block_cols), lambda n, m: (m, n)),
        ],
        out_shape=[jax.ShapeDtypeStruct((count, cols), BF16)] * 2,
        cost_estimate=pl.CostEstimate(
            flops=2 * count * depth * cols, bytes_accessed=20_000_000, transcendentals=0
        ),
        compiler_params=pltpu.CompilerParams(vmem_limit_bytes=40 << 20),
        name="up_gelu",
    )(rows, weight, bias)


def attend_kernel(heads, scaling, query_ref, all_ref, mask_ref, out_ref, total_ref):
    width = heads * HDIM
    queries = query_ref[...]
    mask = mask_ref[...]
    outs, totals = [], []
    for head in range(heads):
        low = head * HDIM
        query = queries[:, low : low + HDIM]
        key = all_ref[:, width + low : width + low + HDIM]
        value = all_ref[:, 2 * width + low : 2 * width + low + HDIM]
        scores = dot_nt(query, key) * (scaling * LOG2E) + mask
        row_max = jnp.max(scores, -1, keepdims=True)
        exp_scores = jnp.exp2(scores - row_max)
        total = jnp.sum(exp_scores, -1, keepdims=True)
        mixed = dot_nn(exp_scores.astype(BF16), value)
        outs.append(mixed * (1.0 / total))
        totals.append(row_max + jnp.log2(total))
    out_ref[...] = jnp.concatenate(outs, -1).astype(BF16)
    for head in range(heads):
        wide = jnp.broadcast_to(totals[head], (totals[head].shape[0], 128))
        total_ref[head : head + 1, :] = wide.T[0:1, :]


def attend(joined, mask_row, heads, scaling):
    count, cols = joined.shape
    block_rows = min(256, count)
    width = heads * HDIM
    return pl.pallas_call(
        functools.partial(attend_kernel, heads, scaling),
        grid=(count // block_rows,),
        in_specs=[
            pl.BlockSpec((block_rows, cols), lambda m: (m, 0)),
            pl.BlockSpec((count, cols), lambda m: (0, 0)),
            pl.BlockSpec((1, count), lambda m: (0, 0)),
        ],
        out_specs=[
            pl.BlockSpec((block_rows, width), lambda m: (m, 0)),
            pl.BlockSpec((heads, block_rows), lambda m: (0, m)),
        ],
        out_shape=[
            jax.ShapeDtypeStruct((count, width), BF16),
            jax.ShapeDtypeStruct((heads, count), F32),
        ],
        cost_estimate=pl.CostEstimate(
            flops=2 * heads * count * count * 512,
            bytes_accessed=4_000_000,
            transcendentals=heads * count * count,
        ),
        compiler_params=pltpu.CompilerParams(vmem_limit_bytes=48 << 20),
        name="attend",
    )(joined, joined, mask_row)


def attend_back_kernel(
    heads, scaling, query_ref, all_ref, grad_ref, total_ref, mask_ref,
    out_ref, sums_ref, key_sum, value_sum,
):
    step = pl.program_id(0)
    steps = pl.num_programs(0)
    width = heads * HDIM
    block_rows = query_ref.shape[0]

    @pl.when(step == 0)
    def _():
        key_sum[...] = jnp.zeros_like(key_sum)
        value_sum[...] = jnp.zeros_like(value_sum)
        sums_ref[...] = jnp.zeros_like(sums_ref)

    queries = query_ref[...]
    grads = grad_ref[...]
    query_outs = []
    for head in range(heads):
        low = head * HDIM
        query = queries[:, low : low + HDIM]
        grad = grads[:, low : low + HDIM]
        key = all_ref[:, width + low : width + low + HDIM]
        value = all_ref[:, 2 * width + low : 2 * width + low + HDIM]
        scores = dot_nt(key, query) * (scaling * LOG2E) + mask_ref[...]
        probs = jnp.exp2(scores - total_ref[head : head + 1, :])
        grad_probs = dot_nt(value, grad)
        shared = jnp.sum(probs * grad_probs, 0, keepdims=True)
        grad_scores = (probs * (grad_probs - shared)).astype(BF16)
        value_sum[head, :, :HDIM] += dot_nn(probs.astype(BF16), grad)
        key_sum[head, :, :HDIM] += dot_nn(grad_scores, query)
        query_outs.append(dot_tn(grad_scores, key) * scaling)
    joined = jnp.concatenate(query_outs, -1)
    sums_ref[0:1, :width] += jnp.sum(joined, 0, keepdims=True)
    rows = pl.ds(pl.multiple_of(step * block_rows, block_rows), block_rows)
    out_ref[rows, :width] = joined.astype(BF16)

    @pl.when(step == steps - 1)
    def _():
        keys = jnp.concatenate([key_sum[head, :, :HDIM] for head in range(heads)], -1)
        values = jnp.concatenate([value_sum[head, :, :HDIM] for head in range(heads)], -1)
        sums_ref[1:2, :width] = jnp.sum(values, 0, keepdims=True)
        out_ref[:, width:] = jnp.concatenate([keys * scaling, values], -1).astype(BF16)


def attend_back(joined, grad_heads, totals, mask_col, heads, scaling):
    count, cols = joined.shape
    block_rows = min(256, count)
    width = heads * HDIM
    return pl.pallas_call(
        functools.partial(attend_back_kernel, heads, scaling),
        grid=(count // block_rows,),
        in_specs=[
            pl.BlockSpec((block_rows, cols), lambda m: (m, 0)),
            pl.BlockSpec((count, cols), lambda m: (0, 0)),
            pl.BlockSpec((block_rows, width), lambda m: (m, 0)),
            pl.BlockSpec((heads, block_rows), lambda m: (0, m)),
            pl.BlockSpec((count, 1), lambda m: (0, 0)),
        ],
        out_specs=[
            pl.BlockSpec((count, cols), lambda m: (0, 0)),
            pl.BlockSpec((8, 256), lambda m: (0, 0)),
        ],
        out_shape=[
            jax.ShapeDtypeStruct((count, cols), BF16),
            jax.ShapeDtypeStruct((8, 256), F32),
        ],
        scratch_shapes=[
            pltpu.VMEM((heads, count, 128), F32),
            pltpu.VMEM((heads, count, 128), F32),
        ],
        cost_estimate=pl.CostEstimate(
            flops=2 * heads * count * count * 1280,
            bytes_accessed=5_000_000,
            transcendentals=heads * count * count,
        ),
        compiler_params=pltpu.CompilerParams(vmem_limit_bytes=56 << 20),
        name="attend_back",
    )(joined, joined, grad_heads, totals, mask_col)


UNIT = 320
SPAN = 640
TURNS = 4


def clamp_rows(ref, start, size):
    return ref.at[pl.ds(pl.multiple_of(start, 16), size)]


def forward_kernel(
    scaling,
    attn_shard, up_shard, down_shard, tokens, cotangent, mask_in, bias_in,
    gain_one, shift_one, gain_two, shift_two, bias_out,
    w_attn_out, w_up_out, w_down, tokens_out, cot_out, mask_out, first_out, second_out, joined_out,
    heads_out, totals_out, middle_out, hidden_out, slope_out,
    w_attn, w_up, tok, first, second, joined, heads, middle, send_rows, got_rows, hidden, slope,
    mask, totals, bias, send_sem, recv_sem, local_sem,
):
    dp, z = lax.axis_index("dp"), lax.axis_index("tensor")
    core, plane = lax.rem(dp, 2), lax.div(dp, 2)
    x_bit, y_bit = lax.rem(plane, 2), lax.div(plane, 2)
    half = tok.shape[0]
    count = 2 * half
    to_x = (y_bit * 4 + (1 - x_bit) * 2 + core, z)
    to_y = ((1 - y_bit) * 4 + x_bit * 2 + core, z)
    to_core = (plane * 2 + 1 - core, z)
    to_clip = (plane * 2 + 1 - core, z + 1 - 2 * lax.rem(z, 2))
    to_z = [(dp, lax.rem(z + k, TURNS)) for k in range(TURNS)]
    moves = core != lax.rem(z, 2)
    plane_x = y_bit * 2 + 1 - x_bit
    plane_y = (1 - y_bit) * 2 + x_bit
    plane_xy = (1 - y_bit) * 2 + 1 - x_bit
    turn = [lax.rem(z + TURNS - k, TURNS) for k in range(TURNS)]

    barrier = pltpu.get_barrier_semaphore()
    partners = [to_x, to_y, to_core, to_clip] + to_z[1:]
    for partner in partners:
        pl.semaphore_signal(barrier, inc=1, device_id=partner, device_id_type=pl.DeviceIdType.MESH)
    pl.semaphore_wait(barrier, len(partners))

    def remote(source, target, sem, device):
        return pltpu.make_async_remote_copy(
            src_ref=source,
            dst_ref=target,
            send_sem=send_sem.at[sem],
            recv_sem=recv_sem.at[sem],
            device_id=device,
            device_id_type=pl.DeviceIdType.MESH,
        )

    sent = []

    def send(source, target, sem, device):
        copy = remote(source, target, sem, device)
        copy.start()
        sent.append(copy)

    def arrived(target, sem):
        remote(target, target, sem, to_core).wait_recv()

    weights = [w_attn, w_up, w_down]
    shards = [attn_shard, up_shard, down_shard]

    def block(array, k, place):
        return weights[array].at[
            pl.ds(pl.multiple_of(place * UNIT, 16), UNIT),
            pl.ds(pl.multiple_of(turn[k] * SPAN, 128), SPAN),
        ]

    def own_half(array, which):
        rows = UNIT // 2
        return weights[array].at[
            pl.ds(pl.multiple_of(plane * UNIT + which * rows, 16), rows),
            pl.ds(pl.multiple_of(z * SPAN, 128), SPAN),
        ]

    def pair_start(array):
        send(shards[array].at[1 - core], own_half(array, core), 48 + array, to_core)
        copy = pltpu.make_async_copy(
            shards[array].at[core], own_half(array, core), local_sem.at[array]
        )
        copy.start()
        return copy

    def pair_wait(array, copy):
        copy.wait()
        arrived(own_half(array, 1 - core), 48 + array)

    def go_plane(array, k):
        send(block(array, k, plane), block(array, k, plane), 16 * array + 4 + k, to_x)
        send(block(array, k, plane), block(array, k, plane), 16 * array + 8 + k, to_y)

    def go_line(array):
        for k in range(1, TURNS):
            send(block(array, 0, plane), block(array, 0, plane), 16 * array + k, to_z[k])

    def from_line(array, k):
        arrived(block(array, k, plane), 16 * array + k)
        go_plane(array, k)

    def forward_on(array, k):
        if k % 2 == 0:
            arrived(block(array, k, plane_x), 16 * array + 4 + k)
            send(block(array, k, plane_x), block(array, k, plane_x), 16 * array + 12 + k, to_y)
        else:
            arrived(block(array, k, plane_y), 16 * array + 8 + k)
            send(block(array, k, plane_y), block(array, k, plane_y), 16 * array + 12 + k, to_x)

    def complete(array, k):
        if k % 2 == 0:
            arrived(block(array, k, plane_y), 16 * array + 8 + k)
        else:
            arrived(block(array, k, plane_x), 16 * array + 4 + k)
        arrived(block(array, k, plane_xy), 16 * array + 12 + k)

    pairs = [pair_start(0)]
    tok_copy = pltpu.make_async_copy(tokens, tok, local_sem.at[3])
    mask_copy = pltpu.make_async_copy(mask_in, mask, local_sem.at[4])
    clip_tok = remote(tokens, tok, 51, to_clip)
    clip_mask = remote(mask_in, mask, 52, to_clip)
    cot_copy = pltpu.make_async_copy(cotangent, cot_out, local_sem.at[5])
    clip_cot = remote(cotangent, cot_out, 59, to_clip)

    @pl.when(moves)
    def _():
        clip_mask.start()
        clip_tok.start()

    @pl.when(jnp.logical_not(moves))
    def _():
        tok_copy.start()
        mask_copy.start()

    bias_copy = pltpu.make_async_copy(bias_in, bias.at[z], local_sem.at[6])
    bias_copy.start()
    for k in range(1, TURNS):
        send(bias_in, bias.at[z], 52 + k, to_z[k])
    pairs += [pair_start(1), pair_start(2)]
    pair_wait(0, pairs[0])
    go_plane(0, 0)
    go_line(0)
    pair_wait(1, pairs[1])
    go_plane(1, 0)
    pair_wait(2, pairs[2])

    @pl.when(moves)
    def _():
        clip_mask.wait()
        clip_tok.wait()

    @pl.when(jnp.logical_not(moves))
    def _():
        tok_copy.wait()
        mask_copy.wait()

    outs = []

    def put(source, target, sem):
        copy = pltpu.make_async_copy(source, target, local_sem.at[sem])
        copy.start()
        outs.append(copy)
        return copy

    put(tok, tokens_out, 7)
    put(mask, mask_out, 8)
    base = pl.multiple_of(core * half, 256)
    other = pl.multiple_of((1 - core) * half, 256)

    def norm_loop(step, _):
        rows = pl.ds(pl.multiple_of(step * 256, 256), 256)
        values = tok[rows, :].astype(F32)
        normed = norm_rows(values, gain_one[...], shift_one[...])
        first[pl.ds(pl.multiple_of(base + step * 256, 256), 256), :] = normed.astype(BF16)
        return 0

    lax.fori_loop(0, half // 256, norm_loop, 0)
    own_rows, other_rows = pl.ds(base, half), pl.ds(other, half)
    send(first.at[own_rows], first.at[own_rows], 56, to_core)
    forward_on(0, 0)
    arrived(first.at[other_rows], 56)
    put(first, first_out, 9)
    bias_copy.wait()
    for k in range(1, TURNS):
        arrived(bias.at[turn[k]], 52 + k)
    forward_on(1, 0)
    for k in range(1, TURNS):
        from_line(0, k)
    go_line(1)

    def project(k):
        complete(0, k)
        columns = pl.ds(pl.multiple_of(turn[k] * SPAN, 128), 480)

        def step_rows(step, _):
            rows = pl.ds(pl.multiple_of(step * half, half), half)
            product = dot_nn(first[rows, :], w_attn[:, columns]) + bias[turn[k], 0:1, :480]
            joined[k, rows, :] = product.astype(BF16)
            return 0

        lax.fori_loop(0, 2, step_rows, 0)
        put(joined.at[k], joined_out.at[turn[k]], 10 + k)

    def attention(k, part):
        def step_rows(step, _):
            rows = pl.ds(pl.multiple_of(step * 256, 256), 256)
            queries = joined[k, rows, :]
            mixes, logs = [jnp.zeros((256, 96), F32)], []
            for head in range(2):
                low = head * HDIM
                query = queries[:, low : low + HDIM]
                key = joined[k, :, 160 + low : 160 + low + HDIM]
                value = joined[k, :, 320 + low : 320 + low + HDIM]
                scores = dot_nt(query, key) * (scaling * LOG2E) + mask[0:1, :]
                row_max = jnp.max(scores, -1, keepdims=True)
                exp_scores = jnp.exp2(scores - row_max)
                total = jnp.sum(exp_scores, -1, keepdims=True)
                mixes.append(dot_nn(exp_scores.astype(BF16), value) * (1.0 / total))
                logs.append(row_max + jnp.log2(total))
            heads[k, rows, :] = jnp.concatenate(mixes, -1).astype(BF16)
            for head in range(2):
                wide = jnp.broadcast_to(logs[head], (256, 128))
                totals[k, head : head + 1, rows] = wide.T[0:1, :]
            return 0

        lax.fori_loop(3 * part, 3 * part + 3, step_rows, 0)
        if part == 1:
            put(heads.at[k], heads_out.at[turn[k]], 14 + k)
            put(totals.at[k], totals_out.at[turn[k]], 18 + k)

    project(0)
    attention(0, 0)
    forward_on(0, 1)
    attention(0, 1)
    forward_on(0, 2)
    forward_on(0, 3)
    project(1)
    attention(1, 0)
    for k in range(1, TURNS):
        from_line(1, k)
    go_plane(2, 0)
    go_line(2)

    @pl.when(moves)
    def _():
        clip_cot.start()

    @pl.when(jnp.logical_not(moves))
    def _():
        cot_copy.start()

    attention(1, 1)
    project(2)
    attention(2, 0)
    forward_on(1, 1)
    forward_on(1, 2)
    attention(2, 1)
    forward_on(1, 3)
    project(3)
    put(w_attn, w_attn_out, 22)
    attention(3, 0)
    forward_on(2, 0)
    attention(3, 1)

    def branch(rows):
        total = None
        for k in range(TURNS):
            columns = pl.ds(pl.multiple_of(turn[k] * SPAN + 384, 128), 256)
            product = dot_nt(heads[k, rows, :], w_attn[:, columns])
            total = product if total is None else total + product
        return total

    def branch_other(step, _):
        rows = pl.ds(pl.multiple_of(other + step * 256, 256), 256)
        send_rows[pl.ds(pl.multiple_of(step * 256, 256), 256), :] = branch(rows).astype(BF16)
        return 0

    lax.fori_loop(0, half // 256, branch_other, 0)
    send(send_rows, got_rows, 57, to_core)
    for k in range(1, TURNS):
        from_line(2, k)

    def branch_own(step, _):
        rows = pl.ds(pl.multiple_of(base + step * 256, 256), 256)
        low = pl.ds(pl.multiple_of(step * 256, 256), 256)
        middle[low, :] = branch(rows) + tok[low, :].astype(F32) + bias_out[...]
        return 0

    lax.fori_loop(0, half // 256, branch_own, 0)
    arrived(got_rows, 57)

    def norm_two(step, _):
        low = pl.ds(pl.multiple_of(step * 256, 256), 256)
        values = middle[low, :] + got_rows[low, :].astype(F32)
        middle[low, :] = values
        normed = norm_rows(values, gain_two[...], shift_two[...])
        second[pl.ds(pl.multiple_of(base + step * 256, 256), 256), :] = normed.astype(BF16)
        return 0

    lax.fori_loop(0, half // 256, norm_two, 0)
    send(second.at[own_rows], second.at[own_rows], 58, to_core)
    put(middle, middle_out, 23)
    forward_on(2, 1)
    arrived(second.at[other_rows], 58)
    put(second, second_out, 24)

    waits = [None, None]

    def lift(k):
        complete(1, k)
        slot = k % 2
        if waits[slot] is not None:
            for copy in waits[slot]:
                copy.wait()
        columns = pl.ds(pl.multiple_of(turn[k] * SPAN, 128), SPAN)

        def step_rows(step, _):
            rows = pl.ds(pl.multiple_of(step * 256, 256), 256)
            pre = dot_nn(second[rows, :], w_up[:, columns]) + bias[turn[k], 1:2, :]
            cdf = 0.5 * lax.erf(pre * (0.5**0.5)) + 0.5
            density = jnp.exp(-0.5 * pre * pre) * 0.3989422804014327
            hidden[slot, rows, :] = (pre * cdf).astype(BF16)
            slope[slot, rows, :] = (cdf + pre * density).astype(BF16)
            return 0

        lax.fori_loop(0, count // 256, step_rows, 0)
        waits[slot] = [
            put(hidden.at[slot], hidden_out.at[:, columns], 25 + slot),
            put(slope.at[slot], slope_out.at[:, columns], 27 + slot),
        ]
        for _ in range(2):
            outs.pop()

    lift(0)
    forward_on(2, 2)
    lift(1)
    forward_on(2, 3)
    lift(2)
    lift(3)
    put(w_up, w_up_out, 29)
    for k in range(TURNS):
        complete(2, k)

    @pl.when(moves)
    def _():
        clip_cot.wait()

    @pl.when(jnp.logical_not(moves))
    def _():
        cot_copy.wait()

    for copy in outs + waits[0] + waits[1]:
        copy.wait()
    for copy in sent:
        copy.wait_send()


def forward_pass(
    shards, tokens, cotangent, mask, bias, gain_one, shift_one, gain_two, shift_two, bias_out
):
    half, features = tokens.shape
    count = 2 * half
    any_space = pl.BlockSpec(memory_space=pl.ANY)
    vmem = pl.BlockSpec(memory_space=pltpu.VMEM)
    wide = (features, TURNS * SPAN)
    shapes = [
        (wide, BF16), (wide, BF16), (wide, BF16), ((half, features), BF16), ((half, features), BF16),
        ((8, count), F32), ((count, features), BF16), ((count, features), BF16),
        ((TURNS, count, 480), BF16), ((TURNS, count, 256), BF16), ((TURNS, 8, count), F32),
        ((half, features), F32), ((count, TURNS * SPAN), BF16), ((count, TURNS * SPAN), BF16),
    ]
    return pl.pallas_call(
        functools.partial(forward_kernel, HDIM ** (-0.5)),
        in_specs=[any_space] * 7 + [vmem] * 5,
        out_specs=[any_space] * len(shapes),
        out_shape=[jax.ShapeDtypeStruct(shape, kind) for shape, kind in shapes],
        scratch_shapes=[
            pltpu.VMEM(wide, BF16),
            pltpu.VMEM(wide, BF16),
            pltpu.VMEM((half, features), BF16),
            pltpu.VMEM((count, features), BF16),
            pltpu.VMEM((count, features), BF16),
            pltpu.VMEM((TURNS, count, 480), BF16),
            pltpu.VMEM((TURNS, count, 256), BF16),
            pltpu.VMEM((half, features), F32),
            pltpu.VMEM((half, features), BF16),
            pltpu.VMEM((half, features), BF16),
            pltpu.VMEM((2, count, SPAN), BF16),
            pltpu.VMEM((2, count, SPAN), BF16),
            pltpu.VMEM((8, count), F32),
            pltpu.VMEM((TURNS, 8, count), F32),
            pltpu.VMEM((TURNS, 8, SPAN), F32),
            pltpu.SemaphoreType.DMA((64,)),
            pltpu.SemaphoreType.DMA((64,)),
            pltpu.SemaphoreType.DMA((32,)),
        ],
        cost_estimate=pl.CostEstimate(
            flops=2 * count * features * 6400, bytes_accessed=80_000_000, transcendentals=30_000_000
        ),
        compiler_params=pltpu.CompilerParams(
            vmem_limit_bytes=60 << 20, collective_id=0, has_side_effects=True
        ),
        name="forward_pass",
    )(*shards, tokens, cotangent, mask, bias, gain_one, shift_one, gain_two, shift_two, bias_out)


class Links:
    def __init__(self):
        self.dp = lax.axis_size("dp")
        self.tensor = lax.axis_size("tensor")
        self.tensor_pos = lax.axis_index("tensor")
        self.half = self.tensor_pos % 2

    def pair(self, value):
        return lax.ppermute(value, "tensor", [(i, i ^ 1) for i in range(self.tensor)])

    def columns(self, shard):
        rows, _, width = shard.shape
        whole = lax.all_gather(shard, ("dp", "tensor"), axis=0)
        whole = lax.dynamic_index_in_dim(whole, self.half, 2, keepdims=False)
        whole = whole.reshape(self.dp, self.tensor, rows, width)
        return [whole[:, k].reshape(self.dp * rows, width) for k in range(self.tensor)]

    def vectors(self, value):
        whole = lax.all_gather(value, "tensor", axis=0)
        return [whole[k] for k in range(self.tensor)]

    def place(self, pieces):
        halves = (jnp.arange(2) == self.half)[None, :, None]
        return jnp.where(halves, jnp.stack(pieces)[:, None, :], 0.0)

    def gradient(self, left, rights):
        whole = jnp.stack([dot_tn(left, right).astype(BF16) for right in rights], 0)
        features, width = whole.shape[1:]
        whole = whole.reshape(self.tensor, self.dp, features // self.dp, width)
        whole = jnp.moveaxis(whole, 1, 0)[:, :, :, None, :]
        halves = (jnp.arange(2) == self.half)[None, None, None, :, None]
        whole = jnp.where(halves, whole, jnp.zeros((), BF16))
        whole = whole.reshape((self.dp * self.tensor,) + whole.shape[2:])
        return lax.psum_scatter(whole, ("dp", "tensor"), tiled=False).astype(F32)

    def merged(self, partial_of):
        got = self.pair(partial_of(1).astype(BF16))
        return partial_of(0) + got.astype(F32)


def summed(vectors, total):
    whole = total(jnp.concatenate(vectors))
    at = 0
    result = []
    for vector in vectors:
        result.append(whole[at : at + vector.shape[0]])
        at += vector.shape[0]
    return result


def halves_of(weight):
    return weight.reshape(weight.shape[0], 2, weight.shape[1] // 2)


def flat(piece):
    return piece.reshape(piece.shape[0], -1)


def local_any(
    tokens,
    lengths,
    cotangent,
    norm1_gain,
    norm1_shift,
    query_weight,
    query_bias,
    key_weight,
    value_weight,
    value_bias,
    out_weight,
    out_bias,
    norm2_gain,
    norm2_shift,
    up_weight,
    up_bias,
    down_weight,
    down_bias,
):
    links = Links()
    rows = tokens.shape[0]
    scaling = HDIM ** (-0.5)
    width = query_weight.shape[1] // 2
    heads = width // HDIM
    units = up_weight.shape[1] // 2
    count = links.tensor

    shard_attn = [query_weight, key_weight, value_weight, out_weight.T]
    w_attn = links.columns(jnp.concatenate([halves_of(w) for w in shard_attn], -1))
    w_up = jnp.concatenate(links.columns(halves_of(up_weight)), 1)
    w_down = jnp.concatenate(links.columns(halves_of(down_weight.T)), 1)
    w_qkv = [block[:, : 3 * width] for block in w_attn]
    w_out = [block[:, 3 * width :] for block in w_attn]
    small = [query_bias.reshape(2, width), value_bias.reshape(2, width), up_bias.reshape(2, units)]
    small = jnp.concatenate(small, -1)
    small = links.vectors(jnp.where(links.half == 0, small[0], small[1]))
    bias_qkv = [
        jnp.concatenate([v[:width], jnp.zeros((width,), F32), v[width : 2 * width]]) for v in small
    ]
    bias_up = jnp.concatenate([v[2 * width :] for v in small])

    place = links.tensor_pos // 2
    clip_length = jnp.sum(jnp.where(jnp.arange(lengths.shape[0]) == place, lengths, 0))
    frames = jnp.arange(rows)
    frames = jnp.concatenate([links.half * rows + frames, (1 - links.half) * rows + frames])
    visible = frames < clip_length
    mask = jnp.where(visible, 0.0, -1e30).astype(F32)

    def part_of(value, part):
        return value[part * rows : (part + 1) * rows]

    def both(value):
        return jnp.concatenate([value, links.pair(value)])

    source = tokens.astype(F32)
    first = both(norm_rows(source, norm1_gain, norm1_shift).astype(BF16))
    joined, heads_out, totals = [], [], []
    for k in range(count):
        joined.append((dot_nn(first, w_qkv[k]) + bias_qkv[k]).astype(BF16))
        mixed, total = attend(joined[k], mask[None, :], heads, scaling)
        heads_out.append(mixed)
        totals.append(total)
    heads_all = jnp.concatenate(heads_out, 1)
    w_out_all = jnp.concatenate(w_out, 1)
    branch = links.merged(lambda part: dot_nt(part_of(heads_all, part), w_out_all))
    middle = source + branch + out_bias
    second = both(norm_rows(middle, norm2_gain, norm2_shift).astype(BF16))
    hidden, slope = up_gelu(second, w_up, bias_up[None, :])
    out_own = cotangent * visible[:rows].astype(BF16)[:, None]
    out_grad = both(out_own)

    def cut(value):
        return [value[:, k * units : (k + 1) * units] for k in range(count)]

    grad_down = links.gradient(out_grad, cut(hidden))
    down_out = links.merged(lambda part: dot_nt(part_of(hidden, part), w_down))
    layer_out = (middle + down_out + down_bias).astype(BF16)
    grad_pre = (dot_nn(out_grad, w_down) * slope.astype(F32)).astype(BF16)
    grad_up = links.gradient(second, cut(grad_pre))
    grad_second = links.merged(lambda part: dot_nt(part_of(grad_pre, part), w_up))
    back_two, grad_gain_two, grad_shift_two = norm_back(middle, norm2_gain, grad_second)
    grad_middle = out_own.astype(F32) + back_two
    branch_grad = both(grad_middle.astype(BF16))
    grad_heads = [dot_nn(branch_grad, w_out[k]).astype(BF16) for k in range(count)]
    grad_out_w = links.gradient(branch_grad, heads_out)
    grad_joined, sums = [], []
    for k in range(count):
        back, sum_k = attend_back(joined[k], grad_heads[k], totals[k], mask[:, None], heads, scaling)
        grad_joined.append(back)
        sums.append(sum_k)
    grad_qkv = links.gradient(first, grad_joined)
    grad_all = jnp.concatenate(grad_joined, 1)
    w_qkv_all = jnp.concatenate(w_qkv, 1)
    grad_first = links.merged(lambda part: dot_nt(part_of(grad_all, part), w_qkv_all))
    back_one, grad_gain_one, grad_shift_one = norm_back(source, norm1_gain, grad_first)
    grad_tokens = (grad_middle + back_one).astype(BF16)

    vectors = [
        links.place([v[0] for v in cut(jnp.sum(grad_pre.astype(F32), 0)[None, :])]).reshape(-1),
        links.place([s[0, :width] for s in sums]).reshape(-1),
        links.place([s[1, :width] for s in sums]).reshape(-1),
        grad_gain_one,
        grad_shift_one,
        jnp.sum(grad_middle, 0),
        grad_gain_two,
        grad_shift_two,
        jnp.sum(out_own.astype(F32), 0),
    ]
    sum_up, sum_query, sum_value, *rest = summed(
        vectors, lambda value: lax.psum(value, ("dp", "tensor"))
    )
    sum_gain_one, sum_shift_one, sum_out, sum_gain_two, sum_shift_two, sum_down = rest

    def own(vector):
        size = vector.shape[0] // count
        return lax.dynamic_slice_in_dim(vector, links.tensor_pos * size, size, 0)

    return (
        layer_out,
        grad_tokens,
        sum_gain_one,
        sum_shift_one,
        flat(grad_qkv[:, :, :width]),
        own(sum_query),
        flat(grad_qkv[:, :, width : 2 * width]),
        flat(grad_qkv[:, :, 2 * width :]),
        own(sum_value),
        flat(grad_out_w).T,
        sum_out,
        sum_gain_two,
        sum_shift_two,
        flat(grad_up),
        own(sum_up),
        flat(grad_down).T,
        sum_down,
    )


def local_chips(
    tokens,
    lengths,
    cotangent,
    norm1_gain,
    norm1_shift,
    query_weight,
    query_bias,
    key_weight,
    value_weight,
    value_bias,
    out_weight,
    out_bias,
    norm2_gain,
    norm2_shift,
    up_weight,
    up_bias,
    down_weight,
    down_bias,
):
    dp, z = lax.axis_index("dp"), lax.axis_index("tensor")
    core, plane = dp % 2, dp // 2
    half = tokens.shape[0]
    count = 2 * half
    scaling = HDIM ** (-0.5)
    width, units = 160, SPAN

    def split(weight):
        return jnp.moveaxis(halves_of(weight), 1, 0)

    shards = (
        jnp.concatenate([split(w) for w in (query_weight, key_weight, value_weight, out_weight.T)], -1),
        split(up_weight),
        split(down_weight.T),
    )
    place = jnp.sum(jnp.where(jnp.arange(lengths.shape[0]) == z // 2, lengths, 0))
    mask = jnp.where(jnp.arange(count) < place, 0.0, -1e30).astype(F32)
    mask = jnp.broadcast_to(mask[None, :], (8, count))
    small = [query_bias.reshape(2, width), jnp.zeros((2, width), F32), value_bias.reshape(2, width)]
    small = jnp.concatenate(small + [jnp.zeros((2, width), F32)], -1)
    small = jnp.stack([small, up_bias.reshape(2, units)], 1)
    small = jnp.pad(jnp.where(core == 0, small[0], small[1]), ((0, 6), (0, 0)))
    (
        w_attn, w_up, w_down, tok, cot, mask, first, second, joined, heads, totals, middle, hidden, slope,
    ) = forward_pass(
        shards, tokens, cotangent, mask, small,
        norm1_gain[None, :], norm1_shift[None, :], norm2_gain[None, :], norm2_shift[None, :],
        out_bias[None, :],
    )

    def pair(value):
        return lax.ppermute(value, "dp", [(i, i ^ 1) for i in range(8)])

    def along_x(value):
        return lax.ppermute(value, "dp", [(i, i ^ 2) for i in range(8)])

    def along_y(value):
        return lax.ppermute(value, "dp", [(i, i ^ 4) for i in range(8)])

    def along_z(value, shift):
        return lax.ppermute(value, "tensor", [(i, (i + shift) % 4) for i in range(4)])

    def move_rows(value):
        swaps = [
            (a * 4 + b, (a ^ 1) * 4 + (b ^ 1)) for a in range(8) for b in range(4) if a % 2 != b % 2
        ]
        moved = lax.ppermute(value, ("dp", "tensor"), swaps)
        return jnp.where(core == z % 2, value, moved)

    def part_of(value, part):
        start = (core if part == 0 else 1 - core) * half
        return lax.dynamic_slice_in_dim(value, start, half, 0)

    def both(value):
        got = pair(value)
        first_one = core == 0
        return jnp.concatenate([jnp.where(first_one, value, got), jnp.where(first_one, got, value)])

    def merged(partial_of):
        got = pair(partial_of(1).astype(BF16))
        return partial_of(0) + got.astype(F32)

    def scatter(left, right, x_first, blocks):
        def part(index):
            columns = lax.dynamic_slice_in_dim(left, (plane ^ index) * UNIT, UNIT, 1)
            return dot_tn(columns, right)

        near, far = (1, 2) if x_first else (2, 1)
        go, follow = (along_x, along_y) if x_first else (along_y, along_x)
        sent_far = go(part(3).astype(BF16))
        sent_near = go(part(near).astype(BF16))
        second_part = (part(far) + sent_far.astype(F32)).astype(BF16)
        first_part = part(0) + sent_near.astype(F32)
        product = (first_part + follow(second_part).astype(F32)).astype(BF16)
        size = product.shape[1] // blocks
        return [product[:, i * size : (i + 1) * size] for i in range(blocks)]

    def finish(blocks):
        stacked = jnp.stack(blocks)
        picked = [
            lax.dynamic_index_in_dim(stacked, (z - k) % 4, 0, keepdims=False) for k in range(4)
        ]
        total = picked[0].astype(F32)
        for k in range(1, 4):
            total = total + along_z(picked[k], -k).astype(F32)
        rows = UNIT // 2
        first_one = core == 0
        keep = jnp.where(first_one, total[:rows], total[rows:])
        got = pair(jnp.where(first_one, total[rows:], total[:rows]))
        return jnp.where(first_one, jnp.stack([keep, got], 1), jnp.stack([got, keep], 1))

    def gradient(left, right):
        cut = right.shape[1] // 2
        return finish(
            scatter(left, right[:, :cut], True, 2) + scatter(left, right[:, cut:], False, 2)
        )

    def total(value):
        for bit in (1, 2, 4):
            value = value + lax.ppermute(value, "dp", [(i, i ^ bit) for i in range(8)])
        for bit in (1, 2):
            value = value + lax.ppermute(value, "tensor", [(i, i ^ bit) for i in range(4)])
        return value

    def spread(pieces):
        halves = (jnp.arange(2) == core)[None, :, None]
        return jnp.where(halves, jnp.stack(pieces)[:, None, :], 0.0).reshape(-1)

    source = tok.astype(F32)
    valid = (part_of(mask[0], 0) == 0.0).astype(BF16)[:, None]
    out_own = cot * valid
    out_grad = both(out_own)
    grad_down = gradient(out_grad, hidden)
    down_out = merged(lambda part: dot_nt(part_of(hidden, part), w_down))
    layer_out = move_rows((middle + down_out + down_bias).astype(BF16))
    grad_pre = (dot_nn(out_grad, w_down) * slope.astype(F32)).astype(BF16)
    grad_up = gradient(second, grad_pre)
    grad_second = merged(lambda part: dot_nt(part_of(grad_pre, part), w_up))
    back_two, grad_gain_two, grad_shift_two = norm_back(middle, norm2_gain, grad_second)
    grad_middle = out_own.astype(F32) + back_two
    branch_grad = both(grad_middle.astype(BF16))
    w_qkv = [w_attn[:, k * SPAN : k * SPAN + 480] for k in range(4)]
    w_out = [w_attn[:, k * SPAN + 480 : (k + 1) * SPAN] for k in range(4)]
    grad_heads = [dot_nn(branch_grad, w_out[k]).astype(BF16) for k in range(4)]
    heads_all = jnp.concatenate([heads[k, :, 96:] for k in range(4)], 1)
    grad_out_w = finish(scatter(branch_grad, heads_all, True, 4))
    grad_joined, sums = [], []
    for k in range(4):
        back, sum_k = attend_back(
            joined[k], grad_heads[k], totals[k, :2], mask[0][:, None], 2, scaling
        )
        grad_joined.append(back)
        sums.append(sum_k)
    grad_qkv = finish(
        [scatter(first, grad_joined[k], k % 2 == 0, 1)[0] for k in range(4)]
    )
    grad_all = jnp.concatenate(grad_joined, 1)
    w_qkv_all = jnp.concatenate(w_qkv, 1)
    grad_first = merged(lambda part: dot_nt(part_of(grad_all, part), w_qkv_all))
    back_one, grad_gain_one, grad_shift_one = norm_back(source, norm1_gain, grad_first)
    grad_tokens = move_rows((grad_middle + back_one).astype(BF16))

    up_sum = jnp.sum(grad_pre.astype(F32), 0)
    sum_up, sum_out, sum_gain_two, sum_shift_two, sum_down = summed(
        [
            spread([up_sum[k * units : (k + 1) * units] for k in range(4)]),
            jnp.sum(grad_middle, 0),
            grad_gain_two,
            grad_shift_two,
            jnp.sum(out_own.astype(F32), 0),
        ],
        total,
    )
    sum_query, sum_value, sum_gain_one, sum_shift_one = summed(
        [
            spread([s[0, :width] for s in sums]),
            spread([s[1, :width] for s in sums]),
            grad_gain_one,
            grad_shift_one,
        ],
        total,
    )

    def own(vector):
        size = vector.shape[0] // 4
        return lax.dynamic_slice_in_dim(vector, z * size, size, 0)

    return (
        layer_out,
        grad_tokens,
        sum_gain_one,
        sum_shift_one,
        flat(grad_qkv[:, :, :width]),
        own(sum_query),
        flat(grad_qkv[:, :, width : 2 * width]),
        flat(grad_qkv[:, :, 2 * width :]),
        own(sum_value),
        flat(grad_out_w).T,
        sum_out,
        sum_gain_two,
        sum_shift_two,
        flat(grad_up),
        own(sum_up),
        flat(grad_down).T,
        sum_down,
    )


def solution(mesh):
    rows = P(("dp", "tensor"), None)
    wide, tall = P("dp", "tensor"), P("tensor", "dp")
    piece, same = P("tensor"), P()
    chips = mesh.shape["dp"] == 8 and mesh.shape["tensor"] == 4
    return jax.shard_map(
        local_chips if chips else local_any,
        mesh=mesh,
        in_specs=(
            rows, P("dp"), rows, same, same, wide, piece, wide, wide, piece, tall, same, same, same,
            wide, piece, tall, same,
        ),
        out_specs=(
            rows, rows, same, same, wide, piece, wide, wide, piece, tall, same, same, same, wide, piece,
            tall, same,
        ),
        check_vma=False,
    )
```

time: 1010 us -> 810 us (0.80)
  Pallas kernels: 158 us -> 299 us
  waiting for transfers between devices: 233 us -> 99.7 us
  other arithmetic: 156 us -> 33.6 us
  starting transfers between devices: 166 us -> 90.7 us
    pallas_call x5 -> x1, Pallas kernels: 64.2 us -> 204 us  [forward_pass(): pl.pallas_call(functools.partial(forward_kernel, HDIM ** (-0.5)), in_spec...]
    concatenate x12 -> x3, other arithmetic: 111 us -> 1.11 us  [the longest x1 1.02 us: local_chips(): jnp.concatenate([split(w) for w in (query_weight, key_weight, value_weigh...]
    ppermute x31 -> x13, waiting for transfers between devices: 97.1 us -> 41.7 us  [along_y(): return lax.ppermute(value, 'dp', [(i, i ^ 4) for i in range(8)])]
    ppermute x24 -> x12, waiting for transfers between devices: 75.2 us -> 26.3 us  [along_z(): lax.ppermute(value, 'tensor', [(i, (i + shift) % 4) for i in range(4)])]
    ppermute x32 -> x14, waiting for transfers between devices: 48.9 us -> 20.2 us  [along_x(): return lax.ppermute(value, 'dp', [(i, i ^ 2) for i in range(8)])]
    ppermute x24 -> x12, starting transfers between devices: 29 us -> 8.59 us  [along_z(): lax.ppermute(value, 'tensor', [(i, (i + shift) % 4) for i in range(4)])]
    ppermute x32 -> x14, starting transfers between devices: 31.3 us -> 11.3 us  [along_x(): return lax.ppermute(value, 'dp', [(i, i ^ 2) for i in range(8)])]
    concatenate x25 -> x3, local copies, waits for them, and re-layouts: 39.1 us -> 19.5 us  [the longest x1 10.4 us: local_chips(): grad_all = jnp.concatenate(grad_joined, 1)]
  transfers between devices with their start and end apart: 117 -> 60, of which waited for: 37 -> 20; matrix products, arithmetic and copies ran while one was open for 37% -> 26% of each run, Pallas kernels for 6% -> 0%
where the time goes in v2:
time: 810 us; the launch traced here: 798 us
  Pallas kernels  299 us (37%)
  matrix products  188 us (23%)
  waiting for transfers between devices  99.7 us (12%)
  starting transfers between devices  90.7 us (11%)
  local copies, waits for them, and re-layouts  84.6 us (10%)
  other arithmetic  33.6 us (4%)
    pallas_call x1, Pallas kernels, forward_pass(): pl.pallas_call(functools.partial(forward_kernel, HDIM ** (-0.5)), in_spec...  204 us
    dot_general x36, matrix products, dot_tn(): lax.dot_general(left, right, (((0,), (0,)), ((), ())), preferred_element_...  103 us
    pallas_call x4, Pallas kernels, attend_back(): pl.pallas_call(functools.partial(attend_back_kernel, heads, scaling), gri...  94.5 us
    dot_general x6, matrix products, dot_nt(): lax.dot_general(left, right, (((1,), (1,)), ((), ())), preferred_element_...  55.7 us
    ppermute x13, waiting for transfers between devices, along_y(): return lax.ppermute(value, 'dp', [(i, i ^ 4) for i in range(8)])  41.7 us
    ppermute x9, starting transfers between devices, pair(): return lax.ppermute(value, 'dp', [(i, i ^ 1) for i in range(8)])  34.6 us
    dot_general x5, matrix products, dot_nn(): return jnp.dot(left, right, preferred_element_type=F32)  29.1 us
    ppermute x12, waiting for transfers between devices, along_z(): lax.ppermute(value, 'tensor', [(i, (i + shift) % 4) for i in range(4)])  26.3 us
  transfers between devices with their start and end apart: 60, of which 20 were waited for; matrix products, arithmetic and copies ran while one was open for 26% of the time, Pallas kernels for 0%

profile of v2, /device:TPU:1, one launch (start us, length us, event | category | flops | bytes accessed | tf_op | source)
XLA Modules:
  0.0 797.8 jit_solution(16907046463578607967)
XLA Ops:
  18.9 204.1 %forward_pass.1 = (bf16[1280,2560]{1,0:T(8,128)(2,1)}, bf16[1280,2560]{1,0:T(8,128)(2,1)}, bf16[1280,2560]{1,0:T(8,128)(2,1)}, bf16[768,1280]{1,0:T(8,128)(2,1)}...) custom-call(bf16[2,160,640]{2,1,0:T(8,128)(2,1)} %pad_maximum_fusion, ...), custom_call_target="tpu_custom_call" | custom-call | flops 25165824000 | bytes 80000000 | tf_op jit(solution)/shard_map/forward_pass/pallas_call | solution.py:582
  226.6 9.9 %fusion.24 = bf16[768,1280]{1,0:T(8,128)(2,1)} fusion(bf16[1280,2560]{1,0:T(8,128)(2,1)} %get-tuple-element.41, bf16[1536,2560]{1,0:T(8,128)(2,1)} %get-tuple-element.40, s32[]{:T(128)S(6)} %select_n.319), kind=kOutput, calls=%fused_computation.53 | convolution fusion | flops 5034147840 | bytes 12451844 | tf_op jit(solution)/shard_map/dot_general | solution.py:42
  238.9 2.6 multiply_reduce_fusion.2
  242.8 4.7 fusion.196
  249.1 9.0 %concatenate.32 = bf16[1280,1920]{1,0:T(8,128)(2,1)} concatenate(bf16[1280,480]{1,0:T(8,128)(2,1)} %get-tuple-element.76, bf16[1280,480]{1,0:T(8,128)(2,1)} %get-tuple-element.75, bf16[1280,480]{1,0:T(8,128)(2,1)} %get-tuple-element.74, bf16[1280,480]{1,0:T(8,128)(2,1)S(1)} %get-tuple-element.73), dimensions={1} | concatenate | bytes 9830400 | tf_op jit(solution)/shard_map/concatenate | solution.py:971
  260.3 5.4 slice_bitcast_fusion.7
  265.7 5.7 slice_bitcast_fusion
  273.2 3.0 convolution_convert_fusion.3
  276.2 3.0 convolution_convert_fusion.1
  279.2 3.0 convolution_convert_fusion.4
  282.2 15.8 %convert_reduce_fusion = (f32[2560]{0:T(1024)S(1)}, bf16[1536,2560]{1,0:T(8,128)(2,1)S(1)}) fusion(bf16[1536,2560]{1,0:T(8,128)(2,1)} %get-tuple-element.44, bf16[1280,2560]{1,0:T(8,128)(2,1)} %get-tuple-element.41, bf16[768,1280]{1,0:T(8,128)(2,1)S(1)} %get-tuple-element.84, bf16[768,1280]{1,0:T(8,128)(2,1)S(1)} %get-tuple-element.83), kind=kOutput, calls=%fused_computation | convolution fusion | flops 10093852672 | bytes 26224640 | tf_op jit(solution)/shard_map/dot_general | solution.py:34
  298.1 5.0 convolution_convert_fusion.7
  303.7 2.6 convolution_convert_fusion.8
  307.8 3.0 convolution_convert_fusion.2
  312.3 2.9 fusion.51
  315.2 2.9 fusion.45
  320.7 9.5 %fusion.27 = bf16[768,1280]{1,0:T(8,128)(2,1)} fusion(bf16[1280,2560]{1,0:T(8,128)(2,1)} %get-tuple-element.45, bf16[1536,2560]{1,0:T(8,128)(2,1)S(1)} %get-tuple-element.155, s32[]{:T(128)S(6)} %select_n.319), kind=kOutput, calls=%fused_computation.54 | convolution fusion | flops 5034147840 | bytes 12451844 | tf_op jit(solution)/shard_map/dot_general | solution.py:42
  330.5 10.7 %add_convert_fusion = bf16[768,1280]{1,0:T(8,128)(2,1)} fusion(f32[768,1280]{1,0:T(8,128)S(1)} %copy-done.13, bf16[768,1280]{1,0:T(8,128)(2,1)} %collective-permute-done, bf16[1280,2560]{1,0:T(8,128)(2,1)} %get-tuple-element.41, bf16[1536,2560]{1,0:T(8,128)(2,1)} %get-tuple-element.40, s32[]{:T(128)S(6)} %select_n.318, f32[1280]{0:T(1024)S(1)} %copy-done.60), kind=kOutput, calls=%fused_computation.45 | convolution fusion | flops 5038080000 | bytes 18355204 | tf_op jit(solution)/shard_map/dot_general | solution.py:42
  341.2 4.0 convolution_convert_fusion.6
  346.5 4.8 fusion.37
  351.7 4.6 fusion.38
  356.3 4.8 collective-permute-done.41
  361.4 3.5 add_convert_fusion.4
  364.9 4.2 collective-permute-done.44
  369.1 3.2 add_convert_fusion.2
  372.4 14.2 %collective-permute-done.52 = bf16[320,1280]{1,0:T(8,128)(2,1)S(1)} collective-permute-done((bf16[320,1280]{1,0:T(8,128)(2,1)S(1)}, bf16[320,1280]{1,0:T(8,128)(2,1)S(1)}, u32[]{:S(2)}, u32[]{:S(2)}) %collective-permute-start.52) | collective-permute-done | bytes 819232 | tf_op jit(solution)/shard_map/ppermute | solution.py:871
  386.7 5.4 collective-permute-start.3
  392.1 3.3 fusion.39
  401.2 20.6 %collective-permute-done.42 = bf16[320,1280]{1,0:T(8,128)(2,1)S(1)} collective-permute-done((bf16[320,1280]{1,0:T(8,128)(2,1)S(1)}, bf16[320,1280]{1,0:T(8,128)(2,1)S(1)}, u32[]{:S(2)}, u32[]{:S(2)}) %collective-permute-start.42) | collective-permute-done | bytes 819232 | tf_op jit(solution)/shard_map/ppermute | solution.py:871
  426.2 10.2 %multiply_reduce_fusion = (f32[1280]{0:T(1024)S(1)}, f32[768]{0:T(1024)S(1)}, f32[768]{0:T(1024)S(1)}, f32[1280]{0:T(1024)S(1)}, f32[768,1280]{1,0:T(8,128)S(1)}) fusion(f32[768,1280]{1,0:T(8,128)S(1)} %copy-done.14, f32[768]{0:T(1024)S(1)} %add_rsqrt_fusion.1, f32[768]{0:T(1024)S(1)} %broadcast_multiply_fusion.5, f32[1280]{0:T(1024)S(1)} %copy-done.53, ...), kind=kOutput, calls=%fused_computation.36 | convolution fusion | flops 5043974144 | bytes 20343812 | tf_op jit(solution)/shard_map/dot_general | solution.py:42
  438.3 3.6 collective-permute-start.35
  448.8 6.3 collective-permute-done.57
  458.6 21.2 %collective-permute-start.59 = (f32[160,640]{1,0:T(8,128)S(1)}, f32[160,640]{1,0:T(8,128)S(1)}, u32[]{:S(2)}, u32[]{:S(2)}) collective-permute-start(f32[160,640]{1,0:T(8,128)S(1)} %get-tuple-element.99), channel_id=1, source_target_pairs={{0,4},{4,0},{8,12},{12,8},{16,20},{20,16},{24,28},{28,24},{1,5},{5... | collective-permute-start | bytes 1228808 | tf_op jit(solution)/shard_map/ppermute | solution.py:865
  480.7 9.4 %collective-permute-done.47 = bf16[320,640]{1,0:T(8,128)(2,1)S(1)} collective-permute-done((bf16[320,640]{1,0:T(8,128)(2,1)S(1)}, bf16[320,640]{1,0:T(8,128)(2,1)S(1)}, u32[]{:S(2)}, u32[]{:S(2)}) %collective-permute-start.47) | collective-permute-done | bytes 409632 | tf_op jit(solution)/shard_map/ppermute | solution.py:874
  490.4 5.5 collective-permute-start.39
  503.2 3.3 convolution_convert_fusion.14
  506.5 3.3 convolution_convert_fusion.13
  509.8 2.8 convolution_convert_fusion.12
  513.7 23.5 %attend_back.4 = (bf16[1536,480]{1,0:T(8,128)(2,1)}, f32[8,256]{1,0:T(8,128)}) custom-call(bf16[1536,480]{1,0:T(8,128)(2,1)} %get-tuple-element.80.query_ref.all_ref, bf16[1536,480]{1,0:T(8,128)(2,1)} %get-tuple-element.80.query_ref.all_ref, bf16[1536,160]{1,0:T(8,128)(2,1)} %copy.65.grad_ref, f32[2,1536]{1,0:T(2,128)} %get-tuple-element.127.total_ref, ...), custom_call_target="tpu_custom_call" | custom-call | flops 12079595520 | bytes 5000000 | tf_op jit(solution)/shard_map/attend_back/pallas_call | solution.py:180
  537.3 3.5 convolution_convert_fusion.22
  544.7 3.5 convolution_convert_fusion.11
  550.4 23.9 %attend_back.5 = (bf16[1536,480]{1,0:T(8,128)(2,1)}, f32[8,256]{1,0:T(8,128)}) custom-call(bf16[1536,480]{1,0:T(8,128)(2,1)} %get-tuple-element.79.query_ref.all_ref, bf16[1536,480]{1,0:T(8,128)(2,1)} %get-tuple-element.79.query_ref.all_ref, bf16[1536,160]{1,0:T(8,128)(2,1)} %copy.67.grad_ref, f32[2,1536]{1,0:T(2,128)} %get-tuple-element.126.total_ref, ...), custom_call_target="tpu_custom_call" | custom-call | flops 12079595520 | bytes 5000000 | tf_op jit(solution)/shard_map/attend_back/pallas_call | solution.py:180
  574.3 3.5 convolution_convert_fusion.20
  581.8 3.5 convolution_convert_fusion.10
  587.5 23.5 %attend_back.6 = (bf16[1536,480]{1,0:T(8,128)(2,1)}, f32[8,256]{1,0:T(8,128)}) custom-call(bf16[1536,480]{1,0:T(8,128)(2,1)} %get-tuple-element.78.query_ref.all_ref, bf16[1536,480]{1,0:T(8,128)(2,1)} %get-tuple-element.78.query_ref.all_ref, bf16[1536,160]{1,0:T(8,128)(2,1)} %copy.69.grad_ref, f32[2,1536]{1,0:T(2,128)} %get-tuple-element.125.total_ref, ...), custom_call_target="tpu_custom_call" | custom-call | flops 12079595520 | bytes 5000000 | tf_op jit(solution)/shard_map/attend_back/pallas_call | solution.py:180
  611.0 3.5 convolution_convert_fusion.18
  618.6 3.4 convolution_convert_fusion.9
  624.2 23.5 %attend_back.7 = (bf16[1536,480]{1,0:T(8,128)(2,1)}, f32[8,256]{1,0:T(8,128)}) custom-call(bf16[1536,480]{1,0:T(8,128)(2,1)} %get-tuple-element.77.query_ref.all_ref, bf16[1536,480]{1,0:T(8,128)(2,1)} %get-tuple-element.77.query_ref.all_ref, bf16[1536,160]{1,0:T(8,128)(2,1)} %copy.71.grad_ref, f32[2,1536]{1,0:T(2,128)} %get-tuple-element.124.total_ref, ...), custom_call_target="tpu_custom_call" | custom-call | flops 12079595520 | bytes 5000000 | tf_op jit(solution)/shard_map/attend_back/pallas_call | solution.py:180
  647.7 2.8 convolution_convert_fusion.16
  654.5 10.4 %concatenate.31 = bf16[1536,1920]{1,0:T(8,128)(2,1)} concatenate(bf16[1536,480]{1,0:T(8,128)(2,1)S(1)} %copy-done.7, bf16[1536,480]{1,0:T(8,128)(2,1)S(1)} %copy-done.8, bf16[1536,480]{1,0:T(8,128)(2,1)} %get-tuple-element.51, bf16[1536,480]{1,0:T(8,128)(2,1)} %get-tuple-element.52), dimensions={1} | concatenate | bytes 11796480 | tf_op jit(solution)/shard_map/concatenate | solution.py:970
  671.1 8.8 %convolution_convert_fusion = bf16[768,1280]{1,0:T(8,128)(2,1)} fusion(bf16[1280,1920]{1,0:T(8,128)(2,1)} %concatenate.32, bf16[1536,1920]{1,0:T(8,128)(2,1)} %concatenate.31, s32[]{:T(128)S(6)} %select_n.319), kind=kOutput, calls=%fused_computation.55 | convolution fusion | flops 3775856640 | bytes 9830404 | tf_op jit(solution)/shard_map/dot_general | solution.py:42
  680.1 8.3 %collective-permute-done.13 = bf16[320,480]{1,0:T(8,128)(2,1)} collective-permute-done((bf16[320,480]{1,0:T(8,128)(2,1)}, bf16[320,480]{1,0:T(8,128)(2,1)}, u32[]{:S(2)}, u32[]{:S(2)}) %collective-permute-start.13) | collective-permute-done | bytes 307232 | tf_op jit(solution)/shard_map/ppermute | solution.py:868
  688.5 2.8 add_convert_fusion.12
  691.6 2.8 add_convert_fusion.10
  700.4 3.6 fusion.63
  706.8 6.3 collective-permute-start.5
  724.9 4.7 collective-permute-done.28
  735.3 3.2 collective-permute-start.31
  738.6 6.7 fusion.10
  747.1 10.2 %collective-permute-done.25 = bf16[320,480]{1,0:T(8,128)(2,1)} collective-permute-done((bf16[320,480]{1,0:T(8,128)(2,1)}, bf16[320,480]{1,0:T(8,128)(2,1)}, u32[]{:S(2)}, u32[]{:S(2)}) %collective-permute-start.25) | collective-permute-done | bytes 307232 | tf_op jit(solution)/shard_map/ppermute | solution.py:874
  757.3 6.8 collective-permute-start.6
  766.1 4.0 collective-permute-start.7
  779.9 6.3 collective-permute-done.10
  794.5 3.0 broadcast_select_fusion.4
  (403 shorter events, 148.4 us)
Async XLA Ops:
  226.0 45.4 %collective-permute-start.2 = (bf16[768,1280]{1,0:T(8,128)(2,1)S(1)}, bf16[768,1280]{1,0:T(8,128)(2,1)}, u32[]{:S(2)}, u32[]{:S(2)}) collective-permute-start(bf16[768,1280]{1,0:T(8,128)(2,1)S(1)} %get-tuple-element.70), channel_id=1, source_target_pairs={{0,4},{4,0},{8,12},{12,8},{16,20},{20,16},{24,28},{28,24},{1,5},{5... | collective-permute-start | bytes 5898248 | tf_op jit(solution)/shard_map/ppermute | solution.py:865
  236.5 93.6 %collective-permute-start = (bf16[768,1280]{1,0:T(8,128)(2,1)}, bf16[768,1280]{1,0:T(8,128)(2,1)}, u32[]{:S(2)}, u32[]{:S(2)}) collective-permute-start(bf16[768,1280]{1,0:T(8,128)(2,1)} %fusion.24), channel_id=1, source_target_pairs={{0,4},{4,0},{8,12},{12,8},{16,20},{20,16},{24,28},{28,24},{1,5},{5... | collective-permute-start | bytes 5898248 | tf_op jit(solution)/shard_map/ppermute | solution.py:865
  273.2 34.6 %copy-start.32 = (bf16[768,1280]{1,0:T(8,128)(2,1)}, bf16[768,1280]{1,0:T(8,128)(2,1)S(1)}, u32[]{:S(2)}) copy-start(bf16[768,1280]{1,0:T(8,128)(2,1)S(1)} %get-tuple-element.83) | copy-start | bytes 5898244
  298.0 43.1 %copy-start.61 = (bf16[1536,2560]{1,0:T(8,128)(2,1)}, bf16[1536,2560]{1,0:T(8,128)(2,1)S(1)}, u32[]{:S(2)}) copy-start(bf16[1536,2560]{1,0:T(8,128)(2,1)S(1)} %get-tuple-element.155) | copy-start | bytes 23592964
  306.3 66.0 %collective-permute-start.50 = (bf16[320,1280]{1,0:T(8,128)(2,1)}, bf16[320,1280]{1,0:T(8,128)(2,1)}, u32[]{:S(2)}, u32[]{:S(2)}) collective-permute-start(bf16[320,1280]{1,0:T(8,128)(2,1)} %convolution_convert_fusion.4), channel_id=1, source_target_pairs={{0,8},{4,12},{8,0},{12,4},{16,24},{20,28},{24,16},{28,20},{1,9},{5... | collective-permute-start | bytes 2457608 | tf_op jit(solution)/shard_map/ppermute | solution.py:868
  306.6 38.8 %collective-permute-start.51 = (bf16[320,1280]{1,0:T(8,128)(2,1)}, bf16[320,1280]{1,0:T(8,128)(2,1)}, u32[]{:S(2)}, u32[]{:S(2)}) collective-permute-start(bf16[320,1280]{1,0:T(8,128)(2,1)} %convolution_convert_fusion.3), channel_id=1, source_target_pairs={{0,8},{4,12},{8,0},{12,4},{16,24},{20,28},{24,16},{28,20},{1,9},{5... | collective-permute-start | bytes 2457608 | tf_op jit(solution)/shard_map/ppermute | solution.py:868
  310.8 84.6 %collective-permute-start.53 = (bf16[320,1280]{1,0:T(8,128)(2,1)}, bf16[320,1280]{1,0:T(8,128)(2,1)S(1)}, u32[]{:S(2)}, u32[]{:S(2)}) collective-permute-start(bf16[320,1280]{1,0:T(8,128)(2,1)} %convolution_convert_fusion.2), channel_id=1, source_target_pairs={{0,16},{4,20},{8,24},{12,28},{16,0},{20,4},{24,8},{28,12},{1,17},{... | collective-permute-start | bytes 2457608 | tf_op jit(solution)/shard_map/ppermute | solution.py:871
  311.1 40.2 %collective-permute-start.54 = (bf16[320,1280]{1,0:T(8,128)(2,1)}, bf16[320,1280]{1,0:T(8,128)(2,1)}, u32[]{:S(2)}, u32[]{:S(2)}) collective-permute-start(bf16[320,1280]{1,0:T(8,128)(2,1)} %convolution_convert_fusion.1), channel_id=1, source_target_pairs={{0,16},{4,20},{8,24},{12,28},{16,0},{20,4},{24,8},{28,12},{1,17},{... | collective-permute-start | bytes 2457608 | tf_op jit(solution)/shard_map/ppermute | solution.py:871
  330.2 30.9 %collective-permute-start.41 = (bf16[320,1280]{1,0:T(8,128)(2,1)}, bf16[320,1280]{1,0:T(8,128)(2,1)}, u32[]{:S(2)}, u32[]{:S(2)}) collective-permute-start(bf16[320,1280]{1,0:T(8,128)(2,1)} %convolution_convert_fusion.7), channel_id=1, source_target_pairs={{0,8},{4,12},{8,0},{12,4},{16,24},{20,28},{24,16},{28,20},{1,9},{5... | collective-permute-start | bytes 2457608 | tf_op jit(solution)/shard_map/ppermute | solution.py:868
  345.4 55.4 %collective-permute-start.40 = (bf16[320,1280]{1,0:T(8,128)(2,1)}, bf16[320,1280]{1,0:T(8,128)(2,1)S(1)}, u32[]{:S(2)}, u32[]{:S(2)}) collective-permute-start(bf16[320,1280]{1,0:T(8,128)(2,1)} %convolution_convert_fusion.8), channel_id=1, source_target_pairs={{0,8},{4,12},{8,0},{12,4},{16,24},{20,28},{24,16},{28,20},{1,9},{5... | collective-permute-start | bytes 2457608 | tf_op jit(solution)/shard_map/ppermute | solution.py:868
  351.3 17.8 %collective-permute-start.44 = (bf16[320,1280]{1,0:T(8,128)(2,1)S(1)}, bf16[320,1280]{1,0:T(8,128)(2,1)S(1)}, u32[]{:S(2)}, u32[]{:S(2)}) collective-permute-start(bf16[320,1280]{1,0:T(8,128)(2,1)S(1)} %copy-done.58), channel_id=1, source_target_pairs={{0,16},{4,20},{8,24},{12,28},{16,0},{20,4},{24,8},{28,12},{1,17},{... | collective-permute-start | bytes 2457608 | tf_op jit(solution)/shard_map/ppermute | solution.py:871
  361.1 25.6 %collective-permute-start.52 = (bf16[320,1280]{1,0:T(8,128)(2,1)S(1)}, bf16[320,1280]{1,0:T(8,128)(2,1)S(1)}, u32[]{:S(2)}, u32[]{:S(2)}) collective-permute-start(bf16[320,1280]{1,0:T(8,128)(2,1)S(1)} %fusion.37), channel_id=1, source_target_pairs={{0,16},{4,20},{8,24},{12,28},{16,0},{20,4},{24,8},{28,12},{1,17},{... | collective-permute-start | bytes 2457608 | tf_op jit(solution)/shard_map/ppermute | solution.py:871
  369.1 28.4 %collective-permute-start.55 = (bf16[320,1280]{1,0:T(8,128)(2,1)S(1)}, bf16[320,1280]{1,0:T(8,128)(2,1)S(1)}, u32[]{:S(2)}, u32[]{:S(2)}) collective-permute-start(bf16[320,1280]{1,0:T(8,128)(2,1)S(1)} %fusion.38), channel_id=1, source_target_pairs={{0,8},{4,12},{8,0},{12,4},{16,24},{20,28},{24,16},{28,20},{1,9},{5... | collective-permute-start | bytes 2457608 | tf_op jit(solution)/shard_map/ppermute | solution.py:868
  372.3 49.8 %collective-permute-start.43 = (bf16[320,1280]{1,0:T(8,128)(2,1)}, bf16[320,1280]{1,0:T(8,128)(2,1)S(1)}, u32[]{:S(2)}, u32[]{:S(2)}) collective-permute-start(bf16[320,1280]{1,0:T(8,128)(2,1)} %convolution_convert_fusion.6), channel_id=1, source_target_pairs={{0,16},{4,20},{8,24},{12,28},{16,0},{20,4},{24,8},{28,12},{1,17},{... | collective-permute-start | bytes 2457608 | tf_op jit(solution)/shard_map/ppermute | solution.py:871
  386.7 37.7 %collective-permute-start.3 = (bf16[768,1280]{1,0:T(8,128)(2,1)S(1)}, bf16[768,1280]{1,0:T(8,128)(2,1)}, u32[]{:S(2)}, u32[]{:S(2)}) collective-permute-start(bf16[768,1280]{1,0:T(8,128)(2,1)S(1)} %copy-done.56), channel_id=1, source_target_pairs={{0,4},{4,0},{8,12},{12,8},{16,20},{20,16},{24,28},{28,24},{1,5},{5... | collective-permute-start | bytes 5898248 | tf_op jit(solution)/shard_map/ppermute | solution.py:865
  395.4 47.7 %collective-permute-start.1 = (bf16[768,1280]{1,0:T(8,128)(2,1)S(1)}, bf16[768,1280]{1,0:T(8,128)(2,1)S(1)}, u32[]{:S(2)}, u32[]{:S(2)}) collective-permute-start(bf16[768,1280]{1,0:T(8,128)(2,1)S(1)} %copy-done.31), channel_id=1, source_target_pairs={{1,4},{3,6},{4,1},{6,3},{9,12},{11,14},{12,9},{14,11},{17,20},{19,... | collective-permute-start | bytes 5898248 | tf_op jit(solution)/shard_map/ppermute | solution.py:880
  397.5 24.3 %collective-permute-start.42 = (bf16[320,1280]{1,0:T(8,128)(2,1)S(1)}, bf16[320,1280]{1,0:T(8,128)(2,1)S(1)}, u32[]{:S(2)}, u32[]{:S(2)}) collective-permute-start(bf16[320,1280]{1,0:T(8,128)(2,1)S(1)} %add_convert_fusion.4), channel_id=1, source_target_pairs={{0,16},{4,20},{8,24},{12,28},{16,0},{20,4},{24,8},{28,12},{1,17},{... | collective-permute-start | bytes 2457608 | tf_op jit(solution)/shard_map/ppermute | solution.py:871
  400.8 21.7 %collective-permute-start.45 = (bf16[320,1280]{1,0:T(8,128)(2,1)S(1)}, bf16[320,1280]{1,0:T(8,128)(2,1)S(1)}, u32[]{:S(2)}, u32[]{:S(2)}) collective-permute-start(bf16[320,1280]{1,0:T(8,128)(2,1)S(1)} %add_convert_fusion.2), channel_id=1, source_target_pairs={{0,8},{4,12},{8,0},{12,4},{16,24},{20,28},{24,16},{28,20},{1,9},{5... | collective-permute-start | bytes 2457608 | tf_op jit(solution)/shard_map/ppermute | solution.py:868
  421.8 26.9 %collective-permute-start.56 = (bf16[320,640]{1,0:T(8,128)(2,1)S(1)}, bf16[320,640]{1,0:T(8,128)(2,1)S(1)}, u32[]{:S(2)}, u32[]{:S(2)}) collective-permute-start(bf16[320,640]{1,0:T(8,128)(2,1)S(1)} %get-tuple-element.89), channel_id=1, source_target_pairs={{0,3},{1,0},{2,1},{3,2},{4,7},{5,4},{6,5},{7,6},{8,11},{9,8},{10,9... | collective-permute-start | bytes 1228808 | tf_op jit(solution)/shard_map/ppermute | solution.py:874
  422.2 32.9 %collective-permute-start.57 = (bf16[320,640]{1,0:T(8,128)(2,1)S(1)}, bf16[320,640]{1,0:T(8,128)(2,1)}, u32[]{:S(2)}, u32[]{:S(2)}) collective-permute-start(bf16[320,640]{1,0:T(8,128)(2,1)S(1)} %get-tuple-element.91), channel_id=1, source_target_pairs={{0,2},{1,3},{2,0},{3,1},{4,6},{5,7},{6,4},{7,5},{8,10},{9,11},{10,... | collective-permute-start | bytes 1228808 | tf_op jit(solution)/shard_map/ppermute | solution.py:874
  422.5 32.8 %collective-permute-start.58 = (bf16[320,640]{1,0:T(8,128)(2,1)S(1)}, bf16[320,640]{1,0:T(8,128)(2,1)}, u32[]{:S(2)}, u32[]{:S(2)}) collective-permute-start(bf16[320,640]{1,0:T(8,128)(2,1)S(1)} %get-tuple-element.90), channel_id=1, source_target_pairs={{0,1},{1,2},{2,3},{3,0},{4,5},{5,6},{6,7},{7,4},{8,9},{9,10},{10,1... | collective-permute-start | bytes 1228808 | tf_op jit(solution)/shard_map/ppermute | solution.py:874
  438.3 61.7 %copy-start.5 = (f32[768,1280]{1,0:T(8,128)}, f32[768,1280]{1,0:T(8,128)S(1)}, u32[]{:S(2)}) copy-start(f32[768,1280]{1,0:T(8,128)S(1)} %get-tuple-element.72) | copy-start | bytes 11796484
  438.3 4.4 collective-permute-start.35
  442.8 57.2 %collective-permute-start.4 = (bf16[768,1280]{1,0:T(8,128)(2,1)S(1)}, bf16[768,1280]{1,0:T(8,128)(2,1)S(1)}, u32[]{:S(2)}, u32[]{:S(2)}) collective-permute-start(bf16[768,1280]{1,0:T(8,128)(2,1)S(1)} %convert_element_type.326), channel_id=1, source_target_pairs={{0,4},{4,0},{8,12},{12,8},{16,20},{20,16},{24,28},{28,24},{1,5},{5... | collective-permute-start | bytes 5898248 | tf_op jit(solution)/shard_map/ppermute | solution.py:865
  443.1 2.9 collective-permute-start.36
  446.0 33.8 %collective-permute-start.46 = (bf16[320,640]{1,0:T(8,128)(2,1)S(1)}, bf16[320,640]{1,0:T(8,128)(2,1)S(1)}, u32[]{:S(2)}, u32[]{:S(2)}) collective-permute-start(bf16[320,640]{1,0:T(8,128)(2,1)S(1)} %get-tuple-element.92), channel_id=1, source_target_pairs={{0,3},{1,0},{2,1},{3,2},{4,7},{5,4},{6,5},{7,6},{8,11},{9,8},{10,9... | collective-permute-start | bytes 1228808 | tf_op jit(solution)/shard_map/ppermute | solution.py:874
  448.7 41.5 %collective-permute-start.47 = (bf16[320,640]{1,0:T(8,128)(2,1)S(1)}, bf16[320,640]{1,0:T(8,128)(2,1)S(1)}, u32[]{:S(2)}, u32[]{:S(2)}) collective-permute-start(bf16[320,640]{1,0:T(8,128)(2,1)S(1)} %get-tuple-element.94), channel_id=1, source_target_pairs={{0,2},{1,3},{2,0},{3,1},{4,6},{5,7},{6,4},{7,5},{8,10},{9,11},{10,... | collective-permute-start | bytes 1228808 | tf_op jit(solution)/shard_map/ppermute | solution.py:874
  455.1 35.1 %collective-permute-start.48 = (bf16[320,640]{1,0:T(8,128)(2,1)S(1)}, bf16[320,640]{1,0:T(8,128)(2,1)S(1)}, u32[]{:S(2)}, u32[]{:S(2)}) collective-permute-start(bf16[320,640]{1,0:T(8,128)(2,1)S(1)} %get-tuple-element.93), channel_id=1, source_target_pairs={{0,1},{1,2},{2,3},{3,0},{4,5},{5,6},{6,7},{7,4},{8,9},{9,10},{10,1... | collective-permute-start | bytes 1228808 | tf_op jit(solution)/shard_map/ppermute | solution.py:874
  455.3 3.3 collective-permute-start.37
  458.6 40.4 %collective-permute-start.59 = (f32[160,640]{1,0:T(8,128)S(1)}, f32[160,640]{1,0:T(8,128)S(1)}, u32[]{:S(2)}, u32[]{:S(2)}) collective-permute-start(f32[160,640]{1,0:T(8,128)S(1)} %get-tuple-element.99), channel_id=1, source_target_pairs={{0,4},{4,0},{8,12},{12,8},{16,20},{20,16},{24,28},{28,24},{1,5},{5... | collective-permute-start | bytes 1228808 | tf_op jit(solution)/shard_map/ppermute | solution.py:865
  479.8 10.5 %collective-permute-start.38 = (f32[10240]{0:T(1024)S(1)}, f32[10240]{0:T(1024)S(1)}, u32[]{:S(2)}, u32[]{:S(2)}) collective-permute-start(f32[10240]{0:T(1024)S(1)} %add.372), channel_id=1, source_target_pairs={{0,1},{1,0},{2,3},{3,2},{4,5},{5,4},{6,7},{7,6},{8,9},{9,8},{10,11... | collective-permute-start | bytes 122888 | tf_op jit(solution)/shard_map/ppermute | solution.py:935
  490.4 7.4 collective-permute-start.39
  500.4 44.4 %copy-start.22 = (bf16[768,1280]{1,0:T(8,128)(2,1)}, bf16[768,1280]{1,0:T(8,128)(2,1)S(1)}, u32[]{:S(2)}) copy-start(bf16[768,1280]{1,0:T(8,128)(2,1)S(1)} %get-tuple-element.81) | copy-start | bytes 5898244
  664.9 34.7 %collective-permute-start.29 = (bf16[320,640]{1,0:T(8,128)(2,1)}, bf16[320,640]{1,0:T(8,128)(2,1)}, u32[]{:S(2)}, u32[]{:S(2)}) collective-permute-start(bf16[320,640]{1,0:T(8,128)(2,1)} %convolution_convert_fusion.13), channel_id=1, source_target_pairs={{0,8},{4,12},{8,0},{12,4},{16,24},{20,28},{24,16},{28,20},{1,9},{5... | collective-permute-start | bytes 1228808 | tf_op jit(solution)/shard_map/ppermute | solution.py:868
  665.0 39.1 %collective-permute-start.12 = (bf16[320,480]{1,0:T(8,128)(2,1)}, bf16[320,480]{1,0:T(8,128)(2,1)}, u32[]{:S(2)}, u32[]{:S(2)}) collective-permute-start(bf16[320,480]{1,0:T(8,128)(2,1)} %convolution_convert_fusion.22), channel_id=1, source_target_pairs={{0,8},{4,12},{8,0},{12,4},{16,24},{20,28},{24,16},{28,20},{1,9},{5... | collective-permute-start | bytes 921608 | tf_op jit(solution)/shard_map/ppermute | solution.py:868
  666.4 22.0 %collective-permute-start.13 = (bf16[320,480]{1,0:T(8,128)(2,1)}, bf16[320,480]{1,0:T(8,128)(2,1)}, u32[]{:S(2)}, u32[]{:S(2)}) collective-permute-start(bf16[320,480]{1,0:T(8,128)(2,1)} %convolution_convert_fusion.21), channel_id=1, source_target_pairs={{0,8},{4,12},{8,0},{12,4},{16,24},{20,28},{24,16},{28,20},{1,9},{5... | collective-permute-start | bytes 921608 | tf_op jit(solution)/shard_map/ppermute | solution.py:868
  666.5 40.3 %collective-permute-start.15 = (bf16[320,480]{1,0:T(8,128)(2,1)}, bf16[320,480]{1,0:T(8,128)(2,1)}, u32[]{:S(2)}, u32[]{:S(2)}) collective-permute-start(bf16[320,480]{1,0:T(8,128)(2,1)} %convolution_convert_fusion.20), channel_id=1, source_target_pairs={{0,16},{4,20},{8,24},{12,28},{16,0},{20,4},{24,8},{28,12},{1,17},{... | collective-permute-start | bytes 921608 | tf_op jit(solution)/shard_map/ppermute | solution.py:871
  666.6 24.6 %collective-permute-start.16 = (bf16[320,480]{1,0:T(8,128)(2,1)}, bf16[320,480]{1,0:T(8,128)(2,1)}, u32[]{:S(2)}, u32[]{:S(2)}) collective-permute-start(bf16[320,480]{1,0:T(8,128)(2,1)} %convolution_convert_fusion.19), channel_id=1, source_target_pairs={{0,16},{4,20},{8,24},{12,28},{16,0},{20,4},{24,8},{28,12},{1,17},{... | collective-permute-start | bytes 921608 | tf_op jit(solution)/shard_map/ppermute | solution.py:871
  688.5 6.7 collective-permute-start.19
  691.3 6.5 collective-permute-start.22
  695.1 21.6 %collective-permute-start.18 = (bf16[320,480]{1,0:T(8,128)(2,1)}, bf16[320,480]{1,0:T(8,128)(2,1)S(1)}, u32[]{:S(2)}, u32[]{:S(2)}) collective-permute-start(bf16[320,480]{1,0:T(8,128)(2,1)} %convolution_convert_fusion.18), channel_id=1, source_target_pairs={{0,8},{4,12},{8,0},{12,4},{16,24},{20,28},{24,16},{28,20},{1,9},{5... | collective-permute-start | bytes 921608 | tf_op jit(solution)/shard_map/ppermute | solution.py:868
  697.8 7.5 collective-permute-start.14
  699.6 13.6 %collective-permute-start.17 = (bf16[320,480]{1,0:T(8,128)(2,1)S(1)}, bf16[320,480]{1,0:T(8,128)(2,1)S(1)}, u32[]{:S(2)}, u32[]{:S(2)}) collective-permute-start(bf16[320,480]{1,0:T(8,128)(2,1)S(1)} %add_convert_fusion.10), channel_id=1, source_target_pairs={{0,8},{4,12},{8,0},{12,4},{16,24},{20,28},{24,16},{28,20},{1,9},{5... | collective-permute-start | bytes 921608 | tf_op jit(solution)/shard_map/ppermute | solution.py:868
  704.1 17.6 %collective-permute-start.21 = (bf16[320,480]{1,0:T(8,128)(2,1)S(1)}, bf16[320,480]{1,0:T(8,128)(2,1)S(1)}, u32[]{:S(2)}, u32[]{:S(2)}) collective-permute-start(bf16[320,480]{1,0:T(8,128)(2,1)S(1)} %convolution_convert_fusion.16), channel_id=1, source_target_pairs={{0,16},{4,20},{8,24},{12,28},{16,0},{20,4},{24,8},{28,12},{1,17},{... | collective-permute-start | bytes 921608 | tf_op jit(solution)/shard_map/ppermute | solution.py:871
  705.3 13.9 %collective-permute-start.20 = (bf16[320,480]{1,0:T(8,128)(2,1)S(1)}, bf16[320,480]{1,0:T(8,128)(2,1)S(1)}, u32[]{:S(2)}, u32[]{:S(2)}) collective-permute-start(bf16[320,480]{1,0:T(8,128)(2,1)S(1)} %add_convert_fusion.8), channel_id=1, source_target_pairs={{0,16},{4,20},{8,24},{12,28},{16,0},{20,4},{24,8},{28,12},{1,17},{... | collective-permute-start | bytes 921608 | tf_op jit(solution)/shard_map/ppermute | solution.py:871
  706.8 27.2 %collective-permute-start.5 = (bf16[768,1280]{1,0:T(8,128)(2,1)S(1)}, bf16[768,1280]{1,0:T(8,128)(2,1)S(1)}, u32[]{:S(2)}, u32[]{:S(2)}) collective-permute-start(bf16[768,1280]{1,0:T(8,128)(2,1)S(1)} %copy-done.55), channel_id=1, source_target_pairs={{0,4},{4,0},{8,12},{12,8},{16,20},{20,16},{24,28},{28,24},{1,5},{5... | collective-permute-start | bytes 5898248 | tf_op jit(solution)/shard_map/ppermute | solution.py:865
  713.1 10.4 %collective-permute-start.23 = (bf16[320,480]{1,0:T(8,128)(2,1)S(1)}, bf16[320,480]{1,0:T(8,128)(2,1)S(1)}, u32[]{:S(2)}, u32[]{:S(2)}) collective-permute-start(bf16[320,480]{1,0:T(8,128)(2,1)S(1)} %add_convert_fusion.6), channel_id=1, source_target_pairs={{0,8},{4,12},{8,0},{12,4},{16,24},{20,28},{24,16},{28,20},{1,9},{5... | collective-permute-start | bytes 921608 | tf_op jit(solution)/shard_map/ppermute | solution.py:868
  716.7 55.7 %collective-permute-start.49 = (f32[160,640]{1,0:T(8,128)}, f32[160,640]{1,0:T(8,128)}, u32[]{:S(2)}, u32[]{:S(2)}) collective-permute-start(f32[160,640]{1,0:T(8,128)} %get-tuple-element.105), channel_id=1, source_target_pairs={{0,4},{4,0},{8,12},{12,8},{16,20},{20,16},{24,28},{28,24},{1,5},{5... | collective-permute-start | bytes 1228808 | tf_op jit(solution)/shard_map/ppermute | solution.py:865
  719.2 10.4 %collective-permute-start.28 = (bf16[320,640]{1,0:T(8,128)(2,1)S(1)}, bf16[320,640]{1,0:T(8,128)(2,1)S(1)}, u32[]{:S(2)}, u32[]{:S(2)}) collective-permute-start(bf16[320,640]{1,0:T(8,128)(2,1)S(1)} %copy-done.59), channel_id=1, source_target_pairs={{0,8},{4,12},{8,0},{12,4},{16,24},{20,28},{24,16},{28,20},{1,9},{5... | collective-permute-start | bytes 1228808 | tf_op jit(solution)/shard_map/ppermute | solution.py:868
  721.7 8.4 %collective-permute-start.30 = (bf16[320,640]{1,0:T(8,128)(2,1)S(1)}, bf16[320,640]{1,0:T(8,128)(2,1)S(1)}, u32[]{:S(2)}, u32[]{:S(2)}) collective-permute-start(bf16[320,640]{1,0:T(8,128)(2,1)S(1)} %fusion.63), channel_id=1, source_target_pairs={{0,16},{4,20},{8,24},{12,28},{16,0},{20,4},{24,8},{28,12},{1,17},{... | collective-permute-start | bytes 1228808 | tf_op jit(solution)/shard_map/ppermute | solution.py:871
  724.9 22.1 %collective-permute-start.24 = (bf16[320,480]{1,0:T(8,128)(2,1)}, bf16[320,480]{1,0:T(8,128)(2,1)S(1)}, u32[]{:S(2)}, u32[]{:S(2)}) collective-permute-start(bf16[320,480]{1,0:T(8,128)(2,1)} %get-tuple-element.95), channel_id=1, source_target_pairs={{0,3},{1,0},{2,1},{3,2},{4,7},{5,4},{6,5},{7,6},{8,11},{9,8},{10,9... | collective-permute-start | bytes 921608 | tf_op jit(solution)/shard_map/ppermute | solution.py:874
  729.6 27.7 %collective-permute-start.25 = (bf16[320,480]{1,0:T(8,128)(2,1)}, bf16[320,480]{1,0:T(8,128)(2,1)}, u32[]{:S(2)}, u32[]{:S(2)}) collective-permute-start(bf16[320,480]{1,0:T(8,128)(2,1)} %get-tuple-element.97), channel_id=1, source_target_pairs={{0,2},{1,3},{2,0},{3,1},{4,6},{5,7},{6,4},{7,5},{8,10},{9,11},{10,... | collective-permute-start | bytes 921608 | tf_op jit(solution)/shard_map/ppermute | solution.py:874
  730.1 27.2 %collective-permute-start.26 = (bf16[320,480]{1,0:T(8,128)(2,1)S(1)}, bf16[320,480]{1,0:T(8,128)(2,1)}, u32[]{:S(2)}, u32[]{:S(2)}) collective-permute-start(bf16[320,480]{1,0:T(8,128)(2,1)S(1)} %get-tuple-element.96), channel_id=1, source_target_pairs={{0,1},{1,2},{2,3},{3,0},{4,5},{5,6},{6,7},{7,4},{8,9},{9,10},{10,1... | collective-permute-start | bytes 921608 | tf_op jit(solution)/shard_map/ppermute | solution.py:874
  735.3 30.2 %collective-permute-start.31 = (bf16[320,160]{1,0:T(8,128)(2,1)}, bf16[320,160]{1,0:T(8,128)(2,1)S(1)}, u32[]{:S(2)}, u32[]{:S(2)}) collective-permute-start(bf16[320,160]{1,0:T(8,128)(2,1)} %get-tuple-element.110), channel_id=1, source_target_pairs={{0,3},{1,0},{2,1},{3,2},{4,7},{5,4},{6,5},{7,6},{8,11},{9,8},{10,9... | collective-permute-start | bytes 307208 | tf_op jit(solution)/shard_map/ppermute | solution.py:874
  747.0 19.0 %collective-permute-start.32 = (bf16[320,160]{1,0:T(8,128)(2,1)S(1)}, bf16[320,160]{1,0:T(8,128)(2,1)S(1)}, u32[]{:S(2)}, u32[]{:S(2)}) collective-permute-start(bf16[320,160]{1,0:T(8,128)(2,1)S(1)} %copy-done.49), channel_id=1, source_target_pairs={{0,2},{1,3},{2,0},{3,1},{4,6},{5,7},{6,4},{7,5},{8,10},{9,11},{10,... | collective-permute-start | bytes 307208 | tf_op jit(solution)/shard_map/ppermute | solution.py:874
  757.3 8.7 %collective-permute-start.33 = (bf16[320,160]{1,0:T(8,128)(2,1)S(1)}, bf16[320,160]{1,0:T(8,128)(2,1)S(1)}, u32[]{:S(2)}, u32[]{:S(2)}) collective-permute-start(bf16[320,160]{1,0:T(8,128)(2,1)S(1)} %get-tuple-element.111), channel_id=1, source_target_pairs={{0,1},{1,2},{2,3},{3,0},{4,5},{5,6},{6,7},{7,4},{8,9},{9,10},{10,1... | collective-permute-start | bytes 307208 | tf_op jit(solution)/shard_map/ppermute | solution.py:874
  757.3 37.2 %collective-permute-start.6 = (bf16[768,1280]{1,0:T(8,128)(2,1)S(1)}, bf16[768,1280]{1,0:T(8,128)(2,1)}, u32[]{:S(2)}, u32[]{:S(2)}) collective-permute-start(bf16[768,1280]{1,0:T(8,128)(2,1)S(1)} %fusion.9), channel_id=1, source_target_pairs={{1,4},{3,6},{4,1},{6,3},{9,12},{11,14},{12,9},{14,11},{17,20},{19,... | collective-permute-start | bytes 5898248 | tf_op jit(solution)/shard_map/ppermute | solution.py:880
  765.5 13.2 %collective-permute-start.27 = (f32[160,480]{1,0:T(8,128)S(1)}, f32[160,480]{1,0:T(8,128)}, u32[]{:S(2)}, u32[]{:S(2)}) collective-permute-start(f32[160,480]{1,0:T(8,128)S(1)} %get-tuple-element.117), channel_id=1, source_target_pairs={{0,4},{4,0},{8,12},{12,8},{16,20},{20,16},{24,28},{28,24},{1,5},{5... | collective-permute-start | bytes 921608 | tf_op jit(solution)/shard_map/ppermute | solution.py:865
  766.1 4.9 collective-permute-start.7
  770.2 7.2 collective-permute-start.34
  771.0 4.6 collective-permute-start.8
  775.6 3.1 collective-permute-start.9
  778.7 7.5 collective-permute-start.10
  786.1 6.5 collective-permute-start.11
  (71 other events, 676.0 us)

commit v3 on v2

--- a/solution.py
+++ b/solution.py
@@ -222,7 +222,7 @@
     scaling,
     attn_shard, up_shard, down_shard, tokens, cotangent, mask_in, bias_in,
     gain_one, shift_one, gain_two, shift_two, bias_out,
-    w_attn_out, w_up_out, w_down, tokens_out, cot_out, mask_out, first_out, second_out, joined_out,
+    w_attn_out, w_up_out, w_down, tokens_out, grad_out, mask_out, first_out, second_out, joined_out,
     heads_out, totals_out, middle_out, hidden_out, slope_out,
     w_attn, w_up, tok, first, second, joined, heads, middle, send_rows, got_rows, hidden, slope,
     mask, totals, bias, send_sem, recv_sem, local_sem,
@@ -329,8 +329,10 @@
     mask_copy = pltpu.make_async_copy(mask_in, mask, local_sem.at[4])
     clip_tok = remote(tokens, tok, 51, to_clip)
     clip_mask = remote(mask_in, mask, 52, to_clip)
-    cot_copy = pltpu.make_async_copy(cotangent, cot_out, local_sem.at[5])
-    clip_cot = remote(cotangent, cot_out, 59, to_clip)
+    there = grad_out.at[pl.ds(pl.multiple_of((1 - core) * half, 256), half)]
+    here = grad_out.at[pl.ds(pl.multiple_of(core * half, 256), half)]
+    cot_copy = pltpu.make_async_copy(cotangent, here, local_sem.at[5])
+    clip_cot = remote(cotangent, there, 59, to_clip)
 
     @pl.when(moves)
     def _():
@@ -405,7 +407,7 @@
         def step_rows(step, _):
             rows = pl.ds(pl.multiple_of(step * half, half), half)
             product = dot_nn(first[rows, :], w_attn[:, columns]) + bias[turn[k], 0:1, :480]
-            joined[k, rows, :] = product.astype(BF16)
+            joined[k, rows, :480] = product.astype(BF16)
             return 0
 
         lax.fori_loop(0, 2, step_rows, 0)
@@ -414,7 +416,7 @@
     def attention(k, part):
         def step_rows(step, _):
             rows = pl.ds(pl.multiple_of(step * 256, 256), 256)
-            queries = joined[k, rows, :]
+            queries = joined[k, rows, :160]
             mixes, logs = [jnp.zeros((256, 96), F32)], []
             for head in range(2):
                 low = head * HDIM
@@ -548,17 +550,20 @@
     lift(2)
     lift(3)
     put(w_up, w_up_out, 29)
-    for k in range(TURNS):
-        complete(2, k)
 
     @pl.when(moves)
     def _():
-        clip_cot.wait()
+        clip_cot.wait_send()
+        arrived(here, 59)
 
     @pl.when(jnp.logical_not(moves))
     def _():
         cot_copy.wait()
 
+    send(here, here, 60, to_core)
+    for k in range(TURNS):
+        complete(2, k)
+    arrived(there, 60)
     for copy in outs + waits[0] + waits[1]:
         copy.wait()
     for copy in sent:
@@ -574,9 +579,9 @@
     vmem = pl.BlockSpec(memory_space=pltpu.VMEM)
     wide = (features, TURNS * SPAN)
     shapes = [
-        (wide, BF16), (wide, BF16), (wide, BF16), ((half, features), BF16), ((half, features), BF16),
+        (wide, BF16), (wide, BF16), (wide, BF16), ((half, features), BF16), ((count, features), BF16),
         ((8, count), F32), ((count, features), BF16), ((count, features), BF16),
-        ((TURNS, count, 480), BF16), ((TURNS, count, 256), BF16), ((TURNS, 8, count), F32),
+        ((TURNS, count, SPAN), BF16), ((TURNS, count, 256), BF16), ((TURNS, 8, count), F32),
         ((half, features), F32), ((count, TURNS * SPAN), BF16), ((count, TURNS * SPAN), BF16),
     ]
     return pl.pallas_call(
@@ -590,7 +595,7 @@
             pltpu.VMEM((half, features), BF16),
             pltpu.VMEM((count, features), BF16),
             pltpu.VMEM((count, features), BF16),
-            pltpu.VMEM((TURNS, count, 480), BF16),
+            pltpu.VMEM((TURNS, count, SPAN), BF16),
             pltpu.VMEM((TURNS, count, 256), BF16),
             pltpu.VMEM((half, features), F32),
             pltpu.VMEM((half, features), BF16),
@@ -612,6 +617,563 @@
         ),
         name="forward_pass",
     )(*shards, tokens, cotangent, mask, bias, gain_one, shift_one, gain_two, shift_two, bias_out)
+
+
+def backward_kernel(
+    scaling,
+    w_attn_in, w_up_in, w_down_in, tok_in, grad_in, first_in, second_in, joined_in, heads_in, middle_in,
+    hidden_in, slope_in, totals_in, key_mask, gain_one, gain_two,
+    tokens_out, down_out, up_out, attn_out, sums_out, pre_out,
+    weight, grad, left, wide, right, grad_heads, totals, middle, send_rows, got_rows, key_sum, value_sum,
+    product, near_got, far_got, turn_got, line_got, line_own, final, final_got, sums, sums_got,
+    send_sem, recv_sem, local_sem, credit,
+):
+    dp, z = lax.axis_index("dp"), lax.axis_index("tensor")
+    core, plane = lax.rem(dp, 2), lax.div(dp, 2)
+    x_bit, y_bit = lax.rem(plane, 2), lax.div(plane, 2)
+    half = middle.shape[0]
+    count = 2 * half
+    features = middle.shape[1]
+    to_x = (y_bit * 4 + (1 - x_bit) * 2 + core, z)
+    to_y = ((1 - y_bit) * 4 + x_bit * 2 + core, z)
+    to_core = (plane * 2 + 1 - core, z)
+    to_clip = (plane * 2 + 1 - core, z + 1 - 2 * lax.rem(z, 2))
+    to_z = [(dp, lax.rem(z + k, TURNS)) for k in range(TURNS)]
+    to_z_pair = (dp, z + 1 - 2 * lax.rem(z, 2))
+    moves = core != lax.rem(z, 2)
+    plane_x = y_bit * 2 + 1 - x_bit
+    plane_y = (1 - y_bit) * 2 + x_bit
+    plane_xy = (1 - y_bit) * 2 + 1 - x_bit
+    turn = [lax.rem(z + TURNS - k, TURNS) for k in range(TURNS)]
+    base = pl.multiple_of(core * half, 256)
+    other = pl.multiple_of((1 - core) * half, 256)
+    own_rows, other_rows = pl.ds(base, half), pl.ds(other, half)
+
+    barrier = pltpu.get_barrier_semaphore()
+    partners = [to_x, to_y, to_core, to_clip] + to_z[1:]
+    for partner in partners:
+        pl.semaphore_signal(barrier, inc=1, device_id=partner, device_id_type=pl.DeviceIdType.MESH)
+    pl.semaphore_wait(barrier, len(partners))
+
+    def remote(source, target, sem, device):
+        return pltpu.make_async_remote_copy(
+            src_ref=source,
+            dst_ref=target,
+            send_sem=send_sem.at[sem],
+            recv_sem=recv_sem.at[sem],
+            device_id=device,
+            device_id_type=pl.DeviceIdType.MESH,
+        )
+
+    def send(source, target, sem, device):
+        copy = remote(source, target, sem, device)
+        copy.start()
+        return copy
+
+    def arrived(target, sem):
+        remote(target, target, sem, to_core).wait_recv()
+
+    def tell(index, device):
+        pl.semaphore_signal(
+            credit.at[index], inc=1, device_id=device, device_id_type=pl.DeviceIdType.MESH
+        )
+
+    def local(source, target, sem):
+        copy = pltpu.make_async_copy(source, target, local_sem.at[sem])
+        copy.start()
+        return copy
+
+    def columns(k):
+        return pl.ds(pl.multiple_of(turn[k] * SPAN, 128), SPAN)
+
+    def load_right(source, k, slot):
+        return local(source.at[:, columns(k)], right.at[slot], slot)
+
+    grad_load = local(grad_in, grad, 2)
+    right_loads = [load_right(hidden_in, 0, 0), None]
+    weight_loads, slope_loads = [], []
+    for k in range(TURNS):
+        weight_loads.append(local(w_down_in.at[:, columns(k)], weight.at[:, columns(k)], 3 + k))
+        slope_loads.append(local(slope_in.at[:, columns(k)], wide.at[:, columns(k)], 7 + k))
+    right_loads[1] = load_right(hidden_in, 1, 1)
+    left_load = local(second_in, left, 11)
+    middle_load = local(middle_in, middle, 12)
+    totals_loads = [local(totals_in.at[turn[k]], totals.at[k], 21 + k) for k in range(TURNS)]
+    sums[...] = jnp.zeros_like(sums)
+
+    in_flight = [[] for _ in range(TURNS)]
+
+    def place(k, where):
+        return product.at[k, pl.ds(pl.multiple_of(where * UNIT, 16), UNIT)]
+
+    def ready(k):
+        for copy in in_flight[k]:
+            copy.wait_send()
+        in_flight[k] = []
+
+    def produce(k, factor, chunk):
+        ready(k)
+
+        def step_part(part, _):
+            rows = pl.ds(pl.multiple_of(part * 640, 640), 640)
+            product[k, rows, :] = dot_tn(factor[:, rows], chunk[...]).astype(BF16)
+            return 0
+
+        lax.fori_loop(0, 2, step_part, 0)
+
+    def ways(k):
+        if k % 2 == 0:
+            return to_x, to_y, plane_x, plane_y
+        return to_y, to_x, plane_y, plane_x
+
+    def stage_one(array, k):
+        go, _, near, _ = ways(k)
+        if array > 0:
+            pl.semaphore_wait(credit.at[k], 1)
+        sem = 16 * array + k
+        in_flight[k].append(send(place(k, plane_xy), far_got.at[k], sem + 4, go))
+        in_flight[k].append(send(place(k, near), near_got.at[k], sem, go))
+
+    def add_to(target, sources):
+        total = target[...].astype(F32)
+        for source in sources:
+            total = total + source[...].astype(F32)
+        return total
+
+    def stage_two(array, k):
+        go, follow, _, far = ways(k)
+        sem = 16 * array + k
+        arrived(far_got.at[k], sem + 4)
+        target = place(k, far)
+        target[...] = add_to(target, [far_got.at[k]]).astype(BF16)
+        if array > 0:
+            pl.semaphore_wait(credit.at[4 + k], 1)
+        in_flight[k].append(send(target, turn_got.at[k], sem + 8, follow))
+        arrived(near_got.at[k], sem)
+        target = place(k, plane)
+        target[...] = add_to(target, [near_got.at[k]]).astype(BF16)
+        if array < 2:
+            tell(k, go)
+
+    def stage_three(array, k):
+        _, follow, _, _ = ways(k)
+        sem = 16 * array + k
+        arrived(turn_got.at[k], sem + 8)
+        target = place(k, plane)
+        total = add_to(target, [turn_got.at[k]]).astype(BF16)
+        if array < 2:
+            tell(4 + k, follow)
+        if k == 0:
+            line_own[...] = total
+            return
+        target[...] = total
+        if array > 0:
+            pl.semaphore_wait(credit.at[8 + k], 1)
+        in_flight[k].append(send(target, line_got.at[k], sem + 12, to_z[(TURNS - k) % TURNS]))
+
+    results = [down_out, up_out, attn_out]
+    final_moves = []
+
+    def final_one(array):
+        for copy in final_moves:
+            copy()
+        final_moves.clear()
+        for k in range(1, TURNS):
+            arrived(line_got.at[k], 16 * array + k + 12)
+        final[...] = add_to(line_own, [line_got.at[k] for k in range(1, TURNS)])
+        if array < 2:
+            for k in range(1, TURNS):
+                tell(8 + k, to_z[k])
+        rows = UNIT // 2
+        keep = pl.ds(pl.multiple_of(core * rows, 16), rows)
+        give = pl.ds(pl.multiple_of((1 - core) * rows, 16), rows)
+        final_moves.append(send(final.at[give], final_got.at[array], 52 + array, to_core).wait_send)
+        target = results[array].at[:, pl.ds(pl.multiple_of(core * SPAN, 128), SPAN)]
+        final_moves.append(local(final.at[keep], target, 13).wait)
+
+    last_moves = []
+
+    def final_two(array):
+        arrived(final_got.at[array], 52 + array)
+        target = results[array].at[:, pl.ds(pl.multiple_of((1 - core) * SPAN, 128), SPAN)]
+        last_moves.append(local(final_got.at[array], target, 14 + array).wait)
+
+    grad_load.wait()
+    right_loads[0].wait()
+    produce(0, grad, right.at[0])
+    stage_one(0, 0)
+    right_loads[0] = load_right(hidden_in, 2, 0)
+    pre_puts = []
+
+    def grad_pre(k):
+        weight_loads[k].wait()
+        slope_loads[k].wait()
+
+        def step_rows(step, total):
+            rows = pl.ds(pl.multiple_of(step * 512, 512), 512)
+            value = dot_nn(grad[rows, :], weight[:, columns(k)])
+            value = value * wide[rows, columns(k)].astype(F32)
+            wide[rows, columns(k)] = value.astype(BF16)
+            return total + jnp.sum(value, 0, keepdims=True)
+
+        total = lax.fori_loop(0, count // 512, step_rows, jnp.zeros((1, SPAN), F32))
+        sums[8 + 2 * turn[k] + core, :, :SPAN] = total
+        pre_puts.append(local(wide.at[:, columns(k)], pre_out.at[:, columns(k)], 17 + k))
+        weight_loads[k] = local(w_up_in.at[:, columns(k)], weight.at[:, columns(k)], 3 + k)
+
+    grad_pre(0)
+    grad_pre(1)
+    right_loads[1].wait()
+    produce(1, grad, right.at[1])
+    stage_one(0, 1)
+    right_loads[1] = load_right(hidden_in, 3, 1)
+    grad_pre(2)
+    grad_pre(3)
+    for load in weight_loads:
+        load.wait()
+
+    def second_part(rows):
+        return dot_nt(wide[rows, :], weight[...])
+
+    def second_other(step, _):
+        rows = pl.ds(pl.multiple_of(other + step * 256, 256), 256)
+        send_rows[pl.ds(pl.multiple_of(step * 256, 256), 256), :] = second_part(rows).astype(BF16)
+        return 0
+
+    lax.fori_loop(0, half // 256, second_other, 0)
+    rows_sent = send(send_rows, got_rows, 48, to_core)
+    stage_two(0, 0)
+    right_loads[0].wait()
+    produce(2, grad, right.at[0])
+    stage_one(0, 2)
+    right_loads[1].wait()
+    produce(3, grad, right.at[1])
+    stage_one(0, 3)
+    tell(12, to_core)
+    middle_load.wait()
+    arrived(got_rows, 48)
+
+    def norm_back_rows(values, gain, above):
+        center = values - jnp.mean(values, -1, keepdims=True)
+        scale = lax.rsqrt(jnp.mean(center * center, -1, keepdims=True) + EPS)
+        normed = center * scale
+        scaled = above * gain
+        back = scaled - jnp.mean(scaled, -1, keepdims=True)
+        back = (back - normed * jnp.mean(scaled * normed, -1, keepdims=True)) * scale
+        return back, jnp.sum(above * normed, 0, keepdims=True), jnp.sum(above, 0, keepdims=True)
+
+    def norm_two(step, total):
+        low = pl.ds(pl.multiple_of(step * 256, 256), 256)
+        rows = pl.ds(pl.multiple_of(base + step * 256, 256), 256)
+        above = second_part(rows) + got_rows[low, :].astype(F32)
+        back, by_gain, by_shift = norm_back_rows(middle[low, :], gain_two[...], above)
+        out_grad = grad[rows, :].astype(F32)
+        below = out_grad + back
+        middle[low, :] = below
+        grad[rows, :] = below.astype(BF16)
+        by_down, by_out = jnp.sum(out_grad, 0, keepdims=True), jnp.sum(below, 0, keepdims=True)
+        return (total[0] + by_down, total[1] + by_out, total[2] + by_gain, total[3] + by_shift)
+
+    zero = jnp.zeros((1, features), F32)
+    parts = lax.fori_loop(0, half // 256, norm_two, (zero,) * 4)
+    for i in range(4):
+        sums[i, :, :] = parts[i]
+    pl.semaphore_wait(credit.at[12], 1)
+    branch_sent = send(grad.at[own_rows], grad.at[own_rows], 49, to_core)
+    for copy in pre_puts:
+        copy.wait()
+    weight_load = local(w_attn_in, weight, 3)
+    joined_loads = [
+        local(joined_in.at[turn[k]], wide.at[:, k * SPAN : (k + 1) * SPAN], 7 + k) for k in range(TURNS)
+    ]
+    pre_loads = [local(pre_out.at[:, columns(k)], right.at[k], k) for k in range(2)]
+    stage_two(0, 1)
+    stage_three(0, 0)
+    weight_load.wait()
+    arrived(grad.at[other_rows], 49)
+
+    def heads_back(k):
+        slab = pl.ds(pl.multiple_of(turn[k] * SPAN + 384, 128), 256)
+
+        def step_rows(step, _):
+            rows = pl.ds(pl.multiple_of(step * 512, 512), 512)
+            grad_heads[rows, :] = dot_nn(grad[rows, :], weight[:, slab]).astype(BF16)
+            return 0
+
+        lax.fori_loop(0, count // 512, step_rows, 0)
+        joined_loads[k].wait()
+        totals_loads[k].wait()
+        key_sum[...] = jnp.zeros_like(key_sum)
+        value_sum[...] = jnp.zeros_like(value_sum)
+
+    one_lane = (lax.broadcasted_iota(jnp.int32, (256, 48), 1) == 0).astype(F32).astype(BF16)
+
+    def attention(k, part, total):
+        low = k * SPAN
+
+        def step_rows(step, total):
+            rows = pl.ds(pl.multiple_of(step * 256, 256), 256)
+            queries = wide[rows, low : low + 160]
+            grads = grad_heads[rows, :]
+            outs = []
+            for head in range(2):
+                at = head * HDIM
+                query = queries[:, at : at + HDIM]
+                above = grads[:, 96 + at : 96 + at + HDIM]
+                key = wide[:, low + 160 + at : low + 160 + at + HDIM]
+                value = wide[:, low + 320 + at : low + 320 + at + HDIM]
+                scores = dot_nt(
+                    jnp.concatenate([key, key_mask[:, :48]], -1),
+                    jnp.concatenate([query, one_lane], -1),
+                )
+                probs = jnp.exp2(
+                    scores * (scaling * LOG2E) - totals[k, head : head + 1, rows]
+                )
+                grad_probs = dot_nt(value, above)
+                shared = jnp.sum(probs * grad_probs, 0, keepdims=True)
+                grad_scores = (probs * (grad_probs - shared)).astype(BF16)
+                value_sum[head, :, :HDIM] += dot_nn(probs.astype(BF16), above)
+                key_sum[head, :, :HDIM] += dot_nn(grad_scores, query)
+                outs.append(dot_tn(grad_scores, key) * scaling)
+            joined = jnp.concatenate(outs, -1)
+            wide[rows, low : low + 160] = joined.astype(BF16)
+            return total + jnp.sum(joined, 0, keepdims=True)
+
+        return lax.fori_loop(2 * part, 2 * part + 2, step_rows, total)
+
+    def attention_end(k, total):
+        low = k * SPAN
+
+        def step_rows(step, value_total):
+            rows = pl.ds(pl.multiple_of(step * 256, 256), 256)
+            keys = [key_sum[head, rows, :HDIM] * scaling for head in range(2)]
+            values = [value_sum[head, rows, :HDIM] for head in range(2)]
+            joined = jnp.concatenate(keys + values, -1)
+            wide[rows, low + 160 : low + 480] = joined.astype(BF16)
+            return value_total + jnp.sum(joined[:, 160:], 0, keepdims=True)
+
+        value_total = lax.fori_loop(0, count // 256, step_rows, jnp.zeros((1, 160), F32))
+        sums[16 + 2 * turn[k] + core, :, :160] = total
+        sums[16 + 2 * turn[k] + core, :, 160:320] = value_total
+
+    def produce_attn(k):
+        heads_load = local(heads_in.at[turn[k]], grad_heads, 4)
+        ready(k)
+        heads_load.wait()
+
+        def step_part(part, _):
+            rows = pl.ds(pl.multiple_of(part * 640, 640), 640)
+            by_first = dot_tn(left[:, rows], wide[:, k * SPAN : k * SPAN + 480])
+            by_branch = dot_tn(grad[:, rows], grad_heads[:, 96:256])
+            product[k, rows, :] = jnp.concatenate([by_first, by_branch], -1).astype(BF16)
+            return 0
+
+        lax.fori_loop(0, 2, step_part, 0)
+
+    start = jnp.zeros((1, 160), F32)
+    left_load.wait()
+
+    def up_chunk(k):
+        slot = k % 2
+        pre_loads[slot].wait()
+        produce(k, left, right.at[slot])
+        stage_one(1, k)
+        if k < 2:
+            pre_loads[slot] = local(pre_out.at[:, columns(k + 2)], right.at[slot], slot)
+
+    heads_back(0)
+    up_chunk(0)
+    total = attention(0, 0, start)
+    stage_two(0, 2)
+    stage_three(0, 1)
+    total = attention(0, 1, total)
+    stage_two(0, 3)
+    up_chunk(1)
+    total = attention(0, 2, total)
+    attention_end(0, total)
+    stage_three(0, 2)
+    stage_two(1, 0)
+    heads_back(1)
+    total = attention(1, 0, start)
+    stage_three(0, 3)
+    up_chunk(2)
+    total = attention(1, 1, total)
+    stage_two(1, 1)
+    final_one(0)
+    up_chunk(3)
+    left_load = local(first_in, left, 11)
+    total = attention(1, 2, total)
+    attention_end(1, total)
+    final_two(0)
+    stage_two(1, 2)
+    stage_three(1, 0)
+    stage_three(1, 1)
+    left_load.wait()
+    produce_attn(0)
+    stage_one(2, 0)
+    produce_attn(1)
+    stage_one(2, 1)
+    heads_back(2)
+    stage_two(1, 3)
+    total = attention(2, 0, start)
+    stage_three(1, 2)
+    total = attention(2, 1, total)
+    stage_two(2, 0)
+    stage_three(1, 3)
+    total = attention(2, 2, total)
+    attention_end(2, total)
+    stage_two(2, 1)
+    produce_attn(2)
+    stage_one(2, 2)
+    final_one(1)
+    heads_back(3)
+    total = attention(3, 0, start)
+    stage_three(2, 0)
+    total = attention(3, 1, total)
+    stage_three(2, 1)
+    final_two(1)
+    total = attention(3, 2, total)
+    attention_end(3, total)
+    produce_attn(3)
+    stage_one(2, 3)
+    branch_sent.wait_send()
+    tok_load = local(tok_in, grad.at[0:half], 2)
+    stage_two(2, 2)
+
+    def first_part(rows):
+        total = None
+        for k in range(TURNS):
+            slab = pl.ds(pl.multiple_of(turn[k] * SPAN, 128), 480)
+            part = dot_nt(wide[rows, k * SPAN : k * SPAN + 480], weight[:, slab])
+            total = part if total is None else total + part
+        return total
+
+    rows_sent.wait_send()
+
+    def first_other(step, _):
+        rows = pl.ds(pl.multiple_of(other + step * 256, 256), 256)
+        send_rows[pl.ds(pl.multiple_of(step * 256, 256), 256), :] = first_part(rows).astype(BF16)
+        return 0
+
+    lax.fori_loop(0, half // 256, first_other, 0)
+    rows_sent = send(send_rows, got_rows, 50, to_core)
+    stage_three(2, 2)
+    tok_load.wait()
+    arrived(got_rows, 50)
+
+    def norm_one(step, total):
+        low = pl.ds(pl.multiple_of(step * 256, 256), 256)
+        rows = pl.ds(pl.multiple_of(base + step * 256, 256), 256)
+        above = first_part(rows) + got_rows[low, :].astype(F32)
+        back, by_gain, by_shift = norm_back_rows(grad[low, :].astype(F32), gain_one[...], above)
+        below = middle[low, :] + back
+        grad[pl.ds(pl.multiple_of(half + step * 256, 256), 256), :] = below.astype(BF16)
+        return (total[0] + by_gain, total[1] + by_shift)
+
+    parts = lax.fori_loop(0, half // 256, norm_one, (zero,) * 2)
+    for i in range(2):
+        sums[4 + i, :, :] = parts[i]
+    tokens_away = remote(grad.at[half:count], tokens_out, 51, to_clip)
+    tokens_here = pltpu.make_async_copy(grad.at[half:count], tokens_out, local_sem.at[2])
+
+    @pl.when(moves)
+    def _():
+        tokens_away.start()
+
+    @pl.when(jnp.logical_not(moves))
+    def _():
+        tokens_here.start()
+
+    def hop(index, device):
+        copy = send(sums, sums_got.at[index], 55 + index, device)
+        copy.wait_send()
+        arrived(sums_got.at[index], 55 + index)
+        sums[...] = sums[...] + sums_got[index]
+
+    hop(0, to_core)
+    hop(1, to_x)
+    stage_two(2, 3)
+    hop(2, to_y)
+    hop(3, to_z_pair)
+    hop(4, to_z[2])
+    sums_put = local(sums, sums_out, 5)
+    stage_three(2, 3)
+    final_one(2)
+    final_two(2)
+
+    @pl.when(moves)
+    def _():
+        tokens_away.wait()
+
+    @pl.when(jnp.logical_not(moves))
+    def _():
+        tokens_here.wait()
+
+    sums_put.wait()
+    rows_sent.wait_send()
+    for wait in final_moves + last_moves:
+        wait()
+    for k in range(TURNS):
+        ready(k)
+
+
+def backward_pass(
+    w_attn, w_up, w_down, tok, grad, first, second, joined, heads, middle, hidden, slope, totals, key_mask,
+    gain_one, gain_two,
+):
+    half, features = tok.shape
+    count = 2 * half
+    any_space = pl.BlockSpec(memory_space=pl.ANY)
+    vmem = pl.BlockSpec(memory_space=pltpu.VMEM)
+    cols = TURNS * SPAN
+    shapes = [
+        ((half, features), BF16), ((UNIT // 2, 2 * SPAN), F32), ((UNIT // 2, 2 * SPAN), F32),
+        ((UNIT // 2, 2 * SPAN), F32), ((24, 1, features), F32), ((count, cols), BF16),
+    ]
+    return pl.pallas_call(
+        functools.partial(backward_kernel, HDIM ** (-0.5)),
+        in_specs=[any_space] * 13 + [vmem] * 3,
+        out_specs=[any_space] * len(shapes),
+        out_shape=[jax.ShapeDtypeStruct(shape, kind) for shape, kind in shapes],
+        scratch_shapes=[
+            pltpu.VMEM((features, cols), BF16),
+            pltpu.VMEM((count, features), BF16),
+            pltpu.VMEM((count, features), BF16),
+            pltpu.VMEM((count, cols), BF16),
+            pltpu.VMEM((2, count, SPAN), BF16),
+            pltpu.VMEM((count, 256), BF16),
+            pltpu.VMEM((TURNS, 8, count), F32),
+            pltpu.VMEM((half, features), F32),
+            pltpu.VMEM((half, features), BF16),
+            pltpu.VMEM((half, features), BF16),
+            pltpu.VMEM((2, count, 128), F32),
+            pltpu.VMEM((2, count, 128), F32),
+            pltpu.VMEM((TURNS, features, SPAN), BF16),
+            pltpu.VMEM((TURNS, UNIT, SPAN), BF16),
+            pltpu.VMEM((TURNS, UNIT, SPAN), BF16),
+            pltpu.VMEM((TURNS, UNIT, SPAN), BF16),
+            pltpu.VMEM((TURNS, UNIT, SPAN), BF16),
+            pltpu.VMEM((UNIT, SPAN), BF16),
+            pltpu.VMEM((UNIT, SPAN), F32),
+            pltpu.VMEM((3, UNIT // 2, SPAN), F32),
+            pltpu.VMEM((24, 1, features), F32),
+            pltpu.VMEM((5, 24, 1, features), F32),
+            pltpu.SemaphoreType.DMA((64,)),
+            pltpu.SemaphoreType.DMA((64,)),
+            pltpu.SemaphoreType.DMA((32,)),
+            pltpu.SemaphoreType.REGULAR((16,)),
+        ],
+        cost_estimate=pl.CostEstimate(
+            flops=4 * count * features * 6400, bytes_accessed=90_000_000, transcendentals=30_000_000
+        ),
+        compiler_params=pltpu.CompilerParams(
+            vmem_limit_bytes=60 << 20, collective_id=1, has_side_effects=True
+        ),
+        name="backward_pass",
+    )(
+        w_attn, w_up, w_down, tok, grad, first, second, joined, heads, middle, hidden, slope, totals,
+        key_mask, gain_one, gain_two,
+    )
 
 
 class Links:
@@ -835,7 +1397,6 @@
     core, plane = dp % 2, dp // 2
     half = tokens.shape[0]
     count = 2 * half
-    scaling = HDIM ** (-0.5)
     width, units = 160, SPAN
 
     def split(weight):
@@ -849,29 +1410,22 @@
     place = jnp.sum(jnp.where(jnp.arange(lengths.shape[0]) == z // 2, lengths, 0))
     mask = jnp.where(jnp.arange(count) < place, 0.0, -1e30).astype(F32)
     mask = jnp.broadcast_to(mask[None, :], (8, count))
+    valid = ((z % 2) * half + jnp.arange(half) < place).astype(BF16)
     small = [query_bias.reshape(2, width), jnp.zeros((2, width), F32), value_bias.reshape(2, width)]
     small = jnp.concatenate(small + [jnp.zeros((2, width), F32)], -1)
     small = jnp.stack([small, up_bias.reshape(2, units)], 1)
     small = jnp.pad(jnp.where(core == 0, small[0], small[1]), ((0, 6), (0, 0)))
     (
-        w_attn, w_up, w_down, tok, cot, mask, first, second, joined, heads, totals, middle, hidden, slope,
+        w_attn, w_up, w_down, tok, out_grad, mask, first, second, joined, heads, totals, middle, hidden,
+        slope,
     ) = forward_pass(
-        shards, tokens, cotangent, mask, small,
+        shards, tokens, cotangent * valid[:, None], mask, small,
         norm1_gain[None, :], norm1_shift[None, :], norm2_gain[None, :], norm2_shift[None, :],
         out_bias[None, :],
     )
 
     def pair(value):
         return lax.ppermute(value, "dp", [(i, i ^ 1) for i in range(8)])
-
-    def along_x(value):
-        return lax.ppermute(value, "dp", [(i, i ^ 2) for i in range(8)])
-
-    def along_y(value):
-        return lax.ppermute(value, "dp", [(i, i ^ 4) for i in range(8)])
-
-    def along_z(value, shift):
-        return lax.ppermute(value, "tensor", [(i, (i + shift) % 4) for i in range(4)])
 
     def move_rows(value):
         swaps = [
@@ -884,138 +1438,44 @@
         start = (core if part == 0 else 1 - core) * half
         return lax.dynamic_slice_in_dim(value, start, half, 0)
 
-    def both(value):
-        got = pair(value)
-        first_one = core == 0
-        return jnp.concatenate([jnp.where(first_one, value, got), jnp.where(first_one, got, value)])
-
-    def merged(partial_of):
-        got = pair(partial_of(1).astype(BF16))
-        return partial_of(0) + got.astype(F32)
-
-    def scatter(left, right, x_first, blocks):
-        def part(index):
-            columns = lax.dynamic_slice_in_dim(left, (plane ^ index) * UNIT, UNIT, 1)
-            return dot_tn(columns, right)
-
-        near, far = (1, 2) if x_first else (2, 1)
-        go, follow = (along_x, along_y) if x_first else (along_y, along_x)
-        sent_far = go(part(3).astype(BF16))
-        sent_near = go(part(near).astype(BF16))
-        second_part = (part(far) + sent_far.astype(F32)).astype(BF16)
-        first_part = part(0) + sent_near.astype(F32)
-        product = (first_part + follow(second_part).astype(F32)).astype(BF16)
-        size = product.shape[1] // blocks
-        return [product[:, i * size : (i + 1) * size] for i in range(blocks)]
-
-    def finish(blocks):
-        stacked = jnp.stack(blocks)
-        picked = [
-            lax.dynamic_index_in_dim(stacked, (z - k) % 4, 0, keepdims=False) for k in range(4)
-        ]
-        total = picked[0].astype(F32)
-        for k in range(1, 4):
-            total = total + along_z(picked[k], -k).astype(F32)
-        rows = UNIT // 2
-        first_one = core == 0
-        keep = jnp.where(first_one, total[:rows], total[rows:])
-        got = pair(jnp.where(first_one, total[rows:], total[:rows]))
-        return jnp.where(first_one, jnp.stack([keep, got], 1), jnp.stack([got, keep], 1))
-
-    def gradient(left, right):
-        cut = right.shape[1] // 2
-        return finish(
-            scatter(left, right[:, :cut], True, 2) + scatter(left, right[:, cut:], False, 2)
-        )
-
-    def total(value):
-        for bit in (1, 2, 4):
-            value = value + lax.ppermute(value, "dp", [(i, i ^ bit) for i in range(8)])
-        for bit in (1, 2):
-            value = value + lax.ppermute(value, "tensor", [(i, i ^ bit) for i in range(4)])
-        return value
-
-    def spread(pieces):
-        halves = (jnp.arange(2) == core)[None, :, None]
-        return jnp.where(halves, jnp.stack(pieces)[:, None, :], 0.0).reshape(-1)
-
-    source = tok.astype(F32)
-    valid = (part_of(mask[0], 0) == 0.0).astype(BF16)[:, None]
-    out_own = cot * valid
-    out_grad = both(out_own)
-    grad_down = gradient(out_grad, hidden)
-    down_out = merged(lambda part: dot_nt(part_of(hidden, part), w_down))
-    layer_out = move_rows((middle + down_out + down_bias).astype(BF16))
-    grad_pre = (dot_nn(out_grad, w_down) * slope.astype(F32)).astype(BF16)
-    grad_up = gradient(second, grad_pre)
-    grad_second = merged(lambda part: dot_nt(part_of(grad_pre, part), w_up))
-    back_two, grad_gain_two, grad_shift_two = norm_back(middle, norm2_gain, grad_second)
-    grad_middle = out_own.astype(F32) + back_two
-    branch_grad = both(grad_middle.astype(BF16))
-    w_qkv = [w_attn[:, k * SPAN : k * SPAN + 480] for k in range(4)]
-    w_out = [w_attn[:, k * SPAN + 480 : (k + 1) * SPAN] for k in range(4)]
-    grad_heads = [dot_nn(branch_grad, w_out[k]).astype(BF16) for k in range(4)]
-    heads_all = jnp.concatenate([heads[k, :, 96:] for k in range(4)], 1)
-    grad_out_w = finish(scatter(branch_grad, heads_all, True, 4))
-    grad_joined, sums = [], []
-    for k in range(4):
-        back, sum_k = attend_back(
-            joined[k], grad_heads[k], totals[k, :2], mask[0][:, None], 2, scaling
-        )
-        grad_joined.append(back)
-        sums.append(sum_k)
-    grad_qkv = finish(
-        [scatter(first, grad_joined[k], k % 2 == 0, 1)[0] for k in range(4)]
+    got = pair(dot_nt(part_of(hidden, 1), w_down).astype(BF16))
+    layer_out = middle + dot_nt(part_of(hidden, 0), w_down) + got.astype(F32) + down_bias
+    layer_out = move_rows(layer_out.astype(BF16))
+
+    lane = jnp.arange(128)[None, :] == 0
+    key_mask = jnp.where(lane, mask[0][:, None], 0.0).astype(BF16)
+    grad_tokens, grad_down, grad_up, grad_attn, sums, _ = backward_pass(
+        w_attn, w_up, w_down, tok, out_grad, first, second, joined, heads, middle, hidden, slope, totals,
+        key_mask, norm1_gain[None, :], norm2_gain[None, :],
     )
-    grad_all = jnp.concatenate(grad_joined, 1)
-    w_qkv_all = jnp.concatenate(w_qkv, 1)
-    grad_first = merged(lambda part: dot_nt(part_of(grad_all, part), w_qkv_all))
-    back_one, grad_gain_one, grad_shift_one = norm_back(source, norm1_gain, grad_first)
-    grad_tokens = move_rows((grad_middle + back_one).astype(BF16))
-
-    up_sum = jnp.sum(grad_pre.astype(F32), 0)
-    sum_up, sum_out, sum_gain_two, sum_shift_two, sum_down = summed(
-        [
-            spread([up_sum[k * units : (k + 1) * units] for k in range(4)]),
-            jnp.sum(grad_middle, 0),
-            grad_gain_two,
-            grad_shift_two,
-            jnp.sum(out_own.astype(F32), 0),
-        ],
-        total,
-    )
-    sum_query, sum_value, sum_gain_one, sum_shift_one = summed(
-        [
-            spread([s[0, :width] for s in sums]),
-            spread([s[1, :width] for s in sums]),
-            grad_gain_one,
-            grad_shift_one,
-        ],
-        total,
-    )
-
-    def own(vector):
-        size = vector.shape[0] // 4
-        return lax.dynamic_slice_in_dim(vector, z * size, size, 0)
+
+    def piece(index):
+        start = index * width
+        both = [grad_attn[:, i * SPAN + start : i * SPAN + start + width] for i in range(2)]
+        return jnp.concatenate(both, 1)
+
+    def own(first_row, start, size):
+        rows = lax.dynamic_slice_in_dim(sums[:, 0], first_row + 2 * z, 2, 0)
+        return rows[:, start : start + size].reshape(-1)
 
     return (
         layer_out,
         grad_tokens,
-        sum_gain_one,
-        sum_shift_one,
-        flat(grad_qkv[:, :, :width]),
-        own(sum_query),
-        flat(grad_qkv[:, :, width : 2 * width]),
-        flat(grad_qkv[:, :, 2 * width :]),
-        own(sum_value),
-        flat(grad_out_w).T,
-        sum_out,
-        sum_gain_two,
-        sum_shift_two,
-        flat(grad_up),
-        own(sum_up),
-        flat(grad_down).T,
-        sum_down,
+        sums[4, 0],
+        sums[5, 0],
+        piece(0),
+        own(16, 0, width),
+        piece(1),
+        piece(2),
+        own(16, width, width),
+        piece(3).T,
+        sums[1, 0],
+        sums[2, 0],
+        sums[3, 0],
+        grad_up,
+        own(8, 0, units),
+        grad_down.T,
+        sums[0, 0],
     )
 
 

time: 810 us -> 589 us (0.73)
  Pallas kernels: 299 us -> 513 us
  matrix products: 188 us -> 19.3 us
  waiting for transfers between devices: 99.7 us -> 1.88 us
  starting transfers between devices: 90.7 us -> 2.61 us
  local copies, waits for them, and re-layouts: 84.6 us -> 25 us
  other arithmetic: 33.6 us -> 14.1 us
    pallas_call x4 -> x1, Pallas kernels: 94.5 us -> 309 us  [backward_pass(): pl.pallas_call(functools.partial(backward_kernel, HDIM ** (-0.5)), in_spe...]
    dot_general x41 -> x0, matrix products: 132 us -> none  [the longest x36 103 us: dot_tn(): lax.dot_general(left, right, (((0,), (0,)), ((), ())), preferred_element_...]
    ppermute x49 -> x0, waiting for transfers between devices: 99.6 us -> none  [the longest x13 41.7 us: along_y(): return lax.ppermute(value, 'dp', [(i, i ^ 4) for i in range(8)])]
    ppermute x49 -> x0, starting transfers between devices: 47.2 us -> none  [the longest x14 11.3 us: along_x(): return lax.ppermute(value, 'dp', [(i, i ^ 2) for i in range(8)])]
    dot_general x6 -> x2, matrix products: 55.7 us -> 19.3 us  [dot_nt(): lax.dot_general(left, right, (((1,), (1,)), ((), ())), preferred_element_...]
    ppermute x9 -> x1, starting transfers between devices: 34.6 us -> 0.69 us  [pair(): return lax.ppermute(value, 'dp', [(i, i ^ 1) for i in range(8)])]
    concatenate x3 -> x0, local copies, waits for them, and re-layouts: 19.5 us -> none  [the longest x1 10.4 us: local_chips(): grad_all = jnp.concatenate(grad_joined, 1)]
    squeeze x7 -> x0, local copies, waits for them, and re-layouts: 14.5 us -> none  [the longest x1 5.71 us: local_chips(): joined[k]]
  transfers between devices with their start and end apart: 60 -> 2, of which waited for: 20 -> 1; matrix products, arithmetic and copies ran while one was open for 26% -> 2% of each run, Pallas kernels for 0% -> 54%
where the time goes in v3:
time: 589 us; the launch traced here: 577 us
  Pallas kernels  513 us (87%)
  local copies, waits for them, and re-layouts  25 us (4%)
  matrix products  19.3 us (3%)
  other arithmetic  14.1 us (2%)
    pallas_call x1, Pallas kernels, backward_pass(): pl.pallas_call(functools.partial(backward_kernel, HDIM ** (-0.5)), in_spe...  309 us
    pallas_call x1, Pallas kernels, forward_pass(): pl.pallas_call(functools.partial(forward_kernel, HDIM ** (-0.5)), in_spec...  204 us
    dot_general x2, matrix products, dot_nt(): lax.dot_general(left, right, (((1,), (1,)), ((), ())), preferred_element_...  19.3 us
  transfers between devices with their start and end apart: 2, of which 1 were waited for; matrix products, arithmetic and copies ran while one was open for 2% of the time, Pallas kernels for 54%

profile of v3, /device:TPU:1, one launch (start us, length us, event | category | flops | bytes accessed | tf_op | source)
XLA Modules:
  0.0 577.0 jit_solution(6275506538476240984)
XLA Ops:
  0.7 0.0 copy-start.4
  0.7 0.0 copy-start.3
  0.7 1.4 fusion.16
  2.1 0.6 fusion.9
  2.7 0.7 fusion.13
  3.4 0.8 reshape.95
  4.2 0.8 reshape.96
  4.9 0.1 pad_maximum_fusion.5
  5.0 0.7 stack_reshape.3
  5.7 0.6 pad.4.bias_in
  6.3 1.0 reshape.91
  7.4 1.0 reshape.92
  8.4 1.0 reshape.89
  9.4 1.0 reshape.90
  10.4 1.3 broadcast_in_dim.64.gain_one
  11.7 1.3 broadcast_in_dim.66.gain_two
  13.0 1.3 broadcast_in_dim.65.shift_one
  14.3 1.3 broadcast_in_dim.67.shift_two
  15.6 1.3 broadcast_in_dim.68.bias_out
  16.9 3.0 broadcast_multiply_fusion.cotangent
  20.0 0.0 copy-done.4
  20.0 0.0 copy-done.3
  20.0 1.0 bitcast_bitcast_fusion
  21.0 1.0 pad_maximum_fusion.attn_shard
  22.0 0.6 broadcast_in_dim.63.mask_in
  22.6 204.1 %forward_pass.1 = (bf16[1280,2560]{1,0:T(8,128)(2,1)}, bf16[1280,2560]{1,0:T(8,128)(2,1)}, bf16[1280,2560]{1,0:T(8,128)(2,1)}, bf16[768,1280]{1,0:T(8,128)(2,1)}...) custom-call(bf16[2,160,640]{2,1,0:T(8,128)(2,1)} %pad_maximum_fusion, ...), custom_call_target="tpu_custom_call" | custom-call | flops 25165824000 | bytes 80000000 | tf_op jit(solution)/shard_map/forward_pass/pallas_call | solution.py:587
  226.7 0.0 copy-start.5
  226.7 9.0 %fusion.6 = bf16[768,1280]{1,0:T(8,128)(2,1)S(1)} fusion(bf16[1280,2560]{1,0:T(8,128)(2,1)} %get-tuple-element.38.w_down_in, bf16[1536,2560]{1,0:T(8,128)(2,1)} %get-tuple-element.37.hidden_in, s32[]{:T(128)S(6)} %select_n.75), kind=kOutput, calls=%fused_computation.5 | convolution fusion | flops 5034147840 | bytes 12451844 | tf_op jit(solution)/shard_map/dot_general | solution.py:42
  235.7 0.7 collective-permute-start
  236.4 0.8 slice_reduce_fusion
  237.2 1.0 select_convert_fusion.key_mask
  238.2 1.9 collective-permute-done
  240.1 0.0 copy-done.5
  240.1 10.4 %add_convert_fusion = bf16[768,1280]{1,0:T(8,128)(2,1)S(1)} fusion(bf16[768,1280]{1,0:T(8,128)(2,1)} %collective-permute-done, f32[768,1280]{1,0:T(8,128)} %get-tuple-element.36.middle_in, bf16[1280,2560]{1,0:T(8,128)(2,1)} %get-tuple-element.38.w_down_in, bf16[1536,2560]{1,0:T(8,128)(2,1)} %get-tuple-element.37.hidden_in, s32[]{:T(128)S(6)} %select_n.74, ...), kind=kOutput, calls=%fused_computation | convolution fusion | flops 5038080000 | bytes 18355204 | tf_op jit(solution)/shard_map/dot_general | solution.py:42
  250.5 1.9 collective-permute-start.1
  252.4 308.9 %backward_pass.1 = (bf16[768,1280]{1,0:T(8,128)(2,1)}, f32[160,1280]{1,0:T(8,128)}, f32[160,1280]{1,0:T(8,128)}, f32[160,1280]{1,0:T(8,128)}, f32[24,1,1280]{2,1,0:T(1,128)}, /*index=5*/bf16[1536,2560]{1,0:T(8,128)(2,1)}) custom-call(bf16[1280,2560]{1,0:T(8,128)(2,1)} %get-tuple-element.39.w_attn_in, bf16[1280,2560]{1,0:T(8,128)(2,1)} %get-tuple-element.40.w_up_in, ...), custom_call_target="tpu_custom_call" | custom-call | flops 50331648000 | bytes 90000000 | tf_op jit(solution)/shard_map/backward_pass/pallas_call | solution.py:1133
  561.3 0.7 constant_dynamic-slice_fusion
  562.1 0.6 reshape.99
  562.7 0.1 fusion.18
  562.8 0.7 reshape.97
  563.4 0.7 reshape.98
  564.1 1.5 slice_reduce_fusion.1
  565.5 1.8 fusion.17
  567.4 0.8 maximum_bitcast_fusion
  568.2 0.0 copy-start
  568.2 0.8 pad_maximum_fusion.3
  569.0 0.8 pad_maximum_fusion.2
  569.8 0.8 pad_maximum_fusion.1
  570.6 0.0 copy-start.2
  570.6 0.0 collective-permute-done.1
  570.6 3.1 broadcast_select_fusion
  573.7 0.0 copy-start.1
  573.7 0.0 copy-done
  573.7 1.3 copy.58
  575.0 0.0 copy-done.2
  575.0 0.9 copy.59
  575.9 0.0 copy-done.1
  575.9 0.9 copy.60
  (9 shorter events, 0.1 us)
Async XLA Ops:
  0.7 19.3 %copy-start.4 = (bf16[160,1280]{1,0:T(8,128)(2,1)S(1)}, bf16[160,1280]{1,0:T(8,128)(2,1)}, u32[]{:S(2)}) copy-start(bf16[160,1280]{1,0:T(8,128)(2,1)} %param.32) | copy-start | bytes 1228804
  0.7 19.3 %copy-start.3 = (bf16[1280,160]{0,1:T(8,128)(2,1)S(1)}, bf16[1280,160]{0,1:T(8,128)(2,1)}, u32[]{:S(2)}) copy-start(bf16[1280,160]{0,1:T(8,128)(2,1)} %param.34) | copy-start | bytes 1228804
  226.7 13.4 %copy-start.5 = (f32[1280]{0:T(1024)S(1)}, f32[1280]{0:T(1024)}, u32[]{:S(2)}) copy-start(f32[1280]{0:T(1024)} %param.35) | copy-start | bytes 15364
  235.7 4.4 collective-permute-start
  250.5 320.1 %collective-permute-start.1 = (bf16[768,1280]{1,0:T(8,128)(2,1)S(1)}, bf16[768,1280]{1,0:T(8,128)(2,1)}, u32[]{:S(2)}, u32[]{:S(2)}) collective-permute-start(bf16[768,1280]{1,0:T(8,128)(2,1)S(1)} %add_convert_fusion), channel_id=1, source_target_pairs={{1,4},{3,6},{4,1},{6,3},{9,12},{11,14},{12,9},{14,11},{17,20},{19,... | collective-permute-start | bytes 5898248 | tf_op jit(solution)/shard_map/ppermute | solution.py:1434
  568.2 5.5 copy-start
  570.6 4.4 copy-start.2
  573.7 2.2 copy-start.1

commit v4 on v3

--- a/solution.py
+++ b/solution.py
@@ -619,6 +619,22 @@
     )(*shards, tokens, cotangent, mask, bias, gain_one, shift_one, gain_two, shift_two, bias_out)
 
 
+BACKWARD_STEPS = (
+    ("load",), ("P", 0, 0), ("pre",), ("P", 0, 1), ("pre",), ("pre",), ("pre",), ("2", 0, 0), ("soth",),
+    ("send", "a"), ("P", 0, 2), ("P", 0, 3), ("wait", "a"), ("ntwo",), ("send", "b"), ("3", 0, 0),
+    ("2", 0, 1), ("2", 0, 2), ("P", 1, 0), ("wait", "b"), ("hb",), ("att",), ("3", 0, 1), ("2", 0, 3),
+    ("att",), ("P", 1, 1), ("att",), ("3", 0, 3), ("3", 0, 2), ("aend",), ("P", 1, 2), ("hb",), ("2", 1, 0),
+    ("att",), ("2", 1, 1), ("att",), ("P", 1, 3), ("2", 1, 2), ("F", 0), ("att",), ("aend",), ("3", 1, 1),
+    ("3", 1, 0), ("P", 2, 0), ("2", 1, 3), ("P", 2, 1), ("hb",), ("3", 1, 2), ("att",), ("G", 0), ("att",),
+    ("att",), ("3", 1, 3), ("aend",), ("P", 2, 2), ("2", 2, 1), ("hb",), ("att",), ("F", 1), ("att",),
+    ("3", 2, 1), ("2", 2, 2), ("att",), ("aend",), ("3", 2, 2), ("foth",), ("send", "c"), ("P", 2, 3),
+    ("tok",), ("2", 2, 0), ("wait", "c"), ("none",), ("reloc",), ("none",), ("2", 2, 3), ("reloc",),
+    ("none",), ("hs", "c"), ("G", 1), ("3", 2, 0), ("hw", "c"), ("hs", "x"), ("hw", "x"), ("hs", "y"),
+    ("3", 2, 3), ("hw", "y"), ("hs", "z1"), ("reloc",), ("F", 2), ("hw", "z1"), ("hs", "z2"), ("wreloc",),
+    ("G", 2), ("hw", "z2"),
+)
+
+
 def backward_kernel(
     scaling,
     w_attn_in, w_up_in, w_down_in, tok_in, grad_in, first_in, second_in, joined_in, heads_in, middle_in,
@@ -702,37 +718,35 @@
     sums[...] = jnp.zeros_like(sums)
 
     in_flight = [[] for _ in range(TURNS)]
-
-    def place(k, where):
-        return product.at[k, pl.ds(pl.multiple_of(where * UNIT, 16), UNIT)]
+    staged = [None] * TURNS
+    rows_half = UNIT // 2
+
+    def place(k, where, part=None):
+        if part is None:
+            return product.at[k, pl.ds(pl.multiple_of(where * UNIT, 16), UNIT)]
+        start = pl.multiple_of(where * UNIT + part * rows_half, 16)
+        return product.at[k, pl.ds(start, rows_half)]
+
+    def slot(ref, k, part):
+        return ref.at[k, part * rows_half : (part + 1) * rows_half]
+
+    def sem_of(array, kind, k):
+        return array * 28 + kind * 4 + k
 
     def ready(k):
         for copy in in_flight[k]:
             copy.wait_send()
         in_flight[k] = []
 
-    def produce(k, factor, chunk):
-        ready(k)
-
-        def step_part(part, _):
-            rows = pl.ds(pl.multiple_of(part * 640, 640), 640)
-            product[k, rows, :] = dot_tn(factor[:, rows], chunk[...]).astype(BF16)
-            return 0
-
-        lax.fori_loop(0, 2, step_part, 0)
-
-    def ways(k):
-        if k % 2 == 0:
-            return to_x, to_y, plane_x, plane_y
-        return to_y, to_x, plane_y, plane_x
-
     def stage_one(array, k):
-        go, _, near, _ = ways(k)
-        if array > 0:
-            pl.semaphore_wait(credit.at[k], 1)
-        sem = 16 * array + k
-        in_flight[k].append(send(place(k, plane_xy), far_got.at[k], sem + 4, go))
-        in_flight[k].append(send(place(k, near), near_got.at[k], sem, go))
+        for part, device, near in ((0, to_x, plane_x), (1, to_y, plane_y)):
+            if array > 0:
+                pl.semaphore_wait(credit.at[4 * part + k], 1)
+            far = place(k, plane_xy, part)
+            in_flight[k] += [
+                send(far, slot(far_got, k, part), sem_of(array, part, k), device),
+                send(place(k, near, part), slot(near_got, k, part), sem_of(array, 2 + part, k), device),
+            ]
 
     def add_to(target, sources):
         total = target[...].astype(F32)
@@ -741,71 +755,83 @@
         return total
 
     def stage_two(array, k):
-        go, follow, _, far = ways(k)
-        sem = 16 * array + k
-        arrived(far_got.at[k], sem + 4)
-        target = place(k, far)
-        target[...] = add_to(target, [far_got.at[k]]).astype(BF16)
-        if array > 0:
-            pl.semaphore_wait(credit.at[4 + k], 1)
-        in_flight[k].append(send(target, turn_got.at[k], sem + 8, follow))
-        arrived(near_got.at[k], sem)
-        target = place(k, plane)
-        target[...] = add_to(target, [near_got.at[k]]).astype(BF16)
+        for part, device, back, far in ((0, to_y, to_x, plane_y), (1, to_x, to_y, plane_x)):
+            arrived(slot(far_got, k, part), sem_of(array, part, k))
+            target = place(k, far, part)
+            target[...] = add_to(target, [slot(far_got, k, part)]).astype(BF16)
+            if array > 0:
+                pl.semaphore_wait(credit.at[8 + 4 * part + k], 1)
+            in_flight[k].append(send(target, slot(turn_got, k, part), sem_of(array, 4 + part, k), device))
+        for part, back in ((0, to_x), (1, to_y)):
+            arrived(slot(near_got, k, part), sem_of(array, 2 + part, k))
+            target = place(k, plane, part)
+            target[...] = add_to(target, [slot(near_got, k, part)]).astype(BF16)
+            if array < 2:
+                tell(4 * part + k, back)
+
+    def stage_three(array, k):
+        for part in range(2):
+            arrived(slot(turn_got, k, part), sem_of(array, 4 + part, k))
+        source = place(k, plane)
+        total = add_to(source, [turn_got.at[k]]).astype(BF16)
         if array < 2:
-            tell(k, go)
-
-    def stage_three(array, k):
-        _, follow, _, _ = ways(k)
-        sem = 16 * array + k
-        arrived(turn_got.at[k], sem + 8)
-        target = place(k, plane)
-        total = add_to(target, [turn_got.at[k]]).astype(BF16)
-        if array < 2:
-            tell(4 + k, follow)
+            tell(8 + k, to_y)
+            tell(12 + k, to_x)
         if k == 0:
             line_own[...] = total
             return
-        target[...] = total
+        if array < 2:
+            if staged[k] is not None:
+                staged[k].wait_send()
+            row, col = (k - 1) % 2, (k - 1) // 2
+            source = send_rows.at[
+                row * UNIT : (row + 1) * UNIT, col * SPAN : (col + 1) * SPAN
+            ]
+        source[...] = total
         if array > 0:
-            pl.semaphore_wait(credit.at[8 + k], 1)
-        in_flight[k].append(send(target, line_got.at[k], sem + 12, to_z[(TURNS - k) % TURNS]))
+            pl.semaphore_wait(credit.at[16 + k], 1)
+        copy = send(source, line_got.at[k], sem_of(array, 6, k), to_z[(TURNS - k) % TURNS])
+        if array < 2:
+            staged[k] = copy
+        else:
+            in_flight[k].append(copy)
 
     results = [down_out, up_out, attn_out]
     final_moves = []
+    last_moves = []
 
     def final_one(array):
-        for copy in final_moves:
-            copy()
+        for wait in final_moves:
+            wait()
         final_moves.clear()
         for k in range(1, TURNS):
-            arrived(line_got.at[k], 16 * array + k + 12)
+            arrived(line_got.at[k], sem_of(array, 6, k))
         final[...] = add_to(line_own, [line_got.at[k] for k in range(1, TURNS)])
         if array < 2:
             for k in range(1, TURNS):
-                tell(8 + k, to_z[k])
-        rows = UNIT // 2
-        keep = pl.ds(pl.multiple_of(core * rows, 16), rows)
-        give = pl.ds(pl.multiple_of((1 - core) * rows, 16), rows)
-        final_moves.append(send(final.at[give], final_got.at[array], 52 + array, to_core).wait_send)
+                tell(16 + k, to_z[k])
+        keep = pl.ds(pl.multiple_of(core * rows_half, 16), rows_half)
+        give = pl.ds(pl.multiple_of((1 - core) * rows_half, 16), rows_half)
+        final_moves.append(send(final.at[give], final_got.at[array], 90 + array, to_core).wait_send)
         target = results[array].at[:, pl.ds(pl.multiple_of(core * SPAN, 128), SPAN)]
         final_moves.append(local(final.at[keep], target, 13).wait)
 
-    last_moves = []
-
     def final_two(array):
-        arrived(final_got.at[array], 52 + array)
+        arrived(final_got.at[array], 90 + array)
         target = results[array].at[:, pl.ds(pl.multiple_of((1 - core) * SPAN, 128), SPAN)]
         last_moves.append(local(final_got.at[array], target, 14 + array).wait)
 
-    grad_load.wait()
-    right_loads[0].wait()
-    produce(0, grad, right.at[0])
-    stage_one(0, 0)
-    right_loads[0] = load_right(hidden_in, 2, 0)
-    pre_puts = []
-
-    def grad_pre(k):
+    pre_puts, pre_loads = [], [None, None]
+    loads = {"left": left_load}
+    exchange = {}
+    start = jnp.zeros((1, 160), F32)
+    att_total = [start]
+
+    def load():
+        grad_load.wait()
+
+    def pre():
+        k = len(pre_puts)
         weight_loads[k].wait()
         slope_loads[k].wait()
 
@@ -821,37 +847,20 @@
         pre_puts.append(local(wide.at[:, columns(k)], pre_out.at[:, columns(k)], 17 + k))
         weight_loads[k] = local(w_up_in.at[:, columns(k)], weight.at[:, columns(k)], 3 + k)
 
-    grad_pre(0)
-    grad_pre(1)
-    right_loads[1].wait()
-    produce(1, grad, right.at[1])
-    stage_one(0, 1)
-    right_loads[1] = load_right(hidden_in, 3, 1)
-    grad_pre(2)
-    grad_pre(3)
-    for load in weight_loads:
-        load.wait()
-
     def second_part(rows):
         return dot_nt(wide[rows, :], weight[...])
 
-    def second_other(step, _):
-        rows = pl.ds(pl.multiple_of(other + step * 256, 256), 256)
-        send_rows[pl.ds(pl.multiple_of(step * 256, 256), 256), :] = second_part(rows).astype(BF16)
-        return 0
-
-    lax.fori_loop(0, half // 256, second_other, 0)
-    rows_sent = send(send_rows, got_rows, 48, to_core)
-    stage_two(0, 0)
-    right_loads[0].wait()
-    produce(2, grad, right.at[0])
-    stage_one(0, 2)
-    right_loads[1].wait()
-    produce(3, grad, right.at[1])
-    stage_one(0, 3)
-    tell(12, to_core)
-    middle_load.wait()
-    arrived(got_rows, 48)
+    def soth():
+        for copy in weight_loads:
+            copy.wait()
+
+        def step_rows(step, _):
+            rows = pl.ds(pl.multiple_of(other + step * 256, 256), 256)
+            low = pl.ds(pl.multiple_of(step * 256, 256), 256)
+            send_rows[low, :] = second_part(rows).astype(BF16)
+            return 0
+
+        lax.fori_loop(0, half // 256, step_rows, 0)
 
     def norm_back_rows(values, gain, above):
         center = values - jnp.mean(values, -1, keepdims=True)
@@ -862,37 +871,109 @@
         back = (back - normed * jnp.mean(scaled * normed, -1, keepdims=True)) * scale
         return back, jnp.sum(above * normed, 0, keepdims=True), jnp.sum(above, 0, keepdims=True)
 
-    def norm_two(step, total):
-        low = pl.ds(pl.multiple_of(step * 256, 256), 256)
-        rows = pl.ds(pl.multiple_of(base + step * 256, 256), 256)
-        above = second_part(rows) + got_rows[low, :].astype(F32)
-        back, by_gain, by_shift = norm_back_rows(middle[low, :], gain_two[...], above)
-        out_grad = grad[rows, :].astype(F32)
-        below = out_grad + back
-        middle[low, :] = below
-        grad[rows, :] = below.astype(BF16)
-        by_down, by_out = jnp.sum(out_grad, 0, keepdims=True), jnp.sum(below, 0, keepdims=True)
-        return (total[0] + by_down, total[1] + by_out, total[2] + by_gain, total[3] + by_shift)
-
     zero = jnp.zeros((1, features), F32)
-    parts = lax.fori_loop(0, half // 256, norm_two, (zero,) * 4)
-    for i in range(4):
-        sums[i, :, :] = parts[i]
-    pl.semaphore_wait(credit.at[12], 1)
-    branch_sent = send(grad.at[own_rows], grad.at[own_rows], 49, to_core)
-    for copy in pre_puts:
-        copy.wait()
-    weight_load = local(w_attn_in, weight, 3)
-    joined_loads = [
-        local(joined_in.at[turn[k]], wide.at[:, k * SPAN : (k + 1) * SPAN], 7 + k) for k in range(TURNS)
-    ]
-    pre_loads = [local(pre_out.at[:, columns(k)], right.at[k], k) for k in range(2)]
-    stage_two(0, 1)
-    stage_three(0, 0)
-    weight_load.wait()
-    arrived(grad.at[other_rows], 49)
-
-    def heads_back(k):
+
+    def ntwo():
+        middle_load.wait()
+
+        def step_rows(step, total):
+            low = pl.ds(pl.multiple_of(step * 256, 256), 256)
+            rows = pl.ds(pl.multiple_of(base + step * 256, 256), 256)
+            above = second_part(rows) + got_rows[low, :].astype(F32)
+            back, by_gain, by_shift = norm_back_rows(middle[low, :], gain_two[...], above)
+            out_grad = grad[rows, :].astype(F32)
+            below = out_grad + back
+            middle[low, :] = below
+            grad[rows, :] = below.astype(BF16)
+            by_down, by_out = jnp.sum(out_grad, 0, keepdims=True), jnp.sum(below, 0, keepdims=True)
+            return (total[0] + by_down, total[1] + by_out, total[2] + by_gain, total[3] + by_shift)
+
+        parts = lax.fori_loop(0, half // 256, step_rows, (zero,) * 4)
+        for i in range(4):
+            sums[i, :, :] = parts[i]
+        exchange["a"].wait_send()
+        for copy in pre_puts[2:]:
+            copy.wait()
+        loads["weight"] = local(w_attn_in, weight, 3)
+        loads["joined"] = [
+            local(joined_in.at[turn[k]], wide.at[:, k * SPAN : (k + 1) * SPAN], 7 + k)
+            for k in range(TURNS)
+        ]
+
+    def hand(name):
+        if name == "a":
+            exchange[name] = send(send_rows, got_rows, 84, to_core)
+        elif name == "b":
+            pl.semaphore_wait(credit.at[20], 1)
+            exchange[name] = send(grad.at[own_rows], grad.at[own_rows], 85, to_core)
+        else:
+            exchange[name] = send(send_rows, got_rows, 86, to_core)
+
+    def take(name):
+        if name == "a":
+            arrived(got_rows, 84)
+        elif name == "b":
+            arrived(grad.at[other_rows], 85)
+        else:
+            arrived(got_rows, 86)
+            loads["tok"].wait()
+
+    def produce(array, k):
+        ready(k)
+        if array < 2:
+            if array == 0:
+                right_loads[k % 2].wait()
+                factor = grad
+            else:
+                pre_loads[k % 2].wait()
+                if k == 0:
+                    loads["left"].wait()
+                factor = left
+
+            def step_part(part, _):
+                rows = pl.ds(pl.multiple_of(part * 640, 640), 640)
+                product[k, rows, :] = dot_tn(factor[:, rows], right[k % 2]).astype(BF16)
+                return 0
+
+            lax.fori_loop(0, 2, step_part, 0)
+            if array == 0 and k < 2:
+                right_loads[k] = load_right(hidden_in, k + 2, k)
+            elif array == 0:
+                pre_puts[k - 2].wait()
+                pre_loads[k - 2] = load_right(pre_out, k - 2, k - 2)
+                if k == 3:
+                    tell(20, to_core)
+            elif k < 2:
+                pre_loads[k] = load_right(pre_out, k + 2, k)
+            if array == 1 and k == 3:
+                loads["left"] = local(first_in, left, 11)
+                loads["first"] = loads["left"]
+        else:
+            heads_load = local(heads_in.at[turn[k]], grad_heads, 4)
+            if "first" in loads:
+                loads.pop("first").wait()
+            heads_load.wait()
+
+            def step_part(part, _):
+                rows = pl.ds(pl.multiple_of(part * 640, 640), 640)
+                by_first = dot_tn(left[:, rows], wide[:, k * SPAN : k * SPAN + 480])
+                by_branch = dot_tn(grad[:, rows], grad_heads[:, 96:256])
+                product[k, rows, :] = jnp.concatenate([by_first, by_branch], -1).astype(BF16)
+                return 0
+
+            lax.fori_loop(0, 2, step_part, 0)
+        stage_one(array, k)
+
+    steps_done = {"hb": 0, "att": 0, "aend": 0, "none": 0, "reloc": 0}
+
+    def count_step(name):
+        steps_done[name] += 1
+        return steps_done[name] - 1
+
+    def hb():
+        k = count_step("hb")
+        if k == 0:
+            loads["weight"].wait()
         slab = pl.ds(pl.multiple_of(turn[k] * SPAN + 384, 128), 256)
 
         def step_rows(step, _):
@@ -901,14 +982,17 @@
             return 0
 
         lax.fori_loop(0, count // 512, step_rows, 0)
-        joined_loads[k].wait()
+        loads["joined"][k].wait()
         totals_loads[k].wait()
         key_sum[...] = jnp.zeros_like(key_sum)
         value_sum[...] = jnp.zeros_like(value_sum)
+        att_total[0] = start
 
     one_lane = (lax.broadcasted_iota(jnp.int32, (256, 48), 1) == 0).astype(F32).astype(BF16)
 
-    def attention(k, part, total):
+    def att():
+        step_at = count_step("att")
+        k, part = step_at // 3, step_at % 3
         low = k * SPAN
 
         def step_rows(step, total):
@@ -926,9 +1010,7 @@
                     jnp.concatenate([key, key_mask[:, :48]], -1),
                     jnp.concatenate([query, one_lane], -1),
                 )
-                probs = jnp.exp2(
-                    scores * (scaling * LOG2E) - totals[k, head : head + 1, rows]
-                )
+                probs = jnp.exp2(scores * (scaling * LOG2E) - totals[k, head : head + 1, rows])
                 grad_probs = dot_nt(value, above)
                 shared = jnp.sum(probs * grad_probs, 0, keepdims=True)
                 grad_scores = (probs * (grad_probs - shared)).astype(BF16)
@@ -939,9 +1021,10 @@
             wide[rows, low : low + 160] = joined.astype(BF16)
             return total + jnp.sum(joined, 0, keepdims=True)
 
-        return lax.fori_loop(2 * part, 2 * part + 2, step_rows, total)
-
-    def attention_end(k, total):
+        att_total[0] = lax.fori_loop(2 * part, 2 * part + 2, step_rows, att_total[0])
+
+    def aend():
+        k = count_step("aend")
         low = k * SPAN
 
         def step_rows(step, value_total):
@@ -952,93 +1035,9 @@
             wide[rows, low + 160 : low + 480] = joined.astype(BF16)
             return value_total + jnp.sum(joined[:, 160:], 0, keepdims=True)
 
-        value_total = lax.fori_loop(0, count // 256, step_rows, jnp.zeros((1, 160), F32))
-        sums[16 + 2 * turn[k] + core, :, :160] = total
+        value_total = lax.fori_loop(0, count // 256, step_rows, start)
+        sums[16 + 2 * turn[k] + core, :, :160] = att_total[0]
         sums[16 + 2 * turn[k] + core, :, 160:320] = value_total
-
-    def produce_attn(k):
-        heads_load = local(heads_in.at[turn[k]], grad_heads, 4)
-        ready(k)
-        heads_load.wait()
-
-        def step_part(part, _):
-            rows = pl.ds(pl.multiple_of(part * 640, 640), 640)
-            by_first = dot_tn(left[:, rows], wide[:, k * SPAN : k * SPAN + 480])
-            by_branch = dot_tn(grad[:, rows], grad_heads[:, 96:256])
-            product[k, rows, :] = jnp.concatenate([by_first, by_branch], -1).astype(BF16)
-            return 0
-
-        lax.fori_loop(0, 2, step_part, 0)
-
-    start = jnp.zeros((1, 160), F32)
-    left_load.wait()
-
-    def up_chunk(k):
-        slot = k % 2
-        pre_loads[slot].wait()
-        produce(k, left, right.at[slot])
-        stage_one(1, k)
-        if k < 2:
-            pre_loads[slot] = local(pre_out.at[:, columns(k + 2)], right.at[slot], slot)
-
-    heads_back(0)
-    up_chunk(0)
-    total = attention(0, 0, start)
-    stage_two(0, 2)
-    stage_three(0, 1)
-    total = attention(0, 1, total)
-    stage_two(0, 3)
-    up_chunk(1)
-    total = attention(0, 2, total)
-    attention_end(0, total)
-    stage_three(0, 2)
-    stage_two(1, 0)
-    heads_back(1)
-    total = attention(1, 0, start)
-    stage_three(0, 3)
-    up_chunk(2)
-    total = attention(1, 1, total)
-    stage_two(1, 1)
-    final_one(0)
-    up_chunk(3)
-    left_load = local(first_in, left, 11)
-    total = attention(1, 2, total)
-    attention_end(1, total)
-    final_two(0)
-    stage_two(1, 2)
-    stage_three(1, 0)
-    stage_three(1, 1)
-    left_load.wait()
-    produce_attn(0)
-    stage_one(2, 0)
-    produce_attn(1)
-    stage_one(2, 1)
-    heads_back(2)
-    stage_two(1, 3)
-    total = attention(2, 0, start)
-    stage_three(1, 2)
-    total = attention(2, 1, total)
-    stage_two(2, 0)
-    stage_three(1, 3)
-    total = attention(2, 2, total)
-    attention_end(2, total)
-    stage_two(2, 1)
-    produce_attn(2)
-    stage_one(2, 2)
-    final_one(1)
-    heads_back(3)
-    total = attention(3, 0, start)
-    stage_three(2, 0)
-    total = attention(3, 1, total)
-    stage_three(2, 1)
-    final_two(1)
-    total = attention(3, 2, total)
-    attention_end(3, total)
-    produce_attn(3)
-    stage_one(2, 3)
-    branch_sent.wait_send()
-    tok_load = local(tok_in, grad.at[0:half], 2)
-    stage_two(2, 2)
 
     def first_part(rows):
         total = None
@@ -1048,73 +1047,97 @@
             total = part if total is None else total + part
         return total
 
-    rows_sent.wait_send()
-
-    def first_other(step, _):
-        rows = pl.ds(pl.multiple_of(other + step * 256, 256), 256)
-        send_rows[pl.ds(pl.multiple_of(step * 256, 256), 256), :] = first_part(rows).astype(BF16)
-        return 0
-
-    lax.fori_loop(0, half // 256, first_other, 0)
-    rows_sent = send(send_rows, got_rows, 50, to_core)
-    stage_three(2, 2)
-    tok_load.wait()
-    arrived(got_rows, 50)
-
-    def norm_one(step, total):
-        low = pl.ds(pl.multiple_of(step * 256, 256), 256)
+    def foth():
+        for copy in staged[1:]:
+            copy.wait_send()
+
+        def step_rows(step, _):
+            rows = pl.ds(pl.multiple_of(other + step * 256, 256), 256)
+            low = pl.ds(pl.multiple_of(step * 256, 256), 256)
+            send_rows[low, :] = first_part(rows).astype(BF16)
+            return 0
+
+        lax.fori_loop(0, half // 256, step_rows, 0)
+
+    def none():
+        step = count_step("none")
+        low = slice(step * 256, step * 256 + 256)
         rows = pl.ds(pl.multiple_of(base + step * 256, 256), 256)
         above = first_part(rows) + got_rows[low, :].astype(F32)
-        back, by_gain, by_shift = norm_back_rows(grad[low, :].astype(F32), gain_one[...], above)
-        below = middle[low, :] + back
-        grad[pl.ds(pl.multiple_of(half + step * 256, 256), 256), :] = below.astype(BF16)
-        return (total[0] + by_gain, total[1] + by_shift)
-
-    parts = lax.fori_loop(0, half // 256, norm_one, (zero,) * 2)
-    for i in range(2):
-        sums[4 + i, :, :] = parts[i]
-    tokens_away = remote(grad.at[half:count], tokens_out, 51, to_clip)
-    tokens_here = pltpu.make_async_copy(grad.at[half:count], tokens_out, local_sem.at[2])
-
-    @pl.when(moves)
-    def _():
-        tokens_away.start()
-
-    @pl.when(jnp.logical_not(moves))
-    def _():
-        tokens_here.start()
-
-    def hop(index, device):
-        copy = send(sums, sums_got.at[index], 55 + index, device)
-        copy.wait_send()
-        arrived(sums_got.at[index], 55 + index)
+        values = got_tok[low, :].astype(F32)
+        back, by_gain, by_shift = norm_back_rows(values, gain_one[...], above)
+        grad[half + step * 256 : half + step * 256 + 256, :] = (middle[low, :] + back).astype(BF16)
+        if step == 0:
+            sums[4, :, :] = by_gain
+            sums[5, :, :] = by_shift
+        else:
+            sums[4, :, :] += by_gain
+            sums[5, :, :] += by_shift
+
+    got_tok = grad.at[0:half]
+
+    def tokens_move(step):
+        rows = pl.ds(step * 256, 256)
+        source = grad.at[half + step * 256 : half + step * 256 + 256]
+        away = remote(source, tokens_out.at[rows], 87 + step, to_clip)
+        here = pltpu.make_async_copy(source, tokens_out.at[rows], local_sem.at[25 + step])
+        return away, here
+
+    def reloc():
+        away, here = tokens_move(count_step("reloc"))
+
+        @pl.when(moves)
+        def _():
+            away.start()
+
+        @pl.when(jnp.logical_not(moves))
+        def _():
+            here.start()
+
+    def wreloc():
+        for step in range(half // 256):
+            away, here = tokens_move(step)
+
+            @pl.when(moves)
+            def _(away=away):
+                away.wait()
+
+            @pl.when(jnp.logical_not(moves))
+            def _(here=here):
+                here.wait()
+
+    hops = {"c": (0, to_core), "x": (1, to_x), "y": (2, to_y), "z1": (3, to_z_pair), "z2": (4, to_z[2])}
+    hop_copies = {}
+
+    def hs(name):
+        index, device = hops[name]
+        hop_copies[name] = send(sums, sums_got.at[index], 93 + index, device)
+
+    def hw(name):
+        index, _ = hops[name]
+        hop_copies[name].wait_send()
+        arrived(sums_got.at[index], 93 + index)
         sums[...] = sums[...] + sums_got[index]
 
-    hop(0, to_core)
-    hop(1, to_x)
-    stage_two(2, 3)
-    hop(2, to_y)
-    hop(3, to_z_pair)
-    hop(4, to_z[2])
+    def token_load():
+        exchange["b"].wait_send()
+        loads["tok"] = local(tok_in, grad.at[0:half], 2)
+
+    actions = {
+        "load": load, "pre": pre, "soth": soth, "ntwo": ntwo, "hb": hb, "att": att, "aend": aend,
+        "foth": foth, "none": none, "reloc": reloc, "wreloc": wreloc, "send": hand, "wait": take,
+        "P": produce, "2": stage_two, "3": stage_three, "F": final_one, "G": final_two, "hs": hs, "hw": hw,
+        "tok": token_load,
+    }
+    for name, *numbers in BACKWARD_STEPS:
+        actions[name](*numbers)
     sums_put = local(sums, sums_out, 5)
-    stage_three(2, 3)
-    final_one(2)
-    final_two(2)
-
-    @pl.when(moves)
-    def _():
-        tokens_away.wait()
-
-    @pl.when(jnp.logical_not(moves))
-    def _():
-        tokens_here.wait()
-
-    sums_put.wait()
-    rows_sent.wait_send()
+    exchange["c"].wait_send()
     for wait in final_moves + last_moves:
         wait()
     for k in range(TURNS):
         ready(k)
+    sums_put.wait()
 
 
 def backward_pass(
@@ -1158,10 +1181,10 @@
             pltpu.VMEM((3, UNIT // 2, SPAN), F32),
             pltpu.VMEM((24, 1, features), F32),
             pltpu.VMEM((5, 24, 1, features), F32),
-            pltpu.SemaphoreType.DMA((64,)),
-            pltpu.SemaphoreType.DMA((64,)),
+            pltpu.SemaphoreType.DMA((100,)),
+            pltpu.SemaphoreType.DMA((100,)),
             pltpu.SemaphoreType.DMA((32,)),
-            pltpu.SemaphoreType.REGULAR((16,)),
+            pltpu.SemaphoreType.REGULAR((24,)),
         ],
         cost_estimate=pl.CostEstimate(
             flops=4 * count * features * 6400, bytes_accessed=90_000_000, transcendentals=30_000_000

time: 589 us -> 509 us (0.86)
  Pallas kernels: 513 us -> 435 us
    pallas_call x1, Pallas kernels: 309 us -> 231 us  [backward_pass(): pl.pallas_call(functools.partial(backward_kernel, HDIM ** (-0.5)), in_spe...]
  transfers between devices with their start and end apart: 2 -> 2, of which waited for: 1 -> 1; matrix products, arithmetic and copies ran while one was open for 2% -> 2% of each run, Pallas kernels for 54% -> 46%
where the time goes in v4:
time: 509 us; the launch traced here: 499 us
  Pallas kernels  435 us (85%)
  local copies, waits for them, and re-layouts  25 us (5%)
  matrix products  19.3 us (4%)
  other arithmetic  14.1 us (3%)
    pallas_call x1, Pallas kernels, backward_pass(): pl.pallas_call(functools.partial(backward_kernel, HDIM ** (-0.5)), in_spe...  231 us
    pallas_call x1, Pallas kernels, forward_pass(): pl.pallas_call(functools.partial(forward_kernel, HDIM ** (-0.5)), in_spec...  204 us
    dot_general x2, matrix products, dot_nt(): lax.dot_general(left, right, (((1,), (1,)), ((), ())), preferred_element_...  19.3 us
  transfers between devices with their start and end apart: 2, of which 1 were waited for; matrix products, arithmetic and copies ran while one was open for 2% of the time, Pallas kernels for 46%

profile of v4, /device:TPU:1, one launch (start us, length us, event | category | flops | bytes accessed | tf_op | source)
XLA Modules:
  0.0 499.1 jit_solution(9139391937793296344)
XLA Ops:
  0.7 0.0 copy-start.4
  0.7 0.0 copy-start.3
  0.7 1.4 fusion.16
  2.1 0.6 fusion.9
  2.7 0.7 fusion.13
  3.4 0.8 reshape.95
  4.2 0.8 reshape.96
  4.9 0.1 pad_maximum_fusion.5
  5.0 0.7 stack_reshape.3
  5.7 0.6 pad.4.bias_in
  6.3 1.0 reshape.91
  7.4 1.0 reshape.92
  8.4 1.0 reshape.89
  9.4 1.0 reshape.90
  10.4 1.3 broadcast_in_dim.64.gain_one
  11.7 1.3 broadcast_in_dim.66.gain_two
  13.0 1.3 broadcast_in_dim.65.shift_one
  14.3 1.3 broadcast_in_dim.67.shift_two
  15.6 1.3 broadcast_in_dim.68.bias_out
  16.9 3.0 broadcast_multiply_fusion.cotangent
  20.0 0.0 copy-done.4
  20.0 0.0 copy-done.3
  20.0 1.0 bitcast_bitcast_fusion
  21.0 1.0 pad_maximum_fusion.attn_shard
  22.0 0.6 broadcast_in_dim.63.mask_in
  22.6 204.1 %forward_pass.1 = (bf16[1280,2560]{1,0:T(8,128)(2,1)}, bf16[1280,2560]{1,0:T(8,128)(2,1)}, bf16[1280,2560]{1,0:T(8,128)(2,1)}, bf16[768,1280]{1,0:T(8,128)(2,1)}...) custom-call(bf16[2,160,640]{2,1,0:T(8,128)(2,1)} %pad_maximum_fusion, ...), custom_call_target="tpu_custom_call" | custom-call | flops 25165824000 | bytes 80000000 | tf_op jit(solution)/shard_map/forward_pass/pallas_call | solution.py:587
  226.7 0.0 copy-start.5
  226.7 9.0 %fusion.6 = bf16[768,1280]{1,0:T(8,128)(2,1)S(1)} fusion(bf16[1280,2560]{1,0:T(8,128)(2,1)} %get-tuple-element.38.w_down_in, bf16[1536,2560]{1,0:T(8,128)(2,1)} %get-tuple-element.37.hidden_in, s32[]{:T(128)S(6)} %select_n.75), kind=kOutput, calls=%fused_computation.5 | convolution fusion | flops 5034147840 | bytes 12451844 | tf_op jit(solution)/shard_map/dot_general | solution.py:42
  235.7 0.7 collective-permute-start
  236.4 0.8 slice_reduce_fusion
  237.2 1.0 select_convert_fusion.key_mask
  238.2 1.9 collective-permute-done
  240.1 0.0 copy-done.5
  240.1 10.4 %add_convert_fusion = bf16[768,1280]{1,0:T(8,128)(2,1)S(1)} fusion(bf16[768,1280]{1,0:T(8,128)(2,1)} %collective-permute-done, f32[768,1280]{1,0:T(8,128)} %get-tuple-element.36.middle_in, bf16[1280,2560]{1,0:T(8,128)(2,1)} %get-tuple-element.38.w_down_in, bf16[1536,2560]{1,0:T(8,128)(2,1)} %get-tuple-element.37.hidden_in, s32[]{:T(128)S(6)} %select_n.74, ...), kind=kOutput, calls=%fused_computation | convolution fusion | flops 5038080000 | bytes 18355204 | tf_op jit(solution)/shard_map/dot_general | solution.py:42
  250.5 1.9 collective-permute-start.1
  252.4 231.0 %backward_pass.1 = (bf16[768,1280]{1,0:T(8,128)(2,1)}, f32[160,1280]{1,0:T(8,128)}, f32[160,1280]{1,0:T(8,128)}, f32[160,1280]{1,0:T(8,128)}, f32[24,1,1280]{2,1,0:T(1,128)}, /*index=5*/bf16[1536,2560]{1,0:T(8,128)(2,1)}) custom-call(bf16[1280,2560]{1,0:T(8,128)(2,1)} %get-tuple-element.39.w_attn_in, bf16[1280,2560]{1,0:T(8,128)(2,1)} %get-tuple-element.40.w_up_in, ...), custom_call_target="tpu_custom_call" | custom-call | flops 50331648000 | bytes 90000000 | tf_op jit(solution)/shard_map/backward_pass/pallas_call | solution.py:1156
  483.5 0.7 constant_dynamic-slice_fusion
  484.2 0.6 reshape.99
  484.8 0.1 fusion.18
  484.9 0.7 reshape.97
  485.6 0.7 reshape.98
  486.2 1.5 slice_reduce_fusion.1
  487.7 1.8 fusion.17
  489.5 0.8 maximum_bitcast_fusion
  490.3 0.0 copy-start
  490.3 0.8 pad_maximum_fusion.3
  491.1 0.8 pad_maximum_fusion.2
  491.9 0.8 pad_maximum_fusion.1
  492.8 0.0 copy-start.2
  492.8 0.0 collective-permute-done.1
  492.8 3.1 broadcast_select_fusion
  495.9 0.0 copy-start.1
  495.9 0.0 copy-done
  495.9 1.3 copy.58
  497.1 0.0 copy-done.2
  497.1 0.9 copy.59
  498.0 0.0 copy-done.1
  498.0 0.9 copy.60
  (9 shorter events, 0.1 us)
Async XLA Ops:
  0.7 19.3 %copy-start.4 = (bf16[160,1280]{1,0:T(8,128)(2,1)S(1)}, bf16[160,1280]{1,0:T(8,128)(2,1)}, u32[]{:S(2)}) copy-start(bf16[160,1280]{1,0:T(8,128)(2,1)} %param.32) | copy-start | bytes 1228804
  0.7 19.3 %copy-start.3 = (bf16[1280,160]{0,1:T(8,128)(2,1)S(1)}, bf16[1280,160]{0,1:T(8,128)(2,1)}, u32[]{:S(2)}) copy-start(bf16[1280,160]{0,1:T(8,128)(2,1)} %param.34) | copy-start | bytes 1228804
  226.7 13.4 %copy-start.5 = (f32[1280]{0:T(1024)S(1)}, f32[1280]{0:T(1024)}, u32[]{:S(2)}) copy-start(f32[1280]{0:T(1024)} %param.35) | copy-start | bytes 15364
  235.7 4.4 collective-permute-start
  250.5 242.3 %collective-permute-start.1 = (bf16[768,1280]{1,0:T(8,128)(2,1)S(1)}, bf16[768,1280]{1,0:T(8,128)(2,1)}, u32[]{:S(2)}, u32[]{:S(2)}) collective-permute-start(bf16[768,1280]{1,0:T(8,128)(2,1)S(1)} %add_convert_fusion), channel_id=1, source_target_pairs={{1,4},{3,6},{4,1},{6,3},{9,12},{11,14},{12,9},{14,11},{17,20},{19,... | collective-permute-start | bytes 5898248 | tf_op jit(solution)/shard_map/ppermute | solution.py:1457
  490.3 5.5 %copy-start = (bf16[768,1280]{1,0:T(8,128)(2,1)S(1)}, bf16[768,1280]{1,0:T(8,128)(2,1)}, u32[]{:S(2)}) copy-start(bf16[768,1280]{1,0:T(8,128)(2,1)} %get-tuple-element.97) | copy-start | bytes 5898244
  492.8 4.4 copy-start.2
  495.9 2.2 copy-start.1

commit v5 on v4

--- a/solution.py
+++ b/solution.py
@@ -218,14 +218,26 @@
     return ref.at[pl.ds(pl.multiple_of(start, 16), size)]
 
 
+FORWARD_STEPS = (
+    ("pr", 0), ("tok",), ("pr", 1), ("zz", 0), ("pp", 0, 0), ("pp", 1, 0), ("pr", 2), ("fw", 0, 0),
+    ("fw", 1, 0), ("tokw",), ("pp", 2, 0), ("norm",), ("send", "a"), ("wait", "a"), ("pp", 0, 1), ("proj",),
+    ("fw", 2, 0), ("att",), ("att",), ("fw", 0, 1), ("zz", 1), ("pp", 0, 2), ("pp", 0, 3), ("proj",),
+    ("att",), ("att",), ("zz", 2), ("fw", 0, 2), ("fw", 0, 3), ("pp", 1, 1), ("cot",), ("pp", 1, 2),
+    ("proj",), ("att",), ("att",), ("pp", 1, 3), ("proj",), ("att",), ("pp", 2, 1), ("att",), ("fw", 1, 3),
+    ("fw", 1, 2), ("both",), ("send", "b"), ("bown",), ("wait", "b"), ("fw", 1, 1), ("ntwo",),
+    ("send", "c"), ("fw", 2, 1), ("pp", 2, 2), ("wait", "c"), ("pp", 2, 3), ("lift",), ("lift",), ("lift",),
+    ("lift",), ("down",), ("fw", 2, 2), ("fw", 2, 3), ("cotx",), ("down",), ("down",), ("cotw",), ("down",),
+)
+
+
 def forward_kernel(
     scaling,
-    attn_shard, up_shard, down_shard, tokens, cotangent, mask_in, bias_in,
-    gain_one, shift_one, gain_two, shift_two, bias_out,
+    lengths, attn_shard, up_shard, down_shard, tokens, cotangent, bias_in,
+    gain_one, shift_one, gain_two, shift_two, bias_out, bias_down,
     w_attn_out, w_up_out, w_down, tokens_out, grad_out, mask_out, first_out, second_out, joined_out,
-    heads_out, totals_out, middle_out, hidden_out, slope_out,
-    w_attn, w_up, tok, first, second, joined, heads, middle, send_rows, got_rows, hidden, slope,
-    mask, totals, bias, send_sem, recv_sem, local_sem,
+    heads_out, totals_out, middle_out, hidden_out, slope_out, layer_own_out, layer_other_out,
+    w_attn, w_up, tok, first, second, joined, heads, middle, send_rows, got_rows, layer_other, slope,
+    mask_own, mask, totals, bias, params, send_sem, recv_sem, local_sem,
 ):
     dp, z = lax.axis_index("dp"), lax.axis_index("tensor")
     core, plane = lax.rem(dp, 2), lax.div(dp, 2)
@@ -242,6 +254,9 @@
     plane_y = (1 - y_bit) * 2 + x_bit
     plane_xy = (1 - y_bit) * 2 + 1 - x_bit
     turn = [lax.rem(z + TURNS - k, TURNS) for k in range(TURNS)]
+    base = pl.multiple_of(core * half, 256)
+    other = pl.multiple_of((1 - core) * half, 256)
+    own_rows, other_rows = pl.ds(base, half), pl.ds(other, half)
 
     barrier = pltpu.get_barrier_semaphore()
     partners = [to_x, to_y, to_core, to_clip] + to_z[1:]
@@ -259,161 +274,228 @@
             device_id_type=pl.DeviceIdType.MESH,
         )
 
-    sent = []
+    sent = {}
 
     def send(source, target, sem, device):
         copy = remote(source, target, sem, device)
         copy.start()
-        sent.append(copy)
+        sent[sem] = copy
+        return copy
 
     def arrived(target, sem):
         remote(target, target, sem, to_core).wait_recv()
 
-    weights = [w_attn, w_up, w_down]
-    shards = [attn_shard, up_shard, down_shard]
-
-    def block(array, k, place):
-        return weights[array].at[
-            pl.ds(pl.multiple_of(place * UNIT, 16), UNIT),
-            pl.ds(pl.multiple_of(turn[k] * SPAN, 128), SPAN),
-        ]
-
-    def own_half(array, which):
-        rows = UNIT // 2
-        return weights[array].at[
-            pl.ds(pl.multiple_of(plane * UNIT + which * rows, 16), rows),
-            pl.ds(pl.multiple_of(z * SPAN, 128), SPAN),
-        ]
-
-    def pair_start(array):
-        send(shards[array].at[1 - core], own_half(array, core), 48 + array, to_core)
-        copy = pltpu.make_async_copy(
-            shards[array].at[core], own_half(array, core), local_sem.at[array]
-        )
-        copy.start()
-        return copy
-
-    def pair_wait(array, copy):
-        copy.wait()
-        arrived(own_half(array, 1 - core), 48 + array)
-
-    def go_plane(array, k):
-        send(block(array, k, plane), block(array, k, plane), 16 * array + 4 + k, to_x)
-        send(block(array, k, plane), block(array, k, plane), 16 * array + 8 + k, to_y)
-
-    def go_line(array):
-        for k in range(1, TURNS):
-            send(block(array, 0, plane), block(array, 0, plane), 16 * array + k, to_z[k])
-
-    def from_line(array, k):
-        arrived(block(array, k, plane), 16 * array + k)
-        go_plane(array, k)
-
-    def forward_on(array, k):
-        if k % 2 == 0:
-            arrived(block(array, k, plane_x), 16 * array + 4 + k)
-            send(block(array, k, plane_x), block(array, k, plane_x), 16 * array + 12 + k, to_y)
-        else:
-            arrived(block(array, k, plane_y), 16 * array + 8 + k)
-            send(block(array, k, plane_y), block(array, k, plane_y), 16 * array + 12 + k, to_x)
-
-    def complete(array, k):
-        if k % 2 == 0:
-            arrived(block(array, k, plane_y), 16 * array + 8 + k)
-        else:
-            arrived(block(array, k, plane_x), 16 * array + 4 + k)
-        arrived(block(array, k, plane_xy), 16 * array + 12 + k)
-
-    pairs = [pair_start(0)]
-    tok_copy = pltpu.make_async_copy(tokens, tok, local_sem.at[3])
-    mask_copy = pltpu.make_async_copy(mask_in, mask, local_sem.at[4])
-    clip_tok = remote(tokens, tok, 51, to_clip)
-    clip_mask = remote(mask_in, mask, 52, to_clip)
-    there = grad_out.at[pl.ds(pl.multiple_of((1 - core) * half, 256), half)]
-    here = grad_out.at[pl.ds(pl.multiple_of(core * half, 256), half)]
-    cot_copy = pltpu.make_async_copy(cotangent, here, local_sem.at[5])
-    clip_cot = remote(cotangent, there, 59, to_clip)
-
-    @pl.when(moves)
-    def _():
-        clip_mask.start()
-        clip_tok.start()
-
-    @pl.when(jnp.logical_not(moves))
-    def _():
-        tok_copy.start()
-        mask_copy.start()
-
-    bias_copy = pltpu.make_async_copy(bias_in, bias.at[z], local_sem.at[6])
-    bias_copy.start()
-    for k in range(1, TURNS):
-        send(bias_in, bias.at[z], 52 + k, to_z[k])
-    pairs += [pair_start(1), pair_start(2)]
-    pair_wait(0, pairs[0])
-    go_plane(0, 0)
-    go_line(0)
-    pair_wait(1, pairs[1])
-    go_plane(1, 0)
-    pair_wait(2, pairs[2])
-
-    @pl.when(moves)
-    def _():
-        clip_mask.wait()
-        clip_tok.wait()
-
-    @pl.when(jnp.logical_not(moves))
-    def _():
-        tok_copy.wait()
-        mask_copy.wait()
-
-    outs = []
+    outs = {}
 
     def put(source, target, sem):
         copy = pltpu.make_async_copy(source, target, local_sem.at[sem])
         copy.start()
-        outs.append(copy)
-        return copy
-
-    put(tok, tokens_out, 7)
-    put(mask, mask_out, 8)
-    base = pl.multiple_of(core * half, 256)
-    other = pl.multiple_of((1 - core) * half, 256)
-
-    def norm_loop(step, _):
-        rows = pl.ds(pl.multiple_of(step * 256, 256), 256)
-        values = tok[rows, :].astype(F32)
-        normed = norm_rows(values, gain_one[...], shift_one[...])
-        first[pl.ds(pl.multiple_of(base + step * 256, 256), 256), :] = normed.astype(BF16)
-        return 0
-
-    lax.fori_loop(0, half // 256, norm_loop, 0)
-    own_rows, other_rows = pl.ds(base, half), pl.ds(other, half)
-    send(first.at[own_rows], first.at[own_rows], 56, to_core)
-    forward_on(0, 0)
-    arrived(first.at[other_rows], 56)
-    put(first, first_out, 9)
-    bias_copy.wait()
-    for k in range(1, TURNS):
-        arrived(bias.at[turn[k]], 52 + k)
-    forward_on(1, 0)
-    for k in range(1, TURNS):
-        from_line(0, k)
-    go_line(1)
-
-    def project(k):
+        outs[sem] = copy
+
+    def done(sem):
+        outs.pop(sem).wait()
+
+    weights = [w_attn, w_up, w_down]
+    shards = [attn_shard, up_shard, down_shard]
+    rows_half = UNIT // 2
+
+    def columns(k):
+        return pl.ds(pl.multiple_of(turn[k] * SPAN, 128), SPAN)
+
+    def block(array, k, where, part=None):
+        if part is None:
+            rows = pl.ds(pl.multiple_of(where * UNIT, 16), UNIT)
+        else:
+            rows = pl.ds(pl.multiple_of(where * UNIT + part * rows_half, 16), rows_half)
+        return weights[array].at[rows, columns(k)]
+
+    def own_piece(array, which):
+        rows = pl.ds(pl.multiple_of(plane * UNIT + which * rows_half, 16), rows_half)
+        return weights[array].at[rows, columns(0)]
+
+    def shard_half(array, which):
+        return shards[array].at[:, pl.ds(pl.multiple_of(which * SPAN, 128), SPAN)]
+
+    pairs = [None] * 3
+
+    def pair_start(array):
+        send(shard_half(array, 1 - core), own_piece(array, core), 72 + array, to_core)
+        copy = pltpu.make_async_copy(
+            shard_half(array, core), own_piece(array, core), local_sem.at[array]
+        )
+        copy.start()
+        pairs[array] = copy
+
+    def pair_wait(array):
+        if pairs[array] is not None:
+            pairs[array].wait()
+            arrived(own_piece(array, 1 - core), 72 + array)
+            pairs[array] = None
+
+    def sem_of(array, kind, k):
+        return array * 24 + kind * 4 + k
+
+    def plane_send(array, k):
+        if k == 0:
+            pair_wait(array)
+        else:
+            arrived(block(array, k, plane), sem_of(array, 0, k))
+        source = block(array, k, plane)
+        send(source, source, sem_of(array, 1, k), to_x)
+        send(source, source, sem_of(array, 2, k), to_y)
+
+    def line_send(array):
+        pair_wait(array)
+        source = block(array, 0, plane)
+        for k in range(1, TURNS):
+            send(source, source, sem_of(array, 0, k), to_z[k])
+
+    def forward_on(array, k):
+        arrived(block(array, k, plane_x), sem_of(array, 1, k))
+        source = block(array, k, plane_x, 0)
+        send(source, source, sem_of(array, 3, k), to_y)
+        arrived(block(array, k, plane_y), sem_of(array, 2, k))
+        source = block(array, k, plane_y, 1)
+        send(source, source, sem_of(array, 4, k), to_x)
+
+    def complete(array, k):
+        for part in range(2):
+            arrived(block(array, k, plane_xy, part), sem_of(array, 3 + part, k))
+
+    there = grad_out.at[other_rows]
+    here = grad_out.at[own_rows]
+    length = lengths[lax.div(z, 2)]
+    frames = lax.broadcasted_iota(jnp.int32, mask_own.shape, 1)
+    mask_own[...] = jnp.where(frames < length, 0.0, -1e30).astype(F32)
+    tok_copy = pltpu.make_async_copy(tokens, tok, local_sem.at[3])
+    mask_copy = pltpu.make_async_copy(mask_own, mask, local_sem.at[4])
+    clip_tok = remote(tokens, tok, 75, to_clip)
+    clip_mask = remote(mask_own, mask, 76, to_clip)
+    cot_copy = pltpu.make_async_copy(send_rows, here, local_sem.at[5])
+    clip_cot = remote(send_rows, there, 77, to_clip)
+    bias_copy = pltpu.make_async_copy(bias_in, bias.at[z], local_sem.at[6])
+    exchange = {}
+    for i, vector in enumerate((gain_one, shift_one, gain_two, shift_two, bias_out, bias_down)):
+        params[i : i + 1, :] = vector[...][None, :]
+
+    def tok_start():
+        @pl.when(moves)
+        def _():
+            clip_mask.start()
+            clip_tok.start()
+
+        @pl.when(jnp.logical_not(moves))
+        def _():
+            tok_copy.start()
+            mask_copy.start()
+
+        bias_copy.start()
+        for k in range(1, TURNS):
+            send(bias_in, bias.at[z], 77 + k, to_z[k])
+        put(cotangent, send_rows, 7)
+
+    def tok_wait():
+        @pl.when(moves)
+        def _():
+            clip_mask.wait()
+            clip_tok.wait()
+
+        @pl.when(jnp.logical_not(moves))
+        def _():
+            tok_copy.wait()
+            mask_copy.wait()
+
+        put(tok, tokens_out, 8)
+        put(mask, mask_out, 9)
+
+    def cot_start():
+        done(7)
+
+        def step_rows(step, _):
+            rows = pl.ds(pl.multiple_of(step * 256, 256), 256)
+            at = lax.broadcasted_iota(jnp.int32, (256, send_rows.shape[1]), 0)
+            at = at + (lax.rem(z, 2) * half + step * 256)
+            values = jnp.where(at < length, send_rows[rows, :].astype(F32), 0.0)
+            send_rows[rows, :] = values.astype(BF16)
+            return 0
+
+        lax.fori_loop(0, half // 256, step_rows, 0)
+
+        @pl.when(moves)
+        def _():
+            clip_cot.start()
+
+        @pl.when(jnp.logical_not(moves))
+        def _():
+            cot_copy.start()
+
+    def cot_pair():
+        @pl.when(moves)
+        def _():
+            arrived(here, 77)
+
+        send(here, here, 81, to_core)
+
+    def cot_wait():
+        arrived(there, 81)
+
+    def norm():
+        def step_rows(step, _):
+            rows = pl.ds(pl.multiple_of(step * 256, 256), 256)
+            values = tok[rows, :].astype(F32)
+            normed = norm_rows(values, params[0:1, :], params[1:2, :])
+            first[pl.ds(pl.multiple_of(base + step * 256, 256), 256), :] = normed.astype(BF16)
+            return 0
+
+        lax.fori_loop(0, half // 256, step_rows, 0)
+
+    def hand(name):
+        if name == "a":
+            exchange[name] = send(first.at[own_rows], first.at[own_rows], 82, to_core)
+        elif name == "b":
+            exchange[name] = send(send_rows, got_rows, 83, to_core)
+        else:
+            exchange[name] = send(second.at[own_rows], second.at[own_rows], 84, to_core)
+
+    def take(name):
+        if name == "a":
+            arrived(first.at[other_rows], 82)
+            put(first, first_out, 10)
+            bias_copy.wait()
+            for k in range(1, TURNS):
+                arrived(bias.at[turn[k]], 77 + k)
+        elif name == "b":
+            arrived(got_rows, 83)
+        else:
+            arrived(second.at[other_rows], 84)
+            put(second, second_out, 11)
+
+    steps_done = {"proj": 0, "att": 0, "lift": 0, "down": 0}
+
+    def count_step(name):
+        steps_done[name] += 1
+        return steps_done[name] - 1
+
+    def proj():
+        k = count_step("proj")
         complete(0, k)
-        columns = pl.ds(pl.multiple_of(turn[k] * SPAN, 128), 480)
+        slab = pl.ds(pl.multiple_of(turn[k] * SPAN, 128), 480)
 
         def step_rows(step, _):
             rows = pl.ds(pl.multiple_of(step * half, half), half)
-            product = dot_nn(first[rows, :], w_attn[:, columns]) + bias[turn[k], 0:1, :480]
+            product = dot_nn(first[rows, :], w_attn[:, slab]) + bias[turn[k], 0:1, :480]
             joined[k, rows, :480] = product.astype(BF16)
             return 0
 
         lax.fori_loop(0, 2, step_rows, 0)
-        put(joined.at[k], joined_out.at[turn[k]], 10 + k)
-
-    def attention(k, part):
+        put(joined.at[k], joined_out.at[turn[k]], 12 + k)
+        if k == TURNS - 1:
+            put(w_attn, w_attn_out, 24)
+
+    def att():
+        step_at = count_step("att")
+        k, part = step_at // 2, step_at % 2
+
         def step_rows(step, _):
             rows = pl.ds(pl.multiple_of(step * 256, 256), 256)
             queries = joined[k, rows, :160]
@@ -437,156 +519,143 @@
 
         lax.fori_loop(3 * part, 3 * part + 3, step_rows, 0)
         if part == 1:
-            put(heads.at[k], heads_out.at[turn[k]], 14 + k)
-            put(totals.at[k], totals_out.at[turn[k]], 18 + k)
-
-    project(0)
-    attention(0, 0)
-    forward_on(0, 1)
-    attention(0, 1)
-    forward_on(0, 2)
-    forward_on(0, 3)
-    project(1)
-    attention(1, 0)
-    for k in range(1, TURNS):
-        from_line(1, k)
-    go_plane(2, 0)
-    go_line(2)
-
-    @pl.when(moves)
-    def _():
-        clip_cot.start()
-
-    @pl.when(jnp.logical_not(moves))
-    def _():
-        cot_copy.start()
-
-    attention(1, 1)
-    project(2)
-    attention(2, 0)
-    forward_on(1, 1)
-    forward_on(1, 2)
-    attention(2, 1)
-    forward_on(1, 3)
-    project(3)
-    put(w_attn, w_attn_out, 22)
-    attention(3, 0)
-    forward_on(2, 0)
-    attention(3, 1)
+            put(heads.at[k], heads_out.at[turn[k]], 16 + k)
+            put(totals.at[k], totals_out.at[turn[k]], 20 + k)
 
     def branch(rows):
         total = None
         for k in range(TURNS):
-            columns = pl.ds(pl.multiple_of(turn[k] * SPAN + 384, 128), 256)
-            product = dot_nt(heads[k, rows, :], w_attn[:, columns])
+            slab = pl.ds(pl.multiple_of(turn[k] * SPAN + 384, 128), 256)
+            product = dot_nt(heads[k, rows, :], w_attn[:, slab])
             total = product if total is None else total + product
         return total
 
-    def branch_other(step, _):
-        rows = pl.ds(pl.multiple_of(other + step * 256, 256), 256)
-        send_rows[pl.ds(pl.multiple_of(step * 256, 256), 256), :] = branch(rows).astype(BF16)
-        return 0
-
-    lax.fori_loop(0, half // 256, branch_other, 0)
-    send(send_rows, got_rows, 57, to_core)
-    for k in range(1, TURNS):
-        from_line(2, k)
-
-    def branch_own(step, _):
-        rows = pl.ds(pl.multiple_of(base + step * 256, 256), 256)
-        low = pl.ds(pl.multiple_of(step * 256, 256), 256)
-        middle[low, :] = branch(rows) + tok[low, :].astype(F32) + bias_out[...]
-        return 0
-
-    lax.fori_loop(0, half // 256, branch_own, 0)
-    arrived(got_rows, 57)
-
-    def norm_two(step, _):
-        low = pl.ds(pl.multiple_of(step * 256, 256), 256)
-        values = middle[low, :] + got_rows[low, :].astype(F32)
-        middle[low, :] = values
-        normed = norm_rows(values, gain_two[...], shift_two[...])
-        second[pl.ds(pl.multiple_of(base + step * 256, 256), 256), :] = normed.astype(BF16)
-        return 0
-
-    lax.fori_loop(0, half // 256, norm_two, 0)
-    send(second.at[own_rows], second.at[own_rows], 58, to_core)
-    put(middle, middle_out, 23)
-    forward_on(2, 1)
-    arrived(second.at[other_rows], 58)
-    put(second, second_out, 24)
-
-    waits = [None, None]
-
-    def lift(k):
+    def both():
+        @pl.when(moves)
+        def _():
+            clip_cot.wait_send()
+
+        @pl.when(jnp.logical_not(moves))
+        def _():
+            cot_copy.wait()
+
+        def step_rows(step, _):
+            rows = pl.ds(pl.multiple_of(other + step * 256, 256), 256)
+            low = pl.ds(pl.multiple_of(step * 256, 256), 256)
+            send_rows[low, :] = branch(rows).astype(BF16)
+            return 0
+
+        lax.fori_loop(0, half // 256, step_rows, 0)
+
+    def bown():
+        def step_rows(step, _):
+            rows = pl.ds(pl.multiple_of(base + step * 256, 256), 256)
+            low = pl.ds(pl.multiple_of(step * 256, 256), 256)
+            middle[low, :] = branch(rows) + tok[low, :].astype(F32) + params[4:5, :]
+            return 0
+
+        lax.fori_loop(0, half // 256, step_rows, 0)
+
+    def ntwo():
+        def step_rows(step, _):
+            low = pl.ds(pl.multiple_of(step * 256, 256), 256)
+            values = middle[low, :] + got_rows[low, :].astype(F32)
+            middle[low, :] = values
+            normed = norm_rows(values, params[2:3, :], params[3:4, :])
+            second[pl.ds(pl.multiple_of(base + step * 256, 256), 256), :] = normed.astype(BF16)
+            return 0
+
+        lax.fori_loop(0, half // 256, step_rows, 0)
+        put(middle, middle_out, 25)
+
+    def lift():
+        k = count_step("lift")
         complete(1, k)
-        slot = k % 2
-        if waits[slot] is not None:
-            for copy in waits[slot]:
-                copy.wait()
-        columns = pl.ds(pl.multiple_of(turn[k] * SPAN, 128), SPAN)
+        if k == 0:
+            for sem in range(12, 16):
+                done(sem)
+        if k >= 2:
+            done(28 + k % 2)
 
         def step_rows(step, _):
             rows = pl.ds(pl.multiple_of(step * 256, 256), 256)
-            pre = dot_nn(second[rows, :], w_up[:, columns]) + bias[turn[k], 1:2, :]
+            pre = dot_nn(second[rows, :], w_up[:, columns(k)]) + bias[turn[k], 1:2, :]
             cdf = 0.5 * lax.erf(pre * (0.5**0.5)) + 0.5
             density = jnp.exp(-0.5 * pre * pre) * 0.3989422804014327
-            hidden[slot, rows, :] = (pre * cdf).astype(BF16)
-            slope[slot, rows, :] = (cdf + pre * density).astype(BF16)
+            joined[k, rows, :] = (pre * cdf).astype(BF16)
+            slope[k % 2, rows, :] = (cdf + pre * density).astype(BF16)
             return 0
 
         lax.fori_loop(0, count // 256, step_rows, 0)
-        waits[slot] = [
-            put(hidden.at[slot], hidden_out.at[:, columns], 25 + slot),
-            put(slope.at[slot], slope_out.at[:, columns], 27 + slot),
-        ]
-        for _ in range(2):
-            outs.pop()
-
-    lift(0)
-    forward_on(2, 2)
-    lift(1)
-    forward_on(2, 3)
-    lift(2)
-    lift(3)
-    put(w_up, w_up_out, 29)
-
-    @pl.when(moves)
-    def _():
-        clip_cot.wait_send()
-        arrived(here, 59)
-
-    @pl.when(jnp.logical_not(moves))
-    def _():
-        cot_copy.wait()
-
-    send(here, here, 60, to_core)
-    for k in range(TURNS):
+        put(joined.at[k], hidden_out.at[:, columns(k)], 12 + k)
+        put(slope.at[k % 2], slope_out.at[:, columns(k)], 28 + k % 2)
+        if k == TURNS - 1:
+            put(w_up, w_up_out, 30)
+
+    def down():
+        k = count_step("down")
         complete(2, k)
-    arrived(there, 60)
-    for copy in outs + waits[0] + waits[1]:
-        copy.wait()
-    for copy in sent:
+        if k == 0:
+            done(24)
+            done(25)
+            for sem in [83] + [sem for sem in sent if sem < 24]:
+                sent.pop(sem).wait_send()
+        slab = pltpu.make_async_copy(w_down.at[:, columns(k)], w_attn.at[:, columns(k)], local_sem.at[31])
+        slab.start()
+        slab.wait()
+
+        def step_rows(step, _):
+            low = pl.ds(pl.multiple_of(step * 256, 256), 256)
+            own = pl.ds(pl.multiple_of(base + step * 256, 256), 256)
+            away = pl.ds(pl.multiple_of(other + step * 256, 256), 256)
+            mine = dot_nt(joined[k, own, :], w_attn[:, columns(k)])
+            yours = dot_nt(joined[k, away, :], w_attn[:, columns(k)])
+            if k == 0:
+                mine = mine + params[5:6, :]
+                layer_other[low, :] = yours
+            elif k < TURNS - 1:
+                layer_other[low, :] += yours
+            else:
+                send_rows[low, :] = (layer_other[low, :] + yours).astype(BF16)
+            middle[low, :] += mine
+            return 0
+
+        lax.fori_loop(0, half // 256, step_rows, 0)
+        if k == TURNS - 1:
+            put(middle, layer_own_out, 26)
+            put(send_rows, layer_other_out, 27)
+
+    actions = {
+        "pr": pair_start, "pp": plane_send, "zz": line_send, "fw": forward_on, "tok": tok_start,
+        "tokw": tok_wait, "cot": cot_start, "cotx": cot_pair, "cotw": cot_wait, "norm": norm, "send": hand,
+        "wait": take, "proj": proj, "att": att, "both": both, "bown": bown, "ntwo": ntwo, "lift": lift,
+        "down": down,
+    }
+    for name, *numbers in FORWARD_STEPS:
+        actions[name](*numbers)
+    for sem in sorted(outs):
+        outs[sem].wait()
+    for copy in sent.values():
         copy.wait_send()
 
 
-def forward_pass(
-    shards, tokens, cotangent, mask, bias, gain_one, shift_one, gain_two, shift_two, bias_out
-):
+def forward_pass(lengths, shards, tokens, cotangent, bias, vectors):
     half, features = tokens.shape
     count = 2 * half
     any_space = pl.BlockSpec(memory_space=pl.ANY)
     vmem = pl.BlockSpec(memory_space=pltpu.VMEM)
+    smem = pl.BlockSpec(memory_space=pltpu.SMEM)
     wide = (features, TURNS * SPAN)
     shapes = [
         (wide, BF16), (wide, BF16), (wide, BF16), ((half, features), BF16), ((count, features), BF16),
         ((8, count), F32), ((count, features), BF16), ((count, features), BF16),
         ((TURNS, count, SPAN), BF16), ((TURNS, count, 256), BF16), ((TURNS, 8, count), F32),
         ((half, features), F32), ((count, TURNS * SPAN), BF16), ((count, TURNS * SPAN), BF16),
+        ((half, features), F32), ((half, features), BF16),
     ]
     return pl.pallas_call(
         functools.partial(forward_kernel, HDIM ** (-0.5)),
-        in_specs=[any_space] * 7 + [vmem] * 5,
+        in_specs=[smem] + [any_space] * 6 + [vmem] * 6,
         out_specs=[any_space] * len(shapes),
         out_shape=[jax.ShapeDtypeStruct(shape, kind) for shape, kind in shapes],
         scratch_shapes=[
@@ -600,46 +669,48 @@
             pltpu.VMEM((half, features), F32),
             pltpu.VMEM((half, features), BF16),
             pltpu.VMEM((half, features), BF16),
+            pltpu.VMEM((half, features), F32),
             pltpu.VMEM((2, count, SPAN), BF16),
-            pltpu.VMEM((2, count, SPAN), BF16),
+            pltpu.VMEM((8, count), F32),
             pltpu.VMEM((8, count), F32),
             pltpu.VMEM((TURNS, 8, count), F32),
             pltpu.VMEM((TURNS, 8, SPAN), F32),
-            pltpu.SemaphoreType.DMA((64,)),
-            pltpu.SemaphoreType.DMA((64,)),
+            pltpu.VMEM((8, features), F32),
+            pltpu.SemaphoreType.DMA((88,)),
+            pltpu.SemaphoreType.DMA((88,)),
             pltpu.SemaphoreType.DMA((32,)),
         ],
         cost_estimate=pl.CostEstimate(
-            flops=2 * count * features * 6400, bytes_accessed=80_000_000, transcendentals=30_000_000
+            flops=2 * count * features * 9000, bytes_accessed=90_000_000, transcendentals=30_000_000
         ),
         compiler_params=pltpu.CompilerParams(
             vmem_limit_bytes=60 << 20, collective_id=0, has_side_effects=True
         ),
         name="forward_pass",
-    )(*shards, tokens, cotangent, mask, bias, gain_one, shift_one, gain_two, shift_two, bias_out)
+    )(lengths, *shards, tokens, cotangent, bias, *vectors)
 
 
 BACKWARD_STEPS = (
-    ("load",), ("P", 0, 0), ("pre",), ("P", 0, 1), ("pre",), ("pre",), ("pre",), ("2", 0, 0), ("soth",),
-    ("send", "a"), ("P", 0, 2), ("P", 0, 3), ("wait", "a"), ("ntwo",), ("send", "b"), ("3", 0, 0),
-    ("2", 0, 1), ("2", 0, 2), ("P", 1, 0), ("wait", "b"), ("hb",), ("att",), ("3", 0, 1), ("2", 0, 3),
-    ("att",), ("P", 1, 1), ("att",), ("3", 0, 3), ("3", 0, 2), ("aend",), ("P", 1, 2), ("hb",), ("2", 1, 0),
-    ("att",), ("2", 1, 1), ("att",), ("P", 1, 3), ("2", 1, 2), ("F", 0), ("att",), ("aend",), ("3", 1, 1),
-    ("3", 1, 0), ("P", 2, 0), ("2", 1, 3), ("P", 2, 1), ("hb",), ("3", 1, 2), ("att",), ("G", 0), ("att",),
-    ("att",), ("3", 1, 3), ("aend",), ("P", 2, 2), ("2", 2, 1), ("hb",), ("att",), ("F", 1), ("att",),
-    ("3", 2, 1), ("2", 2, 2), ("att",), ("aend",), ("3", 2, 2), ("foth",), ("send", "c"), ("P", 2, 3),
-    ("tok",), ("2", 2, 0), ("wait", "c"), ("none",), ("reloc",), ("none",), ("2", 2, 3), ("reloc",),
-    ("none",), ("hs", "c"), ("G", 1), ("3", 2, 0), ("hw", "c"), ("hs", "x"), ("hw", "x"), ("hs", "y"),
-    ("3", 2, 3), ("hw", "y"), ("hs", "z1"), ("reloc",), ("F", 2), ("hw", "z1"), ("hs", "z2"), ("wreloc",),
-    ("G", 2), ("hw", "z2"),
+    ("load",), ("P", 0, 0), ("pre",), ("layer", 0), ("P", 0, 1), ("pre",), ("layer", 1), ("pre",),
+    ("layer", 2), ("pre",), ("2", 0, 0), ("soth",), ("send", "a"), ("P", 0, 2), ("P", 0, 3), ("wait", "a"),
+    ("ntwo",), ("send", "b"), ("3", 0, 0), ("2", 0, 1), ("2", 0, 2), ("P", 1, 0), ("wait", "b"), ("hb",),
+    ("att",), ("3", 0, 1), ("2", 0, 3), ("att",), ("P", 1, 1), ("att",), ("3", 0, 3), ("3", 0, 2),
+    ("aend",), ("P", 1, 2), ("hb",), ("2", 1, 0), ("att",), ("2", 1, 1), ("att",), ("P", 1, 3), ("2", 1, 2),
+    ("F", 0), ("att",), ("aend",), ("3", 1, 1), ("3", 1, 0), ("P", 2, 0), ("2", 1, 3), ("P", 2, 1), ("hb",),
+    ("3", 1, 2), ("att",), ("G", 0), ("att",), ("att",), ("3", 1, 3), ("aend",), ("P", 2, 2), ("2", 2, 1),
+    ("hb",), ("att",), ("F", 1), ("att",), ("3", 2, 1), ("2", 2, 2), ("att",), ("aend",), ("3", 2, 2),
+    ("foth",), ("send", "c"), ("P", 2, 3), ("tok",), ("2", 2, 0), ("wait", "c"), ("none",), ("reloc",),
+    ("none",), ("2", 2, 3), ("reloc",), ("none",), ("hs", "c"), ("G", 1), ("3", 2, 0), ("hw", "c"),
+    ("hs", "x"), ("hw", "x"), ("hs", "y"), ("3", 2, 3), ("hw", "y"), ("hs", "z1"), ("reloc",), ("F", 2),
+    ("hw", "z1"), ("hs", "z2"), ("wreloc",), ("G", 2), ("hw", "z2"), ("layer", 3),
 )
 
 
 def backward_kernel(
     scaling,
     w_attn_in, w_up_in, w_down_in, tok_in, grad_in, first_in, second_in, joined_in, heads_in, middle_in,
-    hidden_in, slope_in, totals_in, key_mask, gain_one, gain_two,
-    tokens_out, down_out, up_out, attn_out, sums_out, pre_out,
+    hidden_in, slope_in, totals_in, layer_own_in, layer_other_in, key_mask, gain_one, gain_two,
+    tokens_out, down_out, up_out, attn_out, sums_out, pre_out, layer_out, layer_got, layer_low,
     weight, grad, left, wide, right, grad_heads, totals, middle, send_rows, got_rows, key_sum, value_sum,
     product, near_got, far_got, turn_got, line_got, line_own, final, final_got, sums, sums_got,
     send_sem, recv_sem, local_sem, credit,
@@ -713,7 +784,8 @@
         slope_loads.append(local(slope_in.at[:, columns(k)], wide.at[:, columns(k)], 7 + k))
     right_loads[1] = load_right(hidden_in, 1, 1)
     left_load = local(second_in, left, 11)
-    middle_load = local(middle_in, middle, 12)
+    layer_sent = send(layer_other_in, layer_got, 98, to_core)
+    layer_load = local(layer_own_in, middle, 12)
     totals_loads = [local(totals_in.at[turn[k]], totals.at[k], 21 + k) for k in range(TURNS)]
     sums[...] = jnp.zeros_like(sums)
 
@@ -874,13 +946,13 @@
     zero = jnp.zeros((1, features), F32)
 
     def ntwo():
-        middle_load.wait()
+        loads["middle"].wait()
 
         def step_rows(step, total):
             low = pl.ds(pl.multiple_of(step * 256, 256), 256)
             rows = pl.ds(pl.multiple_of(base + step * 256, 256), 256)
             above = second_part(rows) + got_rows[low, :].astype(F32)
-            back, by_gain, by_shift = norm_back_rows(middle[low, :], gain_two[...], above)
+            back, by_gain, by_shift = norm_back_rows(middle[low, :], gain_two[...][None, :], above)
             out_grad = grad[rows, :].astype(F32)
             below = out_grad + back
             middle[low, :] = below
@@ -1065,7 +1137,7 @@
         rows = pl.ds(pl.multiple_of(base + step * 256, 256), 256)
         above = first_part(rows) + got_rows[low, :].astype(F32)
         values = got_tok[low, :].astype(F32)
-        back, by_gain, by_shift = norm_back_rows(values, gain_one[...], above)
+        back, by_gain, by_shift = norm_back_rows(values, gain_one[...][None, :], above)
         grad[half + step * 256 : half + step * 256 + 256, :] = (middle[low, :] + back).astype(BF16)
         if step == 0:
             sums[4, :, :] = by_gain
@@ -1119,6 +1191,46 @@
         arrived(sums_got.at[index], 93 + index)
         sums[...] = sums[...] + sums_got[index]
 
+    layer_away = remote(layer_low, layer_out, 99, to_clip)
+    layer_here = pltpu.make_async_copy(layer_low, layer_out, local_sem.at[30])
+
+    def layer(stage):
+        if stage == 0:
+            arrived(layer_got, 98)
+            loads["layer"] = local(layer_got, send_rows, 28)
+        elif stage == 1:
+            layer_load.wait()
+            loads["layer"].wait()
+
+            def step_rows(step, _):
+                rows = pl.ds(pl.multiple_of(step * 256, 256), 256)
+                send_rows[rows, :] = (middle[rows, :] + send_rows[rows, :].astype(F32)).astype(BF16)
+                return 0
+
+            lax.fori_loop(0, half // 256, step_rows, 0)
+            loads["layer"] = local(send_rows, layer_low, 29)
+            loads["middle"] = local(middle_in, middle, 12)
+        elif stage == 2:
+            loads["layer"].wait()
+
+            @pl.when(moves)
+            def _():
+                layer_away.start()
+
+            @pl.when(jnp.logical_not(moves))
+            def _():
+                layer_here.start()
+        else:
+            layer_sent.wait_send()
+
+            @pl.when(moves)
+            def _():
+                layer_away.wait()
+
+            @pl.when(jnp.logical_not(moves))
+            def _():
+                layer_here.wait()
+
     def token_load():
         exchange["b"].wait_send()
         loads["tok"] = local(tok_in, grad.at[0:half], 2)
@@ -1127,7 +1239,7 @@
         "load": load, "pre": pre, "soth": soth, "ntwo": ntwo, "hb": hb, "att": att, "aend": aend,
         "foth": foth, "none": none, "reloc": reloc, "wreloc": wreloc, "send": hand, "wait": take,
         "P": produce, "2": stage_two, "3": stage_three, "F": final_one, "G": final_two, "hs": hs, "hw": hw,
-        "tok": token_load,
+        "tok": token_load, "layer": layer,
     }
     for name, *numbers in BACKWARD_STEPS:
         actions[name](*numbers)
@@ -1141,8 +1253,8 @@
 
 
 def backward_pass(
-    w_attn, w_up, w_down, tok, grad, first, second, joined, heads, middle, hidden, slope, totals, key_mask,
-    gain_one, gain_two,
+    w_attn, w_up, w_down, tok, grad, first, second, joined, heads, middle, hidden, slope, totals, layer_own,
+    layer_other, key_mask, gain_one, gain_two,
 ):
     half, features = tok.shape
     count = 2 * half
@@ -1152,10 +1264,11 @@
     shapes = [
         ((half, features), BF16), ((UNIT // 2, 2 * SPAN), F32), ((UNIT // 2, 2 * SPAN), F32),
         ((UNIT // 2, 2 * SPAN), F32), ((24, 1, features), F32), ((count, cols), BF16),
+        ((half, features), BF16), ((half, features), BF16), ((half, features), BF16),
     ]
     return pl.pallas_call(
         functools.partial(backward_kernel, HDIM ** (-0.5)),
-        in_specs=[any_space] * 13 + [vmem] * 3,
+        in_specs=[any_space] * 15 + [vmem] * 3,
         out_specs=[any_space] * len(shapes),
         out_shape=[jax.ShapeDtypeStruct(shape, kind) for shape, kind in shapes],
         scratch_shapes=[
@@ -1195,7 +1308,7 @@
         name="backward_pass",
     )(
         w_attn, w_up, w_down, tok, grad, first, second, joined, heads, middle, hidden, slope, totals,
-        key_mask, gain_one, gain_two,
+        layer_own, layer_other, key_mask, gain_one, gain_two,
     )
 
 
@@ -1416,60 +1529,32 @@
     down_weight,
     down_bias,
 ):
-    dp, z = lax.axis_index("dp"), lax.axis_index("tensor")
-    core, plane = dp % 2, dp // 2
-    half = tokens.shape[0]
-    count = 2 * half
+    core, z = lax.axis_index("dp") % 2, lax.axis_index("tensor")
     width, units = 160, SPAN
-
-    def split(weight):
-        return jnp.moveaxis(halves_of(weight), 1, 0)
-
+    parts = (query_weight, key_weight, value_weight, out_weight.T)
     shards = (
-        jnp.concatenate([split(w) for w in (query_weight, key_weight, value_weight, out_weight.T)], -1),
-        split(up_weight),
-        split(down_weight.T),
+        jnp.concatenate([w[:, i * width : (i + 1) * width] for i in range(2) for w in parts], 1),
+        up_weight,
+        down_weight.T,
     )
-    place = jnp.sum(jnp.where(jnp.arange(lengths.shape[0]) == z // 2, lengths, 0))
-    mask = jnp.where(jnp.arange(count) < place, 0.0, -1e30).astype(F32)
-    mask = jnp.broadcast_to(mask[None, :], (8, count))
-    valid = ((z % 2) * half + jnp.arange(half) < place).astype(BF16)
-    small = [query_bias.reshape(2, width), jnp.zeros((2, width), F32), value_bias.reshape(2, width)]
-    small = jnp.concatenate(small + [jnp.zeros((2, width), F32)], -1)
-    small = jnp.stack([small, up_bias.reshape(2, units)], 1)
-    small = jnp.pad(jnp.where(core == 0, small[0], small[1]), ((0, 6), (0, 0)))
+
+    def half_of(vector):
+        size = vector.shape[0] // 2
+        return jnp.where(core == 0, vector[:size], vector[size:])
+
+    gap = jnp.zeros((width,), F32)
+    small = [half_of(query_bias), gap, half_of(value_bias), gap, half_of(up_bias)]
+    small = jnp.concatenate(small + [jnp.zeros((6 * SPAN,), F32)]).reshape(8, SPAN)
+    vectors = (norm1_gain, norm1_shift, norm2_gain, norm2_shift, out_bias, down_bias)
     (
         w_attn, w_up, w_down, tok, out_grad, mask, first, second, joined, heads, totals, middle, hidden,
-        slope,
-    ) = forward_pass(
-        shards, tokens, cotangent * valid[:, None], mask, small,
-        norm1_gain[None, :], norm1_shift[None, :], norm2_gain[None, :], norm2_shift[None, :],
-        out_bias[None, :],
-    )
-
-    def pair(value):
-        return lax.ppermute(value, "dp", [(i, i ^ 1) for i in range(8)])
-
-    def move_rows(value):
-        swaps = [
-            (a * 4 + b, (a ^ 1) * 4 + (b ^ 1)) for a in range(8) for b in range(4) if a % 2 != b % 2
-        ]
-        moved = lax.ppermute(value, ("dp", "tensor"), swaps)
-        return jnp.where(core == z % 2, value, moved)
-
-    def part_of(value, part):
-        start = (core if part == 0 else 1 - core) * half
-        return lax.dynamic_slice_in_dim(value, start, half, 0)
-
-    got = pair(dot_nt(part_of(hidden, 1), w_down).astype(BF16))
-    layer_out = middle + dot_nt(part_of(hidden, 0), w_down) + got.astype(F32) + down_bias
-    layer_out = move_rows(layer_out.astype(BF16))
-
+        slope, layer_own, layer_other,
+    ) = forward_pass(lengths, shards, tokens, cotangent, small, vectors)
     lane = jnp.arange(128)[None, :] == 0
     key_mask = jnp.where(lane, mask[0][:, None], 0.0).astype(BF16)
-    grad_tokens, grad_down, grad_up, grad_attn, sums, _ = backward_pass(
+    grad_tokens, grad_down, grad_up, grad_attn, sums, _, layer_out, _, _ = backward_pass(
         w_attn, w_up, w_down, tok, out_grad, first, second, joined, heads, middle, hidden, slope, totals,
-        key_mask, norm1_gain[None, :], norm2_gain[None, :],
+        layer_own, layer_other, key_mask, norm1_gain, norm2_gain,
     )
 
     def piece(index):

time: 509 us -> 472 us (0.927)
  matrix products: 19.3 us -> 0 us
  other arithmetic: 14.1 us -> 5.85 us
  local copies, waits for them, and re-layouts: 25 us -> 17.2 us
    dot_general x2 -> x0, matrix products: 19.3 us -> none  [dot_nt(): lax.dot_general(left, right, (((1,), (1,)), ((), ())), preferred_element_...]
    broadcast_in_dim x6 -> x2, local copies, waits for them, and re-layouts: 7.09 us -> 0.01 us  [the longest x1 0.01 us: local_chips(): jnp.zeros((6 * SPAN,), F32)]
  transfers between devices with their start and end apart: 2 -> 0, of which waited for: 1 -> 0; matrix products, arithmetic and copies ran while one was open for 2% -> 0% of each run, Pallas kernels for 46% -> 0%
where the time goes in v5:
time: 472 us; the launch traced here: 463 us
  Pallas kernels  439 us (93%)
  local copies, waits for them, and re-layouts  17.2 us (4%)
  other arithmetic  5.85 us (1%)
    pallas_call x1, Pallas kernels, backward_pass(): pl.pallas_call(functools.partial(backward_kernel, HDIM ** (-0.5)), in_spe...  236 us
    pallas_call x1, Pallas kernels, forward_pass(): pl.pallas_call(functools.partial(forward_kernel, HDIM ** (-0.5)), in_spec...  203 us

profile of v5, /device:TPU:1, one launch (start us, length us, event | category | flops | bytes accessed | tf_op | source)
XLA Modules:
  0.0 462.9 jit_solution(8886968722412434785)
XLA Ops:
  0.7 0.8 slice_select_fusion.1
  1.5 0.8 slice_select_fusion
  2.3 0.1 concatenate.19
  2.4 0.6 reshape.54.bias_in
  3.0 1.1 fusion.1
  4.1 1.1 fusion.3
  5.2 1.1 concatenate.18.attn_shard
  6.3 202.7 %forward_pass.1 = (bf16[1280,2560]{1,0:T(8,128)(2,1)}, bf16[1280,2560]{1,0:T(8,128)(2,1)}, bf16[1280,2560]{1,0:T(8,128)(2,1)}, bf16[768,1280]{1,0:T(8,128)(2,1)}...) custom-call(s32[2]{0:T(128)} %lengths.1, ...), custom_call_target="tpu_custom_call" | custom-call | flops 35389440000 | bytes 90000000 | tf_op jit(solution)/shard_map/forward_pass/pallas_call | solution.py:656
  209.0 0.8 slice_reduce_fusion
  209.9 1.0 select_convert_fusion.key_mask
  210.9 236.0 %backward_pass.1 = (bf16[768,1280]{1,0:T(8,128)(2,1)}, f32[160,1280]{1,0:T(8,128)}, f32[160,1280]{1,0:T(8,128)}, f32[160,1280]{1,0:T(8,128)}, f32[24,1,1280]{2,1...) custom-call(bf16[1280,2560]{1,0:T(8,128)(2,1)} %get-tuple-element.39, ...), custom_call_target="tpu_custom_call" | custom-call | flops 50331648000 | bytes 90000000 | tf_op jit(solution)/shard_map/backward_pass/pallas_call | solution.py:1269
  446.9 0.0 copy-start
  446.9 2.0 fusion
  448.9 0.8 maximum_bitcast_fusion
  449.7 0.8 pad_maximum_fusion.2
  450.5 0.8 pad_maximum_fusion.1
  451.3 0.8 pad_maximum_fusion
  452.1 0.7 constant_dynamic-slice_fusion
  452.9 0.6 reshape.57
  453.5 0.1 fusion.5
  453.5 0.7 reshape.55
  454.2 0.7 reshape.56
  454.9 1.5 slice_reduce_fusion.1
  456.3 0.0 copy-start.2
  456.3 0.0 copy-start.1
  456.3 3.1 copy.45
  459.4 0.0 copy-done
  459.4 1.3 copy.46
  460.7 0.0 copy-done.2
  460.7 0.9 copy.47
  461.6 0.0 copy-done.1
  461.6 0.9 copy.48
  (6 shorter events, 0.0 us)
Async XLA Ops:
  446.9 12.5 %copy-start = (bf16[768,1280]{1,0:T(8,128)(2,1)S(1)}, bf16[768,1280]{1,0:T(8,128)(2,1)}, u32[]{:S(2)}) copy-start(bf16[768,1280]{1,0:T(8,128)(2,1)} %get-tuple-element.111) | copy-start | bytes 5898244
  456.3 4.3 copy-start.2
  456.3 5.2 %copy-start.1 = (f32[160,1280]{1,0:T(8,128)S(1)}, f32[160,1280]{1,0:T(8,128)}, u32[]{:S(2)}) copy-start(f32[160,1280]{1,0:T(8,128)} %get-tuple-element.60) | copy-start | bytes 2457604

commit v6 on v5

--- a/solution.py
+++ b/solution.py
@@ -232,12 +232,12 @@
 
 def forward_kernel(
     scaling,
-    lengths, attn_shard, up_shard, down_shard, tokens, cotangent, bias_in,
-    gain_one, shift_one, gain_two, shift_two, bias_out, bias_down,
+    lengths, up_shard, down_shard, tokens, cotangent, query_weight, key_weight, value_weight, out_weight,
+    query_bias, value_bias, up_bias, gain_one, shift_one, gain_two, shift_two, bias_out, bias_down,
     w_attn_out, w_up_out, w_down, tokens_out, grad_out, mask_out, first_out, second_out, joined_out,
     heads_out, totals_out, middle_out, hidden_out, slope_out, layer_own_out, layer_other_out,
     w_attn, w_up, tok, first, second, joined, heads, middle, send_rows, got_rows, layer_other, slope,
-    mask_own, mask, totals, bias, params, send_sem, recv_sem, local_sem,
+    mask_own, mask, totals, bias, params, attn_shard, bias_in, send_sem, recv_sem, local_sem,
 ):
     dp, z = lax.axis_index("dp"), lax.axis_index("tensor")
     core, plane = lax.rem(dp, 2), lax.div(dp, 2)
@@ -262,6 +262,21 @@
     partners = [to_x, to_y, to_core, to_clip] + to_z[1:]
     for partner in partners:
         pl.semaphore_signal(barrier, inc=1, device_id=partner, device_id_type=pl.DeviceIdType.MESH)
+    width = UNIT // 2
+    parts = [query_weight[...], key_weight[...], value_weight[...], out_weight[...]]
+    pieces = [part[:, i * width : (i + 1) * width] for i in range(2) for part in parts]
+    attn_shard[...] = jnp.concatenate(pieces, -1)
+
+    def half_of(vector):
+        row = vector[...][None, :]
+        size = row.shape[1] // 2
+        return jnp.where(core == 0, row[:, :size], row[:, size:])
+
+    gap = jnp.zeros((1, width), F32)
+    bias_in[...] = jnp.zeros_like(bias_in)
+    bias_in[0:1, :] = jnp.concatenate([half_of(query_bias), gap, half_of(value_bias), gap], -1)
+    bias_in[1:2, :] = half_of(up_bias)
+
     pl.semaphore_wait(barrier, len(partners))
 
     def remote(source, target, sem, device):
@@ -639,7 +654,7 @@
         copy.wait_send()
 
 
-def forward_pass(lengths, shards, tokens, cotangent, bias, vectors):
+def forward_pass(lengths, shards, tokens, cotangent, weights, vectors):
     half, features = tokens.shape
     count = 2 * half
     any_space = pl.BlockSpec(memory_space=pl.ANY)
@@ -655,7 +670,7 @@
     ]
     return pl.pallas_call(
         functools.partial(forward_kernel, HDIM ** (-0.5)),
-        in_specs=[smem] + [any_space] * 6 + [vmem] * 6,
+        in_specs=[smem] + [any_space] * 4 + [vmem] * 13,
         out_specs=[any_space] * len(shapes),
         out_shape=[jax.ShapeDtypeStruct(shape, kind) for shape, kind in shapes],
         scratch_shapes=[
@@ -676,6 +691,8 @@
             pltpu.VMEM((TURNS, 8, count), F32),
             pltpu.VMEM((TURNS, 8, SPAN), F32),
             pltpu.VMEM((8, features), F32),
+            pltpu.VMEM((UNIT // 2, 2 * SPAN), BF16),
+            pltpu.VMEM((8, SPAN), F32),
             pltpu.SemaphoreType.DMA((88,)),
             pltpu.SemaphoreType.DMA((88,)),
             pltpu.SemaphoreType.DMA((32,)),
@@ -687,7 +704,7 @@
             vmem_limit_bytes=60 << 20, collective_id=0, has_side_effects=True
         ),
         name="forward_pass",
-    )(lengths, *shards, tokens, cotangent, bias, *vectors)
+    )(lengths, *shards, tokens, cotangent, *weights, *vectors)
 
 
 BACKWARD_STEPS = (
@@ -1312,6 +1329,48 @@
     )
 
 
+def finish_kernel(*refs):
+    z = lax.axis_index("tensor")
+    large_in, attn, sums = refs[:4], refs[4], refs[5]
+    large_out, grads, vectors, sem = refs[6:10], refs[10:14], refs[14:-1], refs[-1]
+    copies = [
+        pltpu.make_async_copy(source, target, sem.at[i])
+        for i, (source, target) in enumerate(zip(large_in, large_out))
+    ]
+    for copy in copies:
+        copy.start()
+    width = UNIT // 2
+    for i, grad in enumerate(grads):
+        low = i * width
+        halves = [attn[:, half * SPAN + low : half * SPAN + low + width] for half in range(2)]
+        grad[...] = jnp.concatenate(halves, -1)
+    for vector, row, start, size in zip(vectors, (16, 16, 8), (0, width, 0), (width, width, SPAN)):
+        halves = [sums[row + 2 * z + half][:, start : start + size] for half in range(2)]
+        vector[...] = jnp.concatenate(halves, -1)[0]
+    for i, vector in enumerate(vectors[3:]):
+        vector[...] = sums[i][0]
+    for copy in copies:
+        copy.wait()
+
+
+def finish(layer_out, grad_tokens, grad_up, grad_down, grad_attn, sums):
+    features = layer_out.shape[1]
+    any_space = pl.BlockSpec(memory_space=pl.ANY)
+    vmem = pl.BlockSpec(memory_space=pltpu.VMEM)
+    large = (layer_out, grad_tokens, grad_up, grad_down)
+    shapes = [jax.ShapeDtypeStruct(value.shape, value.dtype) for value in large]
+    shapes += [jax.ShapeDtypeStruct((UNIT // 2, UNIT), F32)] * 4
+    shapes += [jax.ShapeDtypeStruct((size,), F32) for size in (UNIT, UNIT, 2 * SPAN) + (features,) * 6]
+    return pl.pallas_call(
+        finish_kernel,
+        in_specs=[any_space] * 4 + [vmem] * 2,
+        out_specs=[any_space] * 4 + [vmem] * 13,
+        out_shape=shapes,
+        scratch_shapes=[pltpu.SemaphoreType.DMA((4,))],
+        name="finish",
+    )(*large, grad_attn, sums)
+
+
 class Links:
     def __init__(self):
         self.dp = lax.axis_size("dp")
@@ -1529,27 +1588,15 @@
     down_weight,
     down_bias,
 ):
-    core, z = lax.axis_index("dp") % 2, lax.axis_index("tensor")
-    width, units = 160, SPAN
-    parts = (query_weight, key_weight, value_weight, out_weight.T)
-    shards = (
-        jnp.concatenate([w[:, i * width : (i + 1) * width] for i in range(2) for w in parts], 1),
-        up_weight,
-        down_weight.T,
+    weights = (query_weight, key_weight, value_weight, out_weight.T)
+    vectors = (
+        query_bias, value_bias, up_bias, norm1_gain, norm1_shift, norm2_gain, norm2_shift, out_bias,
+        down_bias,
     )
-
-    def half_of(vector):
-        size = vector.shape[0] // 2
-        return jnp.where(core == 0, vector[:size], vector[size:])
-
-    gap = jnp.zeros((width,), F32)
-    small = [half_of(query_bias), gap, half_of(value_bias), gap, half_of(up_bias)]
-    small = jnp.concatenate(small + [jnp.zeros((6 * SPAN,), F32)]).reshape(8, SPAN)
-    vectors = (norm1_gain, norm1_shift, norm2_gain, norm2_shift, out_bias, down_bias)
     (
         w_attn, w_up, w_down, tok, out_grad, mask, first, second, joined, heads, totals, middle, hidden,
         slope, layer_own, layer_other,
-    ) = forward_pass(lengths, shards, tokens, cotangent, small, vectors)
+    ) = forward_pass(lengths, (up_weight, down_weight.T), tokens, cotangent, weights, vectors)
     lane = jnp.arange(128)[None, :] == 0
     key_mask = jnp.where(lane, mask[0][:, None], 0.0).astype(BF16)
     grad_tokens, grad_down, grad_up, grad_attn, sums, _, layer_out, _, _ = backward_pass(
@@ -1557,33 +1604,29 @@
         layer_own, layer_other, key_mask, norm1_gain, norm2_gain,
     )
 
-    def piece(index):
-        start = index * width
-        both = [grad_attn[:, i * SPAN + start : i * SPAN + start + width] for i in range(2)]
-        return jnp.concatenate(both, 1)
-
-    def own(first_row, start, size):
-        rows = lax.dynamic_slice_in_dim(sums[:, 0], first_row + 2 * z, 2, 0)
-        return rows[:, start : start + size].reshape(-1)
-
+    (
+        layer_out, grad_tokens, grad_up, grad_down, grad_query, grad_key, grad_value, grad_out, sum_query,
+        sum_value, sum_up, *sums,
+    ) = finish(layer_out, grad_tokens, grad_up, grad_down, grad_attn, sums)
+    sum_down, sum_out, sum_gain_two, sum_shift_two, sum_gain_one, sum_shift_one = sums
     return (
         layer_out,
         grad_tokens,
-        sums[4, 0],
-        sums[5, 0],
-        piece(0),
-        own(16, 0, width),
-        piece(1),
-        piece(2),
-        own(16, width, width),
-        piece(3).T,
-        sums[1, 0],
-        sums[2, 0],
-        sums[3, 0],
+        sum_gain_one,
+        sum_shift_one,
+        grad_query,
+        sum_query,
+        grad_key,
+        grad_value,
+        sum_value,
+        grad_out.T,
+        sum_out,
+        sum_gain_two,
+        sum_shift_two,
         grad_up,
-        own(8, 0, units),
+        sum_up,
         grad_down.T,
-        sums[0, 0],
+        sum_down,
     )
 
 

time: 472 us -> 623 us (1.32)
  Pallas kernels: 439 us -> 611 us
  local copies, waits for them, and re-layouts: 17.2 us -> 0.83 us
    pallas_call x0 -> x1, Pallas kernels: none -> 172 us  [finish(): pl.pallas_call(finish_kernel, in_specs=[any_space] * 4 + [vmem] * 2, out_...]
where the time goes in v6:
time: 623 us; the launch traced here: 614 us
  Pallas kernels  611 us (98%)
    pallas_call x1, Pallas kernels, backward_pass(): pl.pallas_call(functools.partial(backward_kernel, HDIM ** (-0.5)), in_spe...  236 us
    pallas_call x1, Pallas kernels, forward_pass(): pl.pallas_call(functools.partial(forward_kernel, HDIM ** (-0.5)), in_spec...  203 us
    pallas_call x1, Pallas kernels, finish(): pl.pallas_call(finish_kernel, in_specs=[any_space] * 4 + [vmem] * 2, out_...  172 us

profile of v6, /device:TPU:1, one launch (start us, length us, event | category | flops | bytes accessed | tf_op | source)
XLA Modules:
  0.0 614.3 jit_solution(2772342943856047272)
XLA Ops:
  0.7 203.1 %forward_pass.1 = (bf16[1280,2560]{1,0:T(8,128)(2,1)}, bf16[1280,2560]{1,0:T(8,128)(2,1)}, bf16[1280,2560]{1,0:T(8,128)(2,1)}, bf16[768,1280]{1,0:T(8,128)(2,1)}...) custom-call(s32[2]{0:T(128)} %lengths.1, ...), custom_call_target="tpu_custom_call" | custom-call | flops 35389440000 | bytes 90000000 | tf_op jit(solution)/shard_map/forward_pass/pallas_call | solution.py:671
  203.8 0.8 slice_reduce_fusion
  204.6 1.0 select_convert_fusion.key_mask
  205.6 236.2 %backward_pass.1 = (bf16[768,1280]{1,0:T(8,128)(2,1)}, f32[160,1280]{1,0:T(8,128)}, f32[160,1280]{1,0:T(8,128)}, f32[160,1280]{1,0:T(8,128)}, f32[24,1,1280]{2,1...) custom-call(bf16[1280,2560]{1,0:T(8,128)(2,1)} %get-tuple-element.56, ...), custom_call_target="tpu_custom_call" | custom-call | flops 50331648000 | bytes 90000000 | tf_op jit(solution)/shard_map/backward_pass/pallas_call | solution.py:1286
  441.8 172.0 %finish.1 = (bf16[768,1280]{1,0:T(8,128)(2,1)}, bf16[768,1280]{1,0:T(8,128)(2,1)}, f32[160,1280]{1,0:T(8,128)}, f32[160,1280]{1,0:T(8,128)}, f32[160,320]{1,0:T(...) custom-call(bf16[768,1280]{1,0:T(8,128)(2,1)} %get-tuple-element.72., ...), custom_call_target="tpu_custom_call" | custom-call | tf_op jit(solution)/shard_map/finish/pallas_call | solution.py:1364
  (1 shorter events, 0.0 us)

commit v7 on v6

--- a/solution.py
+++ b/solution.py
@@ -1332,12 +1332,13 @@
 def finish_kernel(*refs):
     z = lax.axis_index("tensor")
     large_in, attn, sums = refs[:4], refs[4], refs[5]
-    large_out, grads, vectors, sem = refs[6:10], refs[10:14], refs[14:-1], refs[-1]
-    copies = [
-        pltpu.make_async_copy(source, target, sem.at[i])
-        for i, (source, target) in enumerate(zip(large_in, large_out))
-    ]
-    for copy in copies:
+    large_out, grads, vectors, held, sem = refs[6:10], refs[10:14], refs[14:-5], refs[-5:-1], refs[-1]
+    loads = [pltpu.make_async_copy(large_in[i], held[i], sem.at[i]) for i in range(4)]
+    copies = [pltpu.make_async_copy(held[i], large_out[i], sem.at[4 + i]) for i in range(4)]
+    for load in loads:
+        load.start()
+    for load, copy in zip(loads, copies):
+        load.wait()
         copy.start()
     width = UNIT // 2
     for i, grad in enumerate(grads):
@@ -1366,7 +1367,9 @@
         in_specs=[any_space] * 4 + [vmem] * 2,
         out_specs=[any_space] * 4 + [vmem] * 13,
         out_shape=shapes,
-        scratch_shapes=[pltpu.SemaphoreType.DMA((4,))],
+        scratch_shapes=[pltpu.VMEM(value.shape, value.dtype) for value in large]
+        + [pltpu.SemaphoreType.DMA((8,))],
+        compiler_params=pltpu.CompilerParams(vmem_limit_bytes=24 << 20),
         name="finish",
     )(*large, grad_attn, sums)
 

time: 623 us -> 463 us (0.74)
  Pallas kernels: 611 us -> 444 us
  local copies, waits for them, and re-layouts: 0.83 us -> 8.24 us
    pallas_call x1, Pallas kernels: 172 us -> 4.34 us  [finish(): pl.pallas_call(finish_kernel, in_specs=[any_space] * 4 + [vmem] * 2, out_...]
    unnamed x0 -> x12, local copies, waits for them, and re-layouts: none -> 7.42 us
where the time goes in v7:
time: 463 us; the launch traced here: 454 us
  Pallas kernels  444 us (96%)
  local copies, waits for them, and re-layouts  8.24 us (2%)
    pallas_call x1, Pallas kernels, backward_pass(): pl.pallas_call(functools.partial(backward_kernel, HDIM ** (-0.5)), in_spe...  236 us
    pallas_call x1, Pallas kernels, forward_pass(): pl.pallas_call(functools.partial(forward_kernel, HDIM ** (-0.5)), in_spec...  203 us

profile of v7, /device:TPU:1, one launch (start us, length us, event | category | flops | bytes accessed | tf_op | source)
XLA Modules:
  0.0 454.0 jit_solution(11990912833018069335)
XLA Ops:
  0.7 203.1 %forward_pass.1 = (bf16[1280,2560]{1,0:T(8,128)(2,1)}, bf16[1280,2560]{1,0:T(8,128)(2,1)}, bf16[1280,2560]{1,0:T(8,128)(2,1)}, bf16[768,1280]{1,0:T(8,128)(2,1)}...) custom-call(s32[2]{0:T(128)} %lengths.1, ...), custom_call_target="tpu_custom_call" | custom-call | flops 35389440000 | bytes 90000000 | tf_op jit(solution)/shard_map/forward_pass/pallas_call | solution.py:671
  203.8 0.8 slice_reduce_fusion
  204.6 1.0 select_convert_fusion.key_mask
  205.6 236.2 %backward_pass.1 = (bf16[768,1280]{1,0:T(8,128)(2,1)}, f32[160,1280]{1,0:T(8,128)}, f32[160,1280]{1,0:T(8,128)}, f32[160,1280]{1,0:T(8,128)}, f32[24,1,1280]{2,1...) custom-call(bf16[1280,2560]{1,0:T(8,128)(2,1)} %get-tuple-element.56, ...), custom_call_target="tpu_custom_call" | custom-call | flops 50331648000 | bytes 90000000 | tf_op jit(solution)/shard_map/backward_pass/pallas_call | solution.py:1286
  441.8 0.0 copy-start
  441.8 1.5 copy-done
  443.3 0.0 copy-start.1
  443.3 1.5 copy-done.1
  444.9 0.0 copy-start.2
  444.9 1.1 copy-done.2
  446.0 0.0 copy-start.3
  446.0 1.1 copy-done.3
  447.2 0.0 copy-start.4
  447.2 1.1 copy-done.4
  448.3 0.0 copy-start.5
  448.3 0.9 copy-done.5
  449.2 4.3 finish.1
  (1 shorter events, 0.0 us)
Async XLA Ops:
  441.8 1.5 copy-start
  443.3 1.5 copy-start.1
  444.9 1.1 copy-start.2
  446.0 1.1 copy-start.3
  447.2 1.1 copy-start.4
  448.3 0.9 copy-start.5
